TPU v7x, 512 devices: a whole 4x4x16 slice. The times are simulated.
512 devices in a mesh: ctx: 64 (over z, x), head: 8 (over y, core).
Axes of the slice: x: 4, y: 4, z: 16, core: 2. Of those that a mesh axis runs over, the one named last changes fastest.
Arguments:
- tokens: bfloat16 [32768, 2048], P('ctx', 'head'), may hold values from -400 to 400
- gain: float32 [2048], replicated, may hold values from 0.1 to 1.9
- w_feat: bfloat16 [2048, 256], P(None, 'head'), may hold values from -0.125 to 0.125
- w_value: bfloat16 [2048, 2048], P(None, 'head'), may hold values from -0.125 to 0.125
- w_window: bfloat16 [2048, 2048], P(None, 'head'), may hold values from -0.6960582 to 0.6960582
- w_out: bfloat16 [2048, 2048], P('head'), may hold values from -0.1875 to 0.1875
Outputs:
- layer_out: bfloat16 [32768, 2048], P('ctx', 'head')
All inputs are finite; a program needn't handle non-finite values.
Results may differ from a plain program's by a relative error of at most 0.02.
Values may be sent and summed in bfloat16 or wider, within the bound.
No kernel may reach another device: no remote copies, remote signals or barrier semaphores. Data moves between devices by JAX's collectives and lax.ppermute only.
A program may use at most 64 MiB of HBM per device.

v0:
```python
import math

import jax
import jax.numpy as jnp
from jax import lax
from jax.sharding import PartitionSpec as P

epsilon = 1e-05


def from_behind(value, axis, steps):
    count = lax.axis_size(axis)
    leading, last = (max(0, -steps), min(count, count - steps))
    return lax.ppermute(value, axis, [(source, source + steps) for source in range(leading, last)])


def carried_in(value, axis, join, neutral):
    place = lax.axis_index(axis)
    gathered = lax.all_gather(value.astype(jnp.bfloat16), axis)
    state = jnp.zeros_like(value) + jnp.asarray(neutral, value.dtype)

    def one(turn, state):
        return join(state, lax.dynamic_index_in_dim(gathered, turn, 0, False).astype(value.dtype))

    return lax.fori_loop(0, place, one, state)


def taylor(rows_in):
    widened = rows_in.astype(jnp.float32)
    count = widened.shape[0]
    width_in = widened.shape[1]
    outer = (widened[:, :, None] * widened[:, None, :]).reshape(count, width_in * width_in) / (
        4.0 * math.sqrt(2.0)
    )
    return jnp.concatenate(
        [jnp.ones((count, 1), jnp.float32), widened / 2.0, outer], axis=1
    ).astype(jnp.bfloat16)


def state_of(k_lin, v_lin):
    return jnp.dot(taylor(k_lin).T, v_lin, preferred_element_type=jnp.float32)


def linear_part(q_lin, k_lin, v_lin, prefix):
    count = q_lin.shape[0]
    inner = jnp.dot(q_lin, k_lin.T, preferred_element_type=jnp.float32)
    series = 1.0 + inner / 4.0 + inner * inner / 32.0
    rows_at = jnp.arange(count, dtype=jnp.int32)
    causal = rows_at[:, None] >= rows_at[None, :]
    weights = jnp.where(causal, series, 0.0).astype(jnp.bfloat16)
    numerator = jnp.dot(weights, v_lin, preferred_element_type=jnp.float32)
    numerator = numerator + jnp.dot(
        taylor(q_lin), prefix.astype(jnp.bfloat16), preferred_element_type=jnp.float32
    )
    scale = lax.rsqrt(jnp.mean(numerator * numerator, axis=1, keepdims=True) + epsilon)
    return (numerator * scale).astype(jnp.bfloat16)


def window_part(q_win, k_win, v_win, prev_keys, prev_values, offset):
    count = q_win.shape[0]
    span = prev_keys.shape[0]
    key_rows = jnp.concatenate([prev_keys, k_win], axis=0)
    value_rows = jnp.concatenate([prev_values, v_win], axis=0)
    query_pos = offset + jnp.arange(count, dtype=jnp.int32)
    key_pos = offset - span + jnp.arange(span + count, dtype=jnp.int32)
    distance = query_pos[:, None] - key_pos[None, :]
    allowed = (key_pos[None, :] >= 0) & (distance >= 0) & (distance < span)
    scores = jnp.dot(q_win, key_rows.T, preferred_element_type=jnp.float32) / math.sqrt(
        q_win.shape[1]
    )
    scores = jnp.where(allowed, scores, -1e30)
    highest = jnp.max(scores, axis=1, keepdims=True)
    lifted = jnp.exp(scores - highest)
    probs = (lifted / jnp.sum(lifted, axis=1, keepdims=True)).astype(jnp.bfloat16)
    return jnp.dot(probs, value_rows, preferred_element_type=jnp.float32).astype(jnp.bfloat16)


def add_states(earlier, later):
    return earlier + later


def shards(tokens, gain, w_feat, w_value, w_window, w_out):
    gathered = lax.all_gather(tokens, "head", axis=1, tiled=True)
    widened = gathered.astype(jnp.float32)
    normed = (
        widened * lax.rsqrt(jnp.mean(widened * widened, axis=1, keepdims=True) + epsilon) * gain
    ).astype(jnp.bfloat16)
    features = jnp.dot(normed, w_feat, preferred_element_type=jnp.float32).astype(jnp.bfloat16)
    values = jnp.dot(normed, w_value, preferred_element_type=jnp.float32).astype(jnp.bfloat16)
    windowed = jnp.dot(normed, w_window, preferred_element_type=jnp.float32).astype(jnp.bfloat16)
    feat_width = w_feat.shape[1] // 2
    head_width = w_value.shape[1] // 2
    q_lin = features[:, :feat_width]
    k_lin = features[:, feat_width:]
    v_lin = values[:, :head_width]
    v_win = values[:, head_width:]
    q_win = windowed[:, :head_width]
    k_win = windowed[:, head_width:]
    count = tokens.shape[0]
    rim_rows = jnp.concatenate([k_win, v_win], axis=1)
    received = from_behind(rim_rows, "ctx", 1)
    own_state = state_of(k_lin, v_lin)
    empty = jnp.zeros_like(own_state)
    prefix = carried_in(own_state, "ctx", add_states, empty)
    offset = lax.axis_index("ctx") * count
    win_out = window_part(
        q_win, k_win, v_win, received[:, :head_width], received[:, head_width:], offset
    )
    lin_out = linear_part(q_lin, k_lin, v_lin, prefix)
    mixture = jnp.concatenate([lin_out, win_out], axis=1)
    terms = jnp.dot(mixture, w_out, preferred_element_type=jnp.float32)
    return lax.psum_scatter(terms.astype(jnp.bfloat16), "head", scatter_dimension=1, tiled=True)


def solution(mesh):
    placed = (
        P("ctx", "head"),
        P(),
        P(None, "head"),
        P(None, "head"),
        P(None, "head"),
        P("head", None),
    )
    return jax.shard_map(
        shards, mesh=mesh, in_specs=placed, out_specs=P("ctx", "head"), check_vma=False
    )
```

profile of v0, /device:TPU:1, one launch (start us, length us, event | category | flops | bytes accessed | tf_op | source)
XLA Modules:
  0.0 304.8 jit_solution(2410144221151309751)
XLA Ops:
  6.5 0.0 copy-start
  6.5 0.0 copy-start.5
  6.5 0.0 copy-start.4
  6.5 0.0 all-gather.5.cloned.1.call-start
  6.5 0.7 all-gather.5.cloned.1.call-update
  7.3 0.0 all-gather.7.cloned.1.call-start
  7.3 42.9 %all-gather.5.cloned.1.call-done = bf16[512,2048]{1,0:T(8,128)(2,1)} async-done(((bf16[512,256]{1,0:T(8,128)(2,1)}), bf16[512,2048]{1,0:T(8,128)(2,1)}) %all-gather.5.cloned.1.call-update) | async-done | bytes 2097168 | tf_op jit(solution)/shard_map/all_gather | solution.py:83
  50.2 0.0 copy-start.1
  50.2 2.2 fusion
  52.4 0.0 copy-done.5
  52.4 0.0 copy-done.4
  52.4 0.0 copy-done.1
  52.4 0.0 copy-start.3
  52.5 0.8 convolution_convert_fusion.5
  53.3 0.3 copy-done.3
  53.7 1.5 convolution_convert_fusion.2
  55.2 1.8 fusion.6
  57.0 0.0 all-gather.7.cloned.1.call-update
  57.0 0.0 reduce-scatter.2.cloned.1.call-start
  57.1 0.9 slice.37
  58.0 2.0 convolution_convert_fusion.1
  60.0 0.0 copy-start.2
  60.1 3.1 %collective-permute-start = (bf16[512,256]{1,0:T(8,128)(2,1)S(1)}, bf16[512,256]{1,0:T(8,128)(2,1)S(1)}, u32[]{:S(2)}, u32[]{:S(2)}) collective-permute-start(bf16[512,256]{1,0:T(8,128)(2,1)S(1)} %pad_maximum_fusion), channel_id=1, source_target_pairs={{0,8},{8,16},{16,24},{24,32},{32,40},{40,48},{48,56},{56,64},{64,7... | collective-permute-start | bytes 786440 | tf_op jit(solution)/shard_map/ppermute | solution.py:14
  63.2 0.0 copy-done.2
  63.3 5.3 %collective-permute-done = bf16[512,256]{1,0:T(8,128)(2,1)S(1)} collective-permute-done((bf16[512,256]{1,0:T(8,128)(2,1)S(1)}, bf16[512,256]{1,0:T(8,128)(2,1)S(1)}, u32[]{:S(2)}, u32[]{:S(2)}) %collective-permute-start) | collective-permute-done | bytes 262176 | tf_op jit(solution)/shard_map/ppermute | solution.py:14
  68.6 1.9 fusion.52
  70.5 0.5 fusion.5
  71.0 0.7 convolution_convert_fusion.3
  71.7 125.2 %all-gather.7.cloned.1.call-done = bf16[64,273,128]{2,1,0:T(8,128)(2,1)} async-done(((bf16[1,273,128]{2,1,0:T(8,128)(2,1)}), bf16[64,273,128]{2,1,0:T(8,128)(2,1)}) %all-gather.7.cloned.1.call-update) | async-done | bytes 4472848 | tf_op jit(solution)/shard_map/all_gather | solution.py:19
  196.9 0.3 fusion.11
  197.2 1.5 multiply_reduce_fusion
  198.7 0.0 copy-done
  198.7 2.1 convolution_convert_fusion
  200.8 0.0 reduce-scatter.2.cloned.1.call-update
  200.9 97.4 %reduce-scatter.2.cloned.1.call-done = bf16[512,256]{1,0:T(8,128)(2,1)} async-done(((bf16[512,2048]{1,0:T(8,128)(2,1)}), bf16[512,256]{1,0:T(8,128)(2,1)}) %reduce-scatter.2.cloned.1.call-update) | async-done | bytes 262160 | tf_op jit(solution)/shard_map/reduce_scatter | solution.py:112
  (16 shorter events, 0.3 us)
Async XLA Ops:
  6.5 192.2 %copy-start = (bf16[256,2048]{1,0:T(8,128)(2,1)S(1)}, bf16[256,2048]{1,0:T(8,128)(2,1)}, u32[]{:S(2)}) copy-start(bf16[256,2048]{1,0:T(8,128)(2,1)} %param.13) | copy-start | bytes 3145732
  6.5 45.9 %copy-start.5 = (f32[2048]{0:T(1024)S(1)}, f32[2048]{0:T(1024)}, u32[]{:S(2)}) copy-start(f32[2048]{0:T(1024)} %param.9) | copy-start | bytes 24580
  6.5 45.9 %copy-start.4 = (bf16[2048,32]{0,1:T(8,128)(2,1)S(1)}, bf16[2048,32]{0,1:T(8,128)(2,1)}, u32[]{:S(2)}) copy-start(bf16[2048,32]{0,1:T(8,128)(2,1)} %param.10) | copy-start | bytes 393220
  6.5 43.6 %all-gather.5.cloned.1.call-start = ((), (), s32[]{:S(2)}) async-start(), calls=%async_computation.1 | async-start | bytes 2359296 | tf_op jit(solution)/shard_map/all_gather | solution.py:83
  7.3 189.6 %all-gather.7.cloned.1.call-start = ((), (), s32[]{:S(2)}) async-start(), calls=%async_computation.3 | async-start | bytes 4659200 | tf_op jit(solution)/shard_map/all_gather | solution.py:19
  50.2 2.3 copy-start.1
  52.4 1.2 copy-start.3
  57.0 241.2 %reduce-scatter.2.cloned.1.call-start = ((), (), s32[]{:S(2)}) async-start(), calls=%async_computation.2 | async-start | bytes 2359296 | tf_op jit(solution)/shard_map/reduce_scatter | solution.py:112
  60.0 3.2 %copy-start.2 = (bf16[512,256]{1,0:T(8,128)(2,1)}, bf16[512,256]{1,0:T(8,128)(2,1)S(1)}, u32[]{:S(2)}) copy-start(bf16[512,256]{1,0:T(8,128)(2,1)S(1)} %convolution_convert_fusion.1) | copy-start | bytes 786436
  60.1 8.5 %collective-permute-start = (bf16[512,256]{1,0:T(8,128)(2,1)S(1)}, bf16[512,256]{1,0:T(8,128)(2,1)S(1)}, u32[]{:S(2)}, u32[]{:S(2)}) collective-permute-start(bf16[512,256]{1,0:T(8,128)(2,1)S(1)} %pad_maximum_fusion), channel_id=1, source_target_pairs={{0,8},{8,16},{16,24},{24,32},{32,40},{40,48},{48,56},{56,64},{64,7... | collective-permute-start | bytes 786440 | tf_op jit(solution)/shard_map/ppermute | solution.py:14
Sparse Core Ops, SparseCore 0:
  9.5 40.6 all-gather.4
  57.1 139.6 all-gather.6
  201.0 97.2 reduce-scatter.1
where the time goes:
time: 309 us; the launch traced here: 305 us
  waiting for transfers between devices  271 us (88%)
  between operations  13.3 us (4%)
  matrix products  12.5 us (4%)
  starting transfers between devices  3.19 us (1%)
    all_gather x1, waiting for transfers between devices, carried_in(): gathered = lax.all_gather(value.astype(jnp.bfloat16), axis)  125 us
    reduce_scatter x1, waiting for transfers between devices, shards(): lax.psum_scatter(terms.astype(jnp.bfloat16), 'head', scatter_dimension=1,...  97.4 us
    all_gather x1, waiting for transfers between devices, shards(): gathered = lax.all_gather(tokens, 'head', axis=1, tiled=True)  42.9 us
  transfers between devices with their start and end apart: 4, of which 4 were waited for; matrix products, arithmetic and copies ran while one was open for 2% of the time, Pallas kernels for 0%

commit v1 on v0

v1 whole, which is shorter than its diff:
```python
import functools
import math

import jax
import jax.numpy as jnp
from jax import lax
from jax.experimental import pallas as pl
from jax.experimental.pallas import tpu as pltpu
from jax.sharding import PartitionSpec as P

EPS = 1e-05
FEAT = 16
ROWS = 160
BF = jnp.bfloat16
F32 = jnp.float32
VMEM = 56 * 1024 * 1024


def call(kernel, outs, scratch=()):
    return pl.pallas_call(
        kernel,
        out_shape=outs,
        scratch_shapes=scratch,
        compiler_params=pltpu.CompilerParams(vmem_limit_bytes=VMEM),
    )


def call_with_scalar(kernel, outs, count):
    return pl.pallas_call(
        kernel,
        out_shape=outs,
        in_specs=[pl.BlockSpec(memory_space=pltpu.SMEM)]
        + [pl.BlockSpec(memory_space=pltpu.VMEM)] * count,
        compiler_params=pltpu.CompilerParams(vmem_limit_bytes=VMEM),
    )


def pick(shape, axis):
    r = lax.broadcasted_iota(jnp.int32, shape, axis)
    u = lax.broadcasted_iota(jnp.int32, shape, 1 - axis)
    first = (r >= 1) & (r <= FEAT) & (u == r - 1)
    second = jnp.zeros(shape, jnp.bool_)
    base = 1 + FEAT
    for i in range(FEAT):
        width = FEAT - i
        inside = (r >= base) & (r < base + width)
        first = first | (inside & (u == i))
        second = second | (inside & (u == i + r - base))
        base += width
    return first.astype(F32).astype(BF), second.astype(F32).astype(BF)


def weights_of(shape, axis, twice):
    r = lax.broadcasted_iota(jnp.int32, shape, axis)
    scale = jnp.where(r == 0, 1.0, jnp.where(r <= FEAT, 0.5, 1.0 / (4.0 * math.sqrt(2.0))))
    if twice:
        base = 1 + FEAT
        square = jnp.zeros(shape, jnp.bool_)
        for i in range(FEAT):
            square = square | (r == base)
            base += FEAT - i
        scale = jnp.where((r > FEAT) & ~square, 2.0 * scale, scale)
    one_first = jnp.where(r == 0, 1.0, 0.0)
    one_second = jnp.where(r <= FEAT, 1.0, 0.0)
    return scale, one_first, one_second


NT = (((1,), (1,)), ((), ()))
NN = (((1,), (0,)), ((), ()))


def dot(a, b, dims=NN):
    return lax.dot_general(a, b, dims, preferred_element_type=F32)


def project_kernel(x_ref, gain_ref, wf_ref, wv_ref, ww_ref, feat_ref, vlin_ref, qwin_ref, rim_ref, state_ref, normed):
    count = x_ref.shape[2]
    step = 128
    for r in range(0, count, step):
        total = jnp.zeros((step, 1), F32)
        for c in range(2):
            for y in range(4):
                x = x_ref[c, y, r : r + step, :].astype(F32)
                total = total + jnp.sum(x * x, axis=1, keepdims=True)
        scale = lax.rsqrt(total * (1.0 / 2048.0) + EPS)
        for c in range(2):
            for y in range(4):
                at = (2 * y + c) * 256
                x = x_ref[c, y, r : r + step, :].astype(F32)
                normed[r : r + step, at : at + 256] = (
                    x * scale * gain_ref[0:1, at : at + 256]
                ).astype(BF)
    n = normed[...]
    feats = dot(n, wf_ref[...]).astype(BF)
    values = dot(n, wv_ref[...]).astype(BF)
    feat_ref[...] = feats
    vlin = values[:, :128]
    vlin_ref[...] = vlin
    first, second = pick((ROWS, FEAT), 0)
    scale, add_first, add_second = weights_of((ROWS, 1), 0, False)
    k = feats[:, FEAT:]
    phi = (dot(first, k, NT) + add_first) * (dot(second, k, NT) + add_second) * scale
    state = dot(phi.astype(BF), vlin).astype(BF)
    for i in range(4):
        state_ref[i, :, :] = state
    windowed = dot(n, ww_ref[...]).astype(BF)
    qwin_ref[...] = windowed[:, :128]
    rim_ref[:, :128] = windowed[:, 128:]
    rim_ref[:, 128:] = values[:, 128:]


def attend_kernel(first_ref, q_ref, own_ref, prev_ref, feat_ref, vlin_ref, win_ref, num_ref):
    count = q_ref.shape[0]
    tile = 256
    no_prev = first_ref[0] == 0
    for t in range(count // tile):
        q = q_ref[t * tile : (t + 1) * tile, :]
        old = prev_ref[t * tile :, :]
        new = own_ref[: (t + 1) * tile, :]
        keys = jnp.concatenate([old[:, :128], new[:, :128]], axis=0)
        vals = jnp.concatenate([old[:, 128:], new[:, 128:]], axis=0)
        width = keys.shape[0]
        scores = dot(q, keys, NT) * (1.0 / math.sqrt(128.0))
        at = lax.broadcasted_iota(jnp.int32, (tile, width), 0) + count
        key = lax.broadcasted_iota(jnp.int32, (tile, width), 1)
        least = jnp.where(no_prev, count - t * tile, 0)
        allowed = (key <= at) & (key > at - count) & (key >= least)
        scores = jnp.where(allowed, scores, -1e30)
        lifted = jnp.exp(scores - jnp.max(scores, axis=1, keepdims=True))
        probs = (lifted / jnp.sum(lifted, axis=1, keepdims=True)).astype(BF)
        win_ref[t * tile : (t + 1) * tile, :] = dot(probs, vals).astype(BF)
        ql = feat_ref[t * tile : (t + 1) * tile, :FEAT]
        kl = feat_ref[: (t + 1) * tile, FEAT:]
        inner = dot(ql, kl, NT)
        width = kl.shape[0]
        row = lax.broadcasted_iota(jnp.int32, (tile, width), 0) + t * tile
        col = lax.broadcasted_iota(jnp.int32, (tile, width), 1)
        series = 1.0 + inner * 0.25 + inner * inner * (1.0 / 32.0)
        weight = jnp.where(row >= col, series, 0.0).astype(BF)
        num_ref[t * tile : (t + 1) * tile, :] = dot(weight, vlin_ref[: (t + 1) * tile, :])


def mix_kernel(core_ref, feat_ref, num_ref, prefix_ref, win_ref, w_ref, mix_ref, other_ref):
    first, second = pick((FEAT, ROWS), 1)
    scale, add_first, add_second = weights_of((1, ROWS), 1, True)
    q = feat_ref[:, :FEAT]
    phi = (dot(q, first) + add_first) * (dot(q, second) + add_second) * scale
    numerator = num_ref[...] + dot(phi.astype(BF), prefix_ref[...])
    mean = jnp.mean(numerator * numerator, axis=1, keepdims=True)
    mix_ref[:, :128] = (numerator * lax.rsqrt(mean + EPS)).astype(BF)
    mix_ref[:, 128:] = win_ref[...]
    mix = mix_ref[...]
    other = 1 - core_ref[0]
    for y in range(4):
        at = pl.multiple_of((2 * y + other) * 256, 256)
        other_ref[y, :, :] = dot(mix, w_ref[:, pl.ds(at, 256)]).astype(BF)


def join_kernel(core_ref, mix_ref, w_ref, got_ref, sum_ref):
    mix = mix_ref[...]
    for y in range(4):
        at = pl.multiple_of((2 * y + core_ref[0]) * 256, 256)
        mine = dot(mix, w_ref[:, pl.ds(at, 256)])
        sum_ref[y, :, :] = (mine + got_ref[y, :, :].astype(F32)).astype(BF)


def level(states, groups, place):
    got = lax.all_to_all(states, "ctx", 0, 0, tiled=True, axis_index_groups=groups)
    wide = got.astype(F32)
    order = lax.broadcasted_iota(jnp.int32, (4, 1, 1), 0)
    before = jnp.sum(jnp.where(order < place, wide, 0.0), axis=0)
    total = jnp.sum(wide, axis=0).astype(BF)
    return before, jnp.broadcast_to(total[None], states.shape)


def shards(tokens, gain, w_feat, w_value, w_window, w_out):
    count = tokens.shape[0]
    head = lax.axis_index("head")
    ctx = lax.axis_index("ctx")
    core = (head % 2).astype(jnp.int32).reshape(1)
    along_y = [[2 * y + c for y in range(4)] for c in range(2)]
    cores = [[2 * y, 2 * y + 1] for y in range(4)]
    spread = lax.all_to_all(
        jnp.broadcast_to(tokens[None], (4,) + tokens.shape), "head", 0, 0, tiled=True, axis_index_groups=along_y
    )
    gathered = lax.all_gather(spread, "head", axis_index_groups=cores)

    def shape(dims, kind=BF):
        return jax.ShapeDtypeStruct(dims, kind)

    feats, v_lin, q_win, rim, states = call(
        project_kernel,
        [shape((count, 32)), shape((count, 128)), shape((count, 128)), shape((count, 256)), shape((4, ROWS, 128))],
        [pltpu.VMEM((count, 2048), BF)],
    )(gathered, gain.reshape(1, -1), w_feat, w_value, w_window)
    prev = lax.ppermute(rim, "ctx", [(b, b + 1) for b in range(63)])
    in_x = [[4 * z + x for x in range(4)] for z in range(16)]
    in_low = [[16 * h + 4 * l + x for l in range(4)] for h in range(4) for x in range(4)]
    in_high = [[16 * h + 4 * l + x for h in range(4)] for l in range(4) for x in range(4)]
    before_x, states = level(states, in_x, ctx % 4)
    before_low, states = level(states, in_low, (ctx // 4) % 4)
    before_high, _ = level(states, in_high, ctx // 16)
    prefix = (before_x + before_low + before_high).astype(BF)
    win_out, numerator = call_with_scalar(attend_kernel, [shape((count, 128)), shape((count, 128), F32)], 5)(
        ctx.astype(jnp.int32).reshape(1), q_win, rim, prev, feats, v_lin
    )
    mix, other = call_with_scalar(mix_kernel, [shape((count, 256)), shape((4, count, 256))], 5)(
        core, feats, numerator, prefix, win_out, w_out
    )
    got = lax.ppermute(other, "head", [(h, h ^ 1) for h in range(8)])
    summed = call_with_scalar(join_kernel, shape((4, count, 256)), 3)(core, mix, w_out, got)
    parts = lax.all_to_all(summed, "head", 0, 0, tiled=True, axis_index_groups=along_y)
    return jnp.sum(parts.astype(F32), axis=0).astype(BF)


def solution(mesh):
    placed = (P("ctx", "head"), P(), P(None, "head"), P(None, "head"), P(None, "head"), P("head", None))
    return jax.shard_map(shards, mesh=mesh, in_specs=placed, out_specs=P("ctx", "head"), check_vma=False)
```

time: 309 us -> 150 us (0.49)
  the two profiles are of different devices: /device:TPU:1 before, /device:TPU:32 now
where the time goes in v1:
time: 150 us
  blocking collectives  49.5 us (33%)
  waiting for transfers between devices  42.7 us (28%)
  starting transfers between devices  20.3 us (14%)
  Pallas kernels  16.6 us (11%)
  between operations  13.5 us (9%)
  local copies, waits for them, and re-layouts  5.1 us (3%)
  other arithmetic  1.91 us (1%)
    all_gather x1, waiting for transfers between devices, shards(): gathered = lax.all_gather(spread, 'head', axis_index_groups=cores)  22.3 us
    all_to_all x1, blocking collectives, shards(): lax.all_to_all(summed, 'head', 0, 0, tiled=True, axis_index_groups=along_y)  19.7 us
    all_to_all x1, blocking collectives, shards(): lax.all_to_all(jnp.broadcast_to(tokens[None], (4,) + tokens.shape), 'head...  19.5 us
    all_to_all x2, starting transfers between devices, level(): lax.all_to_all(states, 'ctx', 0, 0, tiled=True, axis_index_groups=groups)  16 us
    ppermute x1, waiting for transfers between devices, shards(): prev = lax.ppermute(rim, 'ctx', [(b, b + 1) for b in range(63)])  12.1 us
    all_to_all x1, blocking collectives, level(): lax.all_to_all(states, 'ctx', 0, 0, tiled=True, axis_index_groups=groups)  10.4 us
    pallas_call x1, Pallas kernels, shards(): call(project_kernel, [shape((count, 32)), shape((count, 128)), shape((cou...  6.6 us
    all_to_all x2, waiting for transfers between devices, level(): lax.all_to_all(states, 'ctx', 0, 0, tiled=True, axis_index_groups=groups)  5.43 us
  transfers between devices with their start and end apart: 5, of which 4 were waited for; matrix products, arithmetic and copies ran while one was open for 1% of the time, Pallas kernels for 2%

profile of v1, /device:TPU:32, one launch (start us, length us, event | category | flops | bytes accessed | tf_op | source)
XLA Modules:
  0.0 149.6 jit_solution(7026571734245344232)
XLA Ops:
  6.5 0.0 copy-start.2
  6.5 0.0 all-gather.3.cloned.1.call-start
  6.5 1.1 broadcast_in_dim.42
  7.6 19.5 %all_to_all.25 = bf16[4,512,256]{2,1,0:T(8,128)(2,1)} all-to-all(bf16[4,512,256]{2,1,0:T(8,128)(2,1)S(1)} %broadcast_in_dim.42), channel_id=1, replica_groups={{0,2,4,6},{1,3,5,7},{8,10,12,14},{9,11,13,15},{16,18,20,22},{17,19,21,2..., dimensions={0} | all-to-all | bytes 2097152 | tf_op jit(solution)/shard_map/all_to_all | solution.py:183
  27.1 0.0 all-gather.3.cloned.1.call-update
  27.1 0.0 copy-done.2
  27.1 1.0 copy.8.wf_ref
  28.1 22.3 %all-gather.3.cloned.1.call-done = bf16[8,512,256]{2,1,0:T(8,128)(2,1)} async-done(((bf16[4,512,256]{2,1,0:T(8,128)(2,1)}), bf16[8,512,256]{2,1,0:T(8,128)(2,1)}) %all-gather.3.cloned.1.call-update) | async-done | bytes 2097168 | tf_op jit(solution)/shard_map/all_gather | solution.py:186
  50.4 6.6 %shard_map.64 = (bf16[512,32]{1,0:T(8,128)(2,1)}, bf16[512,128]{1,0:T(8,128)(2,1)}, bf16[512,128]{1,0:T(8,128)(2,1)}, bf16[512,256]{1,0:T(8,128)(2,1)}, bf16[4,160,128]{2,1,0:T(8,128)(2,1)}) custom-call(bf16[2,4,512,256]{3,2,1,0:T(8,128)(2,1)} %bitcast.4, f32[1,2048]{1,0:T(1,128)} %bitcast.5, bf16[2048,32]{1,0:T(8,128)(2,1)} %copy.8.wf_ref, ...), custom_call_target="tpu_custom_call" | custom-call | tf_op jit(solution)/shard_map/pallas_call | solution.py:191
  57.0 10.4 %all_to_all.26 = bf16[4,160,128]{2,1,0:T(8,128)(2,1)S(1)} all-to-all(bf16[4,160,128]{2,1,0:T(8,128)(2,1)} %get-tuple-element.19), channel_id=1, replica_groups={{0,8,16,24},{32,40,48,56},{64,72,80,88},{96,104,112,120},{128,136,144,1..., dimensions={0} | all-to-all | bytes 327680 | tf_op jit(solution)/shard_map/all_to_all | solution.py:168
  67.4 0.7 broadcast_in_dim.46
  68.1 5.3 %all-to-all-start.2 = ((bf16[4,160,128]{2,1,0:T(8,128)(2,1)}), bf16[4,160,128]{2,1,0:T(8,128)(2,1)S(1)}, u32[]{:S(2)}, u32[]{:S(2)}) async-start(bf16[4,160,128]{2,1,0:T(8,128)(2,1)} %broadcast_in_dim.46), calls=%async_computation.2 | async-start | bytes 327680 | tf_op jit(solution)/shard_map/all_to_all | solution.py:168
  73.3 5.4 %all-to-all-done.2 = bf16[4,160,128]{2,1,0:T(8,128)(2,1)S(1)} async-done(((bf16[4,160,128]{2,1,0:T(8,128)(2,1)}), bf16[4,160,128]{2,1,0:T(8,128)(2,1)S(1)}, u32[]{:S(2)}, u32[]{:S(2)}) %all-to-all-start.2) | async-done | bytes 163872 | tf_op jit(solution)/shard_map/all_to_all | solution.py:168
  78.8 0.7 broadcast_in_dim.48
  79.5 10.7 %all-to-all-start.3 = ((bf16[4,160,128]{2,1,0:T(8,128)(2,1)}), bf16[4,160,128]{2,1,0:T(8,128)(2,1)S(1)}, u32[]{:S(2)}, u32[]{:S(2)}) async-start(bf16[4,160,128]{2,1,0:T(8,128)(2,1)} %broadcast_in_dim.48), calls=%async_computation.3 | async-start | bytes 327680 | tf_op jit(solution)/shard_map/all_to_all | solution.py:168
  90.2 2.5 %collective-permute-start = (bf16[512,256]{1,0:T(8,128)(2,1)}, bf16[512,256]{1,0:T(8,128)(2,1)S(1)}, u32[]{:S(2)}, u32[]{:S(2)}) collective-permute-start(bf16[512,256]{1,0:T(8,128)(2,1)} %get-tuple-element.16.own_ref), channel_id=1, source_target_pairs={{0,8},{8,16},{16,24},{24,32},{32,40},{40,48},{48,56},{56,64},{64,7... | collective-permute-start | bytes 786440 | tf_op jit(solution)/shard_map/ppermute | solution.py:196
  92.7 0.1 select_reduce_fusion.2
  92.8 12.1 %collective-permute-done.prev_ref = bf16[512,256]{1,0:T(8,128)(2,1)S(1)} collective-permute-done((bf16[512,256]{1,0:T(8,128)(2,1)}, bf16[512,256]{1,0:T(8,128)(2,1)S(1)}, u32[]{:S(2)}, u32[]{:S(2)}) %collective-permute-start) | collective-permute-done | bytes 262176 | tf_op jit(solution)/shard_map/ppermute | solution.py:196
  104.9 0.0 copy-start.1
  104.9 0.7 copy-done.1
  105.6 3.5 %shard_map.65 = (bf16[512,128]{1,0:T(8,128)(2,1)}, f32[512,128]{1,0:T(8,128)}) custom-call(s32[1]{0:T(128)} %bitcast.3.first_ref, bf16[512,128]{1,0:T(8,128)(2,1)} %get-tuple-element.15.q_ref, bf16[512,256]{1,0:T(8,128)(2,1)} %get-tuple-element.16.own_ref, bf16[512,256]{1,0:T(8,128)(2,1)} %copy-done.1, bf16[512,32]{1,0:T(8,128)(2,1)} %get-tuple-element.14.feat_ref, ...), custom_call_target="tpu_custom_call" | custom-call | tf_op jit(solution)/shard_map/pallas_call | solution.py:204
  109.1 0.1 select_reduce_fusion.1
  109.2 0.0 all-to-all-done.3
  109.3 0.1 select_reduce_fusion
  109.4 0.6 add_convert_fusion.prefix_ref
  110.0 3.4 %shard_map.66 = (bf16[512,256]{1,0:T(8,128)(2,1)}, bf16[4,512,256]{2,1,0:T(8,128)(2,1)}) custom-call(s32[1]{0:T(128)} %bitcast.core_ref, bf16[512,32]{1,0:T(8,128)(2,1)} %get-tuple-element.14.feat_ref, f32[512,128]{1,0:T(8,128)} %get-tuple-element.18.num_ref, bf16[160,128]{1,0:T(8,128)(2,1)} %add_convert_fusion.prefix_ref, ...), custom_call_target="tpu_custom_call" | custom-call | tf_op jit(solution)/shard_map/pallas_call | solution.py:207
  113.3 1.9 %collective-permute-start.1 = (bf16[4,512,256]{2,1,0:T(8,128)(2,1)}, bf16[4,512,256]{2,1,0:T(8,128)(2,1)S(1)}, u32[]{:S(2)}, u32[]{:S(2)}) collective-permute-start(bf16[4,512,256]{2,1,0:T(8,128)(2,1)} %get-tuple-element.22), channel_id=1, source_target_pairs={{0,1},{1,0},{2,3},{3,2},{4,5},{5,4},{6,7},{7,6},{8,9},{9,8},{10,11... | collective-permute-start | bytes 3145736 | tf_op jit(solution)/shard_map/ppermute | solution.py:210
  115.3 2.8 %collective-permute-done.1.got_ref = bf16[4,512,256]{2,1,0:T(8,128)(2,1)S(1)} collective-permute-done((bf16[4,512,256]{2,1,0:T(8,128)(2,1)}, bf16[4,512,256]{2,1,0:T(8,128)(2,1)S(1)}, u32[]{:S(2)}, u32[]{:S(2)}) %collective-permute-start.1) | collective-permute-done | bytes 1048608 | tf_op jit(solution)/shard_map/ppermute | solution.py:210
  118.1 0.0 copy-start
  118.1 1.0 copy-done
  119.1 3.1 %shard_map.67 = bf16[4,512,256]{2,1,0:T(8,128)(2,1)} custom-call(s32[1]{0:T(128)} %bitcast.core_ref, bf16[512,256]{1,0:T(8,128)(2,1)} %get-tuple-element.21.mix_ref, bf16[256,2048]{1,0:T(8,128)(2,1)} %w_ref.3, bf16[4,512,256]{2,1,0:T(8,128)(2,1)} %copy-done), custom_call_target="tpu_custom_call" | custom-call | tf_op jit(solution)/shard_map/pallas_call | solution.py:211
  122.2 19.7 %all_to_all.27 = bf16[4,512,256]{2,1,0:T(8,128)(2,1)S(1)} all-to-all(bf16[4,512,256]{2,1,0:T(8,128)(2,1)} %shard_map.67), channel_id=1, replica_groups={{0,2,4,6},{1,3,5,7},{8,10,12,14},{9,11,13,15},{16,18,20,22},{17,19,21,2..., dimensions={0} | all-to-all | bytes 2097152 | tf_op jit(solution)/shard_map/all_to_all | solution.py:212
  141.9 0.9 reduce_sum.68
  (5 shorter events, 0.1 us)
Async XLA Ops:
  6.5 20.6 %copy-start.2 = (bf16[2048,32]{0,1:T(8,128)(2,1)S(1)}, bf16[2048,32]{0,1:T(8,128)(2,1)}, u32[]{:S(2)}) copy-start(bf16[2048,32]{0,1:T(8,128)(2,1)} %param.8) | copy-start | bytes 393220
  6.5 43.8 %all-gather.3.cloned.1.call-start = ((), (), s32[]{:S(2)}) async-start(), calls=%async_computation.5 | async-start | bytes 3145728 | tf_op jit(solution)/shard_map/all_gather | solution.py:186
  68.1 10.7 %all-to-all-start.2 = ((bf16[4,160,128]{2,1,0:T(8,128)(2,1)}), bf16[4,160,128]{2,1,0:T(8,128)(2,1)S(1)}, u32[]{:S(2)}, u32[]{:S(2)}) async-start(bf16[4,160,128]{2,1,0:T(8,128)(2,1)} %broadcast_in_dim.46), calls=%async_computation.2 | async-start | bytes 327680 | tf_op jit(solution)/shard_map/all_to_all | solution.py:168
  79.5 29.8 %all-to-all-start.3 = ((bf16[4,160,128]{2,1,0:T(8,128)(2,1)}), bf16[4,160,128]{2,1,0:T(8,128)(2,1)S(1)}, u32[]{:S(2)}, u32[]{:S(2)}) async-start(bf16[4,160,128]{2,1,0:T(8,128)(2,1)} %broadcast_in_dim.48), calls=%async_computation.3 | async-start | bytes 327680 | tf_op jit(solution)/shard_map/all_to_all | solution.py:168
  90.2 14.8 %collective-permute-start = (bf16[512,256]{1,0:T(8,128)(2,1)}, bf16[512,256]{1,0:T(8,128)(2,1)S(1)}, u32[]{:S(2)}, u32[]{:S(2)}) collective-permute-start(bf16[512,256]{1,0:T(8,128)(2,1)} %get-tuple-element.16.own_ref), channel_id=1, source_target_pairs={{0,8},{8,16},{16,24},{24,32},{32,40},{40,48},{48,56},{56,64},{64,7... | collective-permute-start | bytes 786440 | tf_op jit(solution)/shard_map/ppermute | solution.py:196
  104.9 0.7 copy-start.1
  113.3 4.8 %collective-permute-start.1 = (bf16[4,512,256]{2,1,0:T(8,128)(2,1)}, bf16[4,512,256]{2,1,0:T(8,128)(2,1)S(1)}, u32[]{:S(2)}, u32[]{:S(2)}) collective-permute-start(bf16[4,512,256]{2,1,0:T(8,128)(2,1)} %get-tuple-element.22), channel_id=1, source_target_pairs={{0,1},{1,0},{2,3},{3,2},{4,5},{5,4},{6,7},{7,6},{8,9},{9,8},{10,11... | collective-permute-start | bytes 3145736 | tf_op jit(solution)/shard_map/ppermute | solution.py:210
  118.1 1.0 copy-start
Sparse Core Ops, SparseCore 0:
  27.2 23.1 all-gather.2

commit v2 on v1

--- a/solution.py
+++ b/solution.py
@@ -13,7 +13,7 @@
 ROWS = 160
 BF = jnp.bfloat16
 F32 = jnp.float32
-VMEM = 56 * 1024 * 1024
+VMEM = 24 * 1024 * 1024
 
 
 def call(kernel, outs, scratch=()):
@@ -25,12 +25,13 @@
     )
 
 
-def call_with_scalar(kernel, outs, count):
+def call_with_scalar(kernel, outs, count, scratch=()):
     return pl.pallas_call(
         kernel,
         out_shape=outs,
         in_specs=[pl.BlockSpec(memory_space=pltpu.SMEM)]
         + [pl.BlockSpec(memory_space=pltpu.VMEM)] * count,
+        scratch_shapes=scratch,
         compiler_params=pltpu.CompilerParams(vmem_limit_bytes=VMEM),
     )
 
@@ -73,25 +74,26 @@
     return lax.dot_general(a, b, dims, preferred_element_type=F32)
 
 
-def project_kernel(x_ref, gain_ref, wf_ref, wv_ref, ww_ref, feat_ref, vlin_ref, qwin_ref, rim_ref, state_ref, normed):
-    count = x_ref.shape[2]
+def project_kernel(
+    core_ref, mine_ref, other_ref, gain_ref, wf_ref, wv_ref, ww_ref, feat_ref, vlin_ref, qwin_ref, rim_ref, state_ref, normed
+):
+    count = mine_ref.shape[1]
     step = 128
+    core = core_ref[0]
     for r in range(0, count, step):
-        total = jnp.zeros((step, 1), F32)
-        for c in range(2):
+        total = jnp.zeros((step, 256), F32)
+        for source in (mine_ref, other_ref):
             for y in range(4):
-                x = x_ref[c, y, r : r + step, :].astype(F32)
-                total = total + jnp.sum(x * x, axis=1, keepdims=True)
-        scale = lax.rsqrt(total * (1.0 / 2048.0) + EPS)
-        for c in range(2):
+                x = source[y, r : r + step, :].astype(F32)
+                total = total + x * x
+        scale = lax.rsqrt(jnp.sum(total, axis=1, keepdims=True) * (1.0 / 2048.0) + EPS)
+        for flip, source in enumerate((mine_ref, other_ref)):
             for y in range(4):
-                at = (2 * y + c) * 256
-                x = x_ref[c, y, r : r + step, :].astype(F32)
-                normed[r : r + step, at : at + 256] = (
-                    x * scale * gain_ref[0:1, at : at + 256]
-                ).astype(BF)
+                at = pl.multiple_of((2 * y + (core + flip) % 2) * 256, 256)
+                x = source[y, r : r + step, :].astype(F32)
+                normed[r : r + step, pl.ds(at, 256)] = (x * scale * gain_ref[0:1, pl.ds(at, 256)]).astype(BF)
     n = normed[...]
-    feats = dot(n, wf_ref[...]).astype(BF)
+    feats = dot(n, wf_ref[...], NT).astype(BF)
     values = dot(n, wv_ref[...]).astype(BF)
     feat_ref[...] = feats
     vlin = values[:, :128]
@@ -109,7 +111,22 @@
     rim_ref[:, 128:] = values[:, 128:]
 
 
-def attend_kernel(first_ref, q_ref, own_ref, prev_ref, feat_ref, vlin_ref, win_ref, num_ref):
+def inner_kernel(feat_ref, vlin_ref, num_ref):
+    count = feat_ref.shape[0]
+    tile = 256
+    for t in range(count // tile):
+        ql = feat_ref[t * tile : (t + 1) * tile, :FEAT]
+        kl = feat_ref[: (t + 1) * tile, FEAT:]
+        inner = dot(ql, kl, NT)
+        width = kl.shape[0]
+        row = lax.broadcasted_iota(jnp.int32, (tile, width), 0) + t * tile
+        col = lax.broadcasted_iota(jnp.int32, (tile, width), 1)
+        series = 1.0 + inner * 0.25 + inner * inner * (1.0 / 32.0)
+        weight = jnp.where(row >= col, series, 0.0).astype(BF)
+        num_ref[t * tile : (t + 1) * tile, :] = dot(weight, vlin_ref[: (t + 1) * tile, :])
+
+
+def attend_kernel(first_ref, q_ref, own_ref, prev_ref, win_ref):
     count = q_ref.shape[0]
     tile = 256
     no_prev = first_ref[0] == 0
@@ -129,39 +146,25 @@
         lifted = jnp.exp(scores - jnp.max(scores, axis=1, keepdims=True))
         probs = (lifted / jnp.sum(lifted, axis=1, keepdims=True)).astype(BF)
         win_ref[t * tile : (t + 1) * tile, :] = dot(probs, vals).astype(BF)
-        ql = feat_ref[t * tile : (t + 1) * tile, :FEAT]
-        kl = feat_ref[: (t + 1) * tile, FEAT:]
-        inner = dot(ql, kl, NT)
-        width = kl.shape[0]
-        row = lax.broadcasted_iota(jnp.int32, (tile, width), 0) + t * tile
-        col = lax.broadcasted_iota(jnp.int32, (tile, width), 1)
-        series = 1.0 + inner * 0.25 + inner * inner * (1.0 / 32.0)
-        weight = jnp.where(row >= col, series, 0.0).astype(BF)
-        num_ref[t * tile : (t + 1) * tile, :] = dot(weight, vlin_ref[: (t + 1) * tile, :])
-
-
-def mix_kernel(core_ref, feat_ref, num_ref, prefix_ref, win_ref, w_ref, mix_ref, other_ref):
+
+
+def linear_kernel(feat_ref, num_ref, prefix_ref, lin_ref):
     first, second = pick((FEAT, ROWS), 1)
     scale, add_first, add_second = weights_of((1, ROWS), 1, True)
     q = feat_ref[:, :FEAT]
     phi = (dot(q, first) + add_first) * (dot(q, second) + add_second) * scale
     numerator = num_ref[...] + dot(phi.astype(BF), prefix_ref[...])
     mean = jnp.mean(numerator * numerator, axis=1, keepdims=True)
-    mix_ref[:, :128] = (numerator * lax.rsqrt(mean + EPS)).astype(BF)
-    mix_ref[:, 128:] = win_ref[...]
-    mix = mix_ref[...]
-    other = 1 - core_ref[0]
-    for y in range(4):
-        at = pl.multiple_of((2 * y + other) * 256, 256)
-        other_ref[y, :, :] = dot(mix, w_ref[:, pl.ds(at, 256)]).astype(BF)
-
-
-def join_kernel(core_ref, mix_ref, w_ref, got_ref, sum_ref):
-    mix = mix_ref[...]
+    lin_ref[...] = (numerator * lax.rsqrt(mean + EPS)).astype(BF)
+
+
+def output_kernel(core_ref, lin_ref, win_ref, w_ref, lin2_ref, win2_ref, w2_ref, sum_ref):
+    mine = jnp.concatenate([lin_ref[...], win_ref[...]], axis=1)
+    other = jnp.concatenate([lin2_ref[...], win2_ref[...]], axis=1)
     for y in range(4):
         at = pl.multiple_of((2 * y + core_ref[0]) * 256, 256)
-        mine = dot(mix, w_ref[:, pl.ds(at, 256)])
-        sum_ref[y, :, :] = (mine + got_ref[y, :, :].astype(F32)).astype(BF)
+        total = dot(mine, w_ref[:, pl.ds(at, 256)]) + dot(other, w2_ref[:, pl.ds(at, 256)])
+        sum_ref[y, :, :] = total.astype(BF)
 
 
 def level(states, groups, place):
@@ -179,36 +182,41 @@
     ctx = lax.axis_index("ctx")
     core = (head % 2).astype(jnp.int32).reshape(1)
     along_y = [[2 * y + c for y in range(4)] for c in range(2)]
-    cores = [[2 * y, 2 * y + 1] for y in range(4)]
+
+    def across(value):
+        return lax.ppermute(value, "head", [(h, h ^ 1) for h in range(8)])
+
+    def shape(dims, kind=BF):
+        return jax.ShapeDtypeStruct(dims, kind)
+
     spread = lax.all_to_all(
         jnp.broadcast_to(tokens[None], (4,) + tokens.shape), "head", 0, 0, tiled=True, axis_index_groups=along_y
     )
-    gathered = lax.all_gather(spread, "head", axis_index_groups=cores)
-
-    def shape(dims, kind=BF):
-        return jax.ShapeDtypeStruct(dims, kind)
-
-    feats, v_lin, q_win, rim, states = call(
+    feats, v_lin, q_win, rim, states = call_with_scalar(
         project_kernel,
         [shape((count, 32)), shape((count, 128)), shape((count, 128)), shape((count, 256)), shape((4, ROWS, 128))],
+        6,
         [pltpu.VMEM((count, 2048), BF)],
-    )(gathered, gain.reshape(1, -1), w_feat, w_value, w_window)
+    )(core, spread, across(spread), gain.reshape(1, -1), w_feat.T, w_value, w_window)
     prev = lax.ppermute(rim, "ctx", [(b, b + 1) for b in range(63)])
     in_x = [[4 * z + x for x in range(4)] for z in range(16)]
     in_low = [[16 * h + 4 * l + x for l in range(4)] for h in range(4) for x in range(4)]
     in_high = [[16 * h + 4 * l + x for h in range(4)] for l in range(4) for x in range(4)]
     before_x, states = level(states, in_x, ctx % 4)
+    numerator = call(inner_kernel, shape((count, 128), F32))(feats, v_lin)
+    states, numerator = lax.optimization_barrier((states, numerator))
     before_low, states = level(states, in_low, (ctx // 4) % 4)
+    win_out = call_with_scalar(attend_kernel, shape((count, 128)), 3)(ctx.astype(jnp.int32).reshape(1), q_win, rim, prev)
+    states, win_out, w_later = lax.optimization_barrier((states, win_out, w_out))
+    win_other = across(win_out)
+    w_other = across(w_later)
     before_high, _ = level(states, in_high, ctx // 16)
     prefix = (before_x + before_low + before_high).astype(BF)
-    win_out, numerator = call_with_scalar(attend_kernel, [shape((count, 128)), shape((count, 128), F32)], 5)(
-        ctx.astype(jnp.int32).reshape(1), q_win, rim, prev, feats, v_lin
-    )
-    mix, other = call_with_scalar(mix_kernel, [shape((count, 256)), shape((4, count, 256))], 5)(
-        core, feats, numerator, prefix, win_out, w_out
-    )
-    got = lax.ppermute(other, "head", [(h, h ^ 1) for h in range(8)])
-    summed = call_with_scalar(join_kernel, shape((4, count, 256)), 3)(core, mix, w_out, got)
+    lin_out = call(linear_kernel, shape((count, 128)))(feats, numerator, prefix)
+    lin_other = across(lin_out)
+    summed = call_with_scalar(output_kernel, shape((4, count, 256)), 6)(
+        core, lin_out, win_out, w_out, lin_other, win_other, w_other
+    )
     parts = lax.all_to_all(summed, "head", 0, 0, tiled=True, axis_index_groups=along_y)
     return jnp.sum(parts.astype(F32), axis=0).astype(BF)
 

time: 150 us -> 120 us (0.80)
  the two profiles are of different devices: /device:TPU:32 before, /device:TPU:1 now
where the time goes in v2:
time: 120 us
  starting transfers between devices  50.2 us (42%)
  blocking collectives  32.9 us (27%)
  waiting for transfers between devices  21.5 us (18%)
  Pallas kernels  8.23 us (7%)
  local copies, waits for them, and re-layouts  5.32 us (4%)
  other arithmetic  1.29 us (1%)
    all_to_all x3, starting transfers between devices, level(): lax.all_to_all(states, 'ctx', 0, 0, tiled=True, axis_index_groups=groups)  27.5 us
    ppermute x4, starting transfers between devices, across(): return lax.ppermute(value, 'head', [(h, h ^ 1) for h in range(8)])  20.5 us
    all_to_all x1, blocking collectives, shards(): lax.all_to_all(summed, 'head', 0, 0, tiled=True, axis_index_groups=along_y)  17.3 us
    all_to_all x1, blocking collectives, shards(): lax.all_to_all(jnp.broadcast_to(tokens[None], (4,) + tokens.shape), 'head...  15.6 us
    all_to_all x3, waiting for transfers between devices, level(): lax.all_to_all(states, 'ctx', 0, 0, tiled=True, axis_index_groups=groups)  14.7 us
    pallas_call x1, Pallas kernels, shards(): call_with_scalar(project_kernel, [shape((count, 32)), shape((count, 128))...  5.03 us
    ppermute x1, waiting for transfers between devices, shards(): prev = lax.ppermute(rim, 'ctx', [(b, b + 1) for b in range(63)])  3.5 us
    ppermute x4, waiting for transfers between devices, across(): return lax.ppermute(value, 'head', [(h, h ^ 1) for h in range(8)])  3.33 us
  transfers between devices with their start and end apart: 8, of which 5 were waited for; matrix products, arithmetic and copies ran while one was open for 0% of the time, Pallas kernels for 2%

profile of v2, /device:TPU:1, one launch (start us, length us, event | category | flops | bytes accessed | tf_op | source)
XLA Modules:
  0.0 119.7 jit_solution(12112750613255133028)
XLA Ops:
  0.0 1.0 broadcast_in_dim.42
  1.0 0.0 copy-start
  1.0 0.0 copy-start.1
  1.0 15.6 %all_to_all.25.mine_ref = bf16[4,512,256]{2,1,0:T(8,128)(2,1)S(1)} all-to-all(bf16[4,512,256]{2,1,0:T(8,128)(2,1)S(1)} %broadcast_in_dim.42), channel_id=1, replica_groups={{0,2,4,6},{1,3,5,7},{8,10,12,14},{9,11,13,15},{16,18,20,22},{17,19,21,2..., dimensions={0} | all-to-all | bytes 2097152 | tf_op jit(solution)/shard_map/all_to_all | solution.py:192
  16.6 7.3 %collective-permute-start = (bf16[4,512,256]{2,1,0:T(8,128)(2,1)S(1)}, bf16[4,512,256]{2,1,0:T(8,128)(2,1)}, u32[]{:S(2)}, u32[]{:S(2)}) collective-permute-start(bf16[4,512,256]{2,1,0:T(8,128)(2,1)S(1)} %all_to_all.25.mine_ref), channel_id=1, source_target_pairs={{0,1},{1,0},{2,3},{3,2},{4,5},{5,4},{6,7},{7,6},{8,9},{9,8},{10,11... | collective-permute-start | bytes 3145736 | tf_op jit(solution)/shard_map/ppermute | solution.py:187
  24.0 0.0 copy-start.9
  24.0 2.4 %collective-permute-done.other_ref = bf16[4,512,256]{2,1,0:T(8,128)(2,1)} collective-permute-done((bf16[4,512,256]{2,1,0:T(8,128)(2,1)S(1)}, bf16[4,512,256]{2,1,0:T(8,128)(2,1)}, u32[]{:S(2)}, u32[]{:S(2)}) %collective-permute-start) | collective-permute-done | bytes 1048608 | tf_op jit(solution)/shard_map/ppermute | solution.py:187
  26.3 0.0 copy-done
  26.3 0.0 copy-done.1
  26.3 0.0 copy-done.9
  26.4 0.0 copy-start.4
  26.4 0.9 copy-done.4
  27.3 5.0 %shard_map.64 = (bf16[512,32]{1,0:T(8,128)(2,1)S(1)}, bf16[512,128]{1,0:T(8,128)(2,1)S(1)}, bf16[512,128]{1,0:T(8,128)(2,1)S(1)}, bf16[512,256]{1,0:T(8,128)(2,1)S(1)}, bf16[4,160,128]{2,1,0:T(8,128)(2,1)S(1)}) custom-call(s32[1]{0:T(128)} %bitcast.core_ref, bf16[4,512,256]{2,1,0:T(8,128)(2,1)S(1)} %all_to_all.25.mine_ref, ...), custom_call_target="tpu_custom_call" | custom-call | tf_op jit(solution)/shard_map/pallas_call | solution.py:195
  32.3 0.0 copy-start.3
  32.3 0.7 copy-done.3
  33.0 0.7 copy-done.5
  33.6 0.6 copy-done.7
  34.3 4.1 %all-to-all-start.1 = ((bf16[4,160,128]{2,1,0:T(8,128)(2,1)}), bf16[4,160,128]{2,1,0:T(8,128)(2,1)S(1)}, u32[]{:S(2)}, u32[]{:S(2)}) async-start(bf16[4,160,128]{2,1,0:T(8,128)(2,1)} %copy-done.3), calls=%async_computation.1 | async-start | bytes 327680 | tf_op jit(solution)/shard_map/all_to_all | solution.py:171
  38.4 0.0 copy-done.8
  38.4 0.6 shard_map.65.num_ref
  39.0 0.0 copy-start.2
  39.0 4.4 %all-to-all-done.1 = bf16[4,160,128]{2,1,0:T(8,128)(2,1)S(1)} async-done(((bf16[4,160,128]{2,1,0:T(8,128)(2,1)}), bf16[4,160,128]{2,1,0:T(8,128)(2,1)S(1)}, u32[]{:S(2)}, u32[]{:S(2)}) %all-to-all-start.1) | async-done | bytes 163872 | tf_op jit(solution)/shard_map/all_to_all | solution.py:171
  43.5 0.7 broadcast_in_dim.43
  44.2 0.0 copy-done.10
  44.2 5.6 %all-to-all-start.2 = ((bf16[4,160,128]{2,1,0:T(8,128)(2,1)}), bf16[4,160,128]{2,1,0:T(8,128)(2,1)S(1)}, u32[]{:S(2)}, u32[]{:S(2)}) async-start(bf16[4,160,128]{2,1,0:T(8,128)(2,1)} %broadcast_in_dim.43), calls=%async_computation.2 | async-start | bytes 327680 | tf_op jit(solution)/shard_map/all_to_all | solution.py:171
  49.8 2.2 %collective-permute-start.1 = (bf16[512,256]{1,0:T(8,128)(2,1)S(1)}, bf16[512,256]{1,0:T(8,128)(2,1)S(1)}, u32[]{:S(2)}, u32[]{:S(2)}) collective-permute-start(bf16[512,256]{1,0:T(8,128)(2,1)S(1)} %get-tuple-element.21.own_ref), channel_id=1, source_target_pairs={{0,8},{8,16},{16,24},{24,32},{32,40},{40,48},{48,56},{56,64},{64,7... | collective-permute-start | bytes 786440 | tf_op jit(solution)/shard_map/ppermute | solution.py:201
  52.0 3.5 %collective-permute-done.1.prev_ref = bf16[512,256]{1,0:T(8,128)(2,1)S(1)} collective-permute-done((bf16[512,256]{1,0:T(8,128)(2,1)S(1)}, bf16[512,256]{1,0:T(8,128)(2,1)S(1)}, u32[]{:S(2)}, u32[]{:S(2)}) %collective-permute-start.1) | collective-permute-done | bytes 262176 | tf_op jit(solution)/shard_map/ppermute | solution.py:201
  55.5 0.0 copy-done.6
  55.5 1.3 %shard_map.66.win_ref = bf16[512,128]{1,0:T(8,128)(2,1)S(1)} custom-call(s32[1]{0:T(128)} %bitcast.3.first_ref, bf16[512,128]{1,0:T(8,128)(2,1)S(1)} %copy-done.6, bf16[512,256]{1,0:T(8,128)(2,1)S(1)} %get-tuple-element.21.own_ref, bf16[512,256]{1,0:T(8,128)(2,1)S(1)} %collective-permute-done.1.prev_ref), custom_call_target="tpu_custom_call" | custom-call | tf_op jit(solution)/shard_map/pallas_call | solution.py:209
  56.8 0.0 all-to-all-done.2
  56.9 0.7 broadcast_in_dim.48
  57.6 0.0 copy-done.2
  57.6 5.0 %collective-permute-start.4 = (bf16[256,2048]{1,0:T(8,128)(2,1)S(1)}, bf16[256,2048]{1,0:T(8,128)(2,1)S(1)}, u32[]{:S(2)}, u32[]{:S(2)}) collective-permute-start(bf16[256,2048]{1,0:T(8,128)(2,1)S(1)} %copy-done.2), channel_id=1, source_target_pairs={{0,1},{1,0},{2,3},{3,2},{4,5},{5,4},{6,7},{7,6},{8,9},{9,8},{10,11... | collective-permute-start | bytes 3145736 | tf_op jit(solution)/shard_map/ppermute | solution.py:187
  62.6 17.8 %all-to-all-start.3 = ((bf16[4,160,128]{2,1,0:T(8,128)(2,1)}), bf16[4,160,128]{2,1,0:T(8,128)(2,1)S(1)}, u32[]{:S(2)}, u32[]{:S(2)}) async-start(bf16[4,160,128]{2,1,0:T(8,128)(2,1)} %broadcast_in_dim.48), calls=%async_computation.3 | async-start | bytes 327680 | tf_op jit(solution)/shard_map/all_to_all | solution.py:171
  80.4 0.0 copy-done.11
  80.4 0.1 select_reduce_fusion.2
  80.5 2.2 %collective-permute-start.3 = (bf16[512,128]{1,0:T(8,128)(2,1)S(1)}, bf16[512,128]{1,0:T(8,128)(2,1)S(1)}, u32[]{:S(2)}, u32[]{:S(2)}) collective-permute-start(bf16[512,128]{1,0:T(8,128)(2,1)S(1)} %shard_map.66.win_ref), channel_id=1, source_target_pairs={{0,1},{1,0},{2,3},{3,2},{4,5},{5,4},{6,7},{7,6},{8,9},{9,8},{10,11... | collective-permute-start | bytes 393224 | tf_op jit(solution)/shard_map/ppermute | solution.py:187
  82.7 0.1 select_reduce_fusion.1
  82.8 10.3 %all-to-all-done.3 = bf16[4,160,128]{2,1,0:T(8,128)(2,1)S(1)} async-done(((bf16[4,160,128]{2,1,0:T(8,128)(2,1)}), bf16[4,160,128]{2,1,0:T(8,128)(2,1)S(1)}, u32[]{:S(2)}, u32[]{:S(2)}) %all-to-all-start.3) | async-done | bytes 163872 | tf_op jit(solution)/shard_map/all_to_all | solution.py:171
  93.1 0.1 select_reduce_fusion
  93.2 0.6 shard_map.67.lin_ref
  93.8 6.0 %collective-permute-start.2 = (bf16[512,128]{1,0:T(8,128)(2,1)S(1)}, bf16[512,128]{1,0:T(8,128)(2,1)S(1)}, u32[]{:S(2)}, u32[]{:S(2)}) collective-permute-start(bf16[512,128]{1,0:T(8,128)(2,1)S(1)} %shard_map.67.lin_ref), channel_id=1, source_target_pairs={{0,1},{1,0},{2,3},{3,2},{4,5},{5,4},{6,7},{7,6},{8,9},{9,8},{10,11... | collective-permute-start | bytes 393224 | tf_op jit(solution)/shard_map/ppermute | solution.py:187
  99.8 0.0 collective-permute-done.3.win2_ref
  99.8 1.0 collective-permute-done.2.lin2_ref
  100.8 0.0 collective-permute-done.4.w2_ref
  100.8 0.7 shard_map.68
  101.5 17.3 %all_to_all.26 = bf16[4,512,256]{2,1,0:T(8,128)(2,1)S(1)} all-to-all(bf16[4,512,256]{2,1,0:T(8,128)(2,1)S(1)} %shard_map.68), channel_id=1, replica_groups={{0,2,4,6},{1,3,5,7},{8,10,12,14},{9,11,13,15},{16,18,20,22},{17,19,21,2..., dimensions={0} | all-to-all | bytes 2097152 | tf_op jit(solution)/shard_map/all_to_all | solution.py:220
  118.8 0.9 reduce_sum.68
  (12 shorter events, 0.1 us)
Async XLA Ops:
  1.0 25.3 %copy-start = (bf16[2048,256]{1,0:T(8,128)(2,1)S(1)}, bf16[2048,256]{1,0:T(8,128)(2,1)}, u32[]{:S(2)}) copy-start(bf16[2048,256]{1,0:T(8,128)(2,1)} %wv_ref.1) | copy-start | bytes 3145732
  1.0 25.3 %copy-start.1 = (bf16[2048,256]{1,0:T(8,128)(2,1)S(1)}, bf16[2048,256]{1,0:T(8,128)(2,1)}, u32[]{:S(2)}) copy-start(bf16[2048,256]{1,0:T(8,128)(2,1)} %ww_ref.1) | copy-start | bytes 3145732
  16.6 9.7 %collective-permute-start = (bf16[4,512,256]{2,1,0:T(8,128)(2,1)S(1)}, bf16[4,512,256]{2,1,0:T(8,128)(2,1)}, u32[]{:S(2)}, u32[]{:S(2)}) collective-permute-start(bf16[4,512,256]{2,1,0:T(8,128)(2,1)S(1)} %all_to_all.25.mine_ref), channel_id=1, source_target_pairs={{0,1},{1,0},{2,3},{3,2},{4,5},{5,4},{6,7},{7,6},{8,9},{9,8},{10,11... | collective-permute-start | bytes 3145736 | tf_op jit(solution)/shard_map/ppermute | solution.py:187
  24.0 2.4 %copy-start.9 = (f32[2048]{0:T(1024)S(1)}, f32[2048]{0:T(1024)}, u32[]{:S(2)}) copy-start(f32[2048]{0:T(1024)} %param.7) | copy-start | bytes 24580
  26.4 0.9 copy-start.4
  32.3 0.7 copy-start.3
  33.0 0.7 copy-start.5
  33.6 0.6 copy-start.7
  34.3 4.2 %copy-start.8 = (bf16[512,128]{1,0:T(8,128)(2,1)S(1)}, bf16[512,128]{1,0:T(8,128)(2,1)}, u32[]{:S(2)}) copy-start(bf16[512,128]{1,0:T(8,128)(2,1)} %copy-done.7) | copy-start | bytes 393220
  34.3 9.2 %all-to-all-start.1 = ((bf16[4,160,128]{2,1,0:T(8,128)(2,1)}), bf16[4,160,128]{2,1,0:T(8,128)(2,1)S(1)}, u32[]{:S(2)}, u32[]{:S(2)}) async-start(bf16[4,160,128]{2,1,0:T(8,128)(2,1)} %copy-done.3), calls=%async_computation.1 | async-start | bytes 327680 | tf_op jit(solution)/shard_map/all_to_all | solution.py:171
  38.4 17.1 %copy-start.6 = (bf16[512,128]{1,0:T(8,128)(2,1)S(1)}, bf16[512,128]{1,0:T(8,128)(2,1)}, u32[]{:S(2)}) copy-start(bf16[512,128]{1,0:T(8,128)(2,1)} %copy-done.5) | copy-start | bytes 393220
  39.0 18.5 %copy-start.2 = (bf16[256,2048]{1,0:T(8,128)(2,1)S(1)}, bf16[256,2048]{1,0:T(8,128)(2,1)}, u32[]{:S(2)}) copy-start(bf16[256,2048]{1,0:T(8,128)(2,1)} %w_ref.1) | copy-start | bytes 3145732
  43.4 0.7 copy-start.10
  44.2 12.7 %all-to-all-start.2 = ((bf16[4,160,128]{2,1,0:T(8,128)(2,1)}), bf16[4,160,128]{2,1,0:T(8,128)(2,1)S(1)}, u32[]{:S(2)}, u32[]{:S(2)}) async-start(bf16[4,160,128]{2,1,0:T(8,128)(2,1)} %broadcast_in_dim.43), calls=%async_computation.2 | async-start | bytes 327680 | tf_op jit(solution)/shard_map/all_to_all | solution.py:171
  49.8 5.8 %collective-permute-start.1 = (bf16[512,256]{1,0:T(8,128)(2,1)S(1)}, bf16[512,256]{1,0:T(8,128)(2,1)S(1)}, u32[]{:S(2)}, u32[]{:S(2)}) collective-permute-start(bf16[512,256]{1,0:T(8,128)(2,1)S(1)} %get-tuple-element.21.own_ref), channel_id=1, source_target_pairs={{0,8},{8,16},{16,24},{24,32},{32,40},{40,48},{48,56},{56,64},{64,7... | collective-permute-start | bytes 786440 | tf_op jit(solution)/shard_map/ppermute | solution.py:201
  57.6 22.8 %copy-start.11 = (bf16[4,160,128]{2,1,0:T(8,128)(2,1)S(1)}, bf16[4,160,128]{2,1,0:T(8,128)(2,1)}, u32[]{:S(2)}) copy-start(bf16[4,160,128]{2,1,0:T(8,128)(2,1)} %copy-done.10) | copy-start | bytes 491524
  57.6 43.2 %collective-permute-start.4 = (bf16[256,2048]{1,0:T(8,128)(2,1)S(1)}, bf16[256,2048]{1,0:T(8,128)(2,1)S(1)}, u32[]{:S(2)}, u32[]{:S(2)}) collective-permute-start(bf16[256,2048]{1,0:T(8,128)(2,1)S(1)} %copy-done.2), channel_id=1, source_target_pairs={{0,1},{1,0},{2,3},{3,2},{4,5},{5,4},{6,7},{7,6},{8,9},{9,8},{10,11... | collective-permute-start | bytes 3145736 | tf_op jit(solution)/shard_map/ppermute | solution.py:187
  62.6 30.6 %all-to-all-start.3 = ((bf16[4,160,128]{2,1,0:T(8,128)(2,1)}), bf16[4,160,128]{2,1,0:T(8,128)(2,1)S(1)}, u32[]{:S(2)}, u32[]{:S(2)}) async-start(bf16[4,160,128]{2,1,0:T(8,128)(2,1)} %broadcast_in_dim.48), calls=%async_computation.3 | async-start | bytes 327680 | tf_op jit(solution)/shard_map/all_to_all | solution.py:171
  80.5 19.3 %collective-permute-start.3 = (bf16[512,128]{1,0:T(8,128)(2,1)S(1)}, bf16[512,128]{1,0:T(8,128)(2,1)S(1)}, u32[]{:S(2)}, u32[]{:S(2)}) collective-permute-start(bf16[512,128]{1,0:T(8,128)(2,1)S(1)} %shard_map.66.win_ref), channel_id=1, source_target_pairs={{0,1},{1,0},{2,3},{3,2},{4,5},{5,4},{6,7},{7,6},{8,9},{9,8},{10,11... | collective-permute-start | bytes 393224 | tf_op jit(solution)/shard_map/ppermute | solution.py:187
  93.8 6.9 %collective-permute-start.2 = (bf16[512,128]{1,0:T(8,128)(2,1)S(1)}, bf16[512,128]{1,0:T(8,128)(2,1)S(1)}, u32[]{:S(2)}, u32[]{:S(2)}) collective-permute-start(bf16[512,128]{1,0:T(8,128)(2,1)S(1)} %shard_map.67.lin_ref), channel_id=1, source_target_pairs={{0,1},{1,0},{2,3},{3,2},{4,5},{5,4},{6,7},{7,6},{8,9},{9,8},{10,11... | collective-permute-start | bytes 393224 | tf_op jit(solution)/shard_map/ppermute | solution.py:187

commit v3 on v2

--- a/solution.py
+++ b/solution.py
@@ -10,7 +10,9 @@
 
 EPS = 1e-05
 FEAT = 16
-ROWS = 160
+PARTS = 64
+DEEP = 3
+ROWS = PARTS * DEEP
 BF = jnp.bfloat16
 F32 = jnp.float32
 VMEM = 24 * 1024 * 1024
@@ -103,8 +105,8 @@
     k = feats[:, FEAT:]
     phi = (dot(first, k, NT) + add_first) * (dot(second, k, NT) + add_second) * scale
     state = dot(phi.astype(BF), vlin).astype(BF)
-    for i in range(4):
-        state_ref[i, :, :] = state
+    for i in range(DEEP):
+        state_ref[:, i, :] = state[PARTS * i : PARTS * (i + 1), :]
     windowed = dot(n, ww_ref[...]).astype(BF)
     qwin_ref[...] = windowed[:, :128]
     rim_ref[:, :128] = windowed[:, 128:]
@@ -153,7 +155,8 @@
     scale, add_first, add_second = weights_of((1, ROWS), 1, True)
     q = feat_ref[:, :FEAT]
     phi = (dot(q, first) + add_first) * (dot(q, second) + add_second) * scale
-    numerator = num_ref[...] + dot(phi.astype(BF), prefix_ref[...])
+    prefix = jnp.concatenate([prefix_ref[:, i, :] for i in range(DEEP)], axis=0)
+    numerator = num_ref[...] + dot(phi.astype(BF), prefix)
     mean = jnp.mean(numerator * numerator, axis=1, keepdims=True)
     lin_ref[...] = (numerator * lax.rsqrt(mean + EPS)).astype(BF)
 
@@ -167,13 +170,11 @@
         sum_ref[y, :, :] = total.astype(BF)
 
 
-def level(states, groups, place):
-    got = lax.all_to_all(states, "ctx", 0, 0, tiled=True, axis_index_groups=groups)
-    wide = got.astype(F32)
-    order = lax.broadcasted_iota(jnp.int32, (4, 1, 1), 0)
-    before = jnp.sum(jnp.where(order < place, wide, 0.0), axis=0)
-    total = jnp.sum(wide, axis=0).astype(BF)
-    return before, jnp.broadcast_to(total[None], states.shape)
+def prefix_kernel(got_ref, out_ref):
+    earlier = lax.broadcasted_iota(jnp.int32, (PARTS, PARTS), 1) < lax.broadcasted_iota(jnp.int32, (PARTS, PARTS), 0)
+    earlier = earlier.astype(F32).astype(BF)
+    for i in range(DEEP):
+        out_ref[:, i, :] = dot(earlier, got_ref[:, i, :]).astype(BF)
 
 
 def shards(tokens, gain, w_feat, w_value, w_window, w_out):
@@ -194,24 +195,21 @@
     )
     feats, v_lin, q_win, rim, states = call_with_scalar(
         project_kernel,
-        [shape((count, 32)), shape((count, 128)), shape((count, 128)), shape((count, 256)), shape((4, ROWS, 128))],
+        [shape((count, 32)), shape((count, 128)), shape((count, 128)), shape((count, 256)), shape((PARTS, DEEP, 128))],
         6,
         [pltpu.VMEM((count, 2048), BF)],
     )(core, spread, across(spread), gain.reshape(1, -1), w_feat.T, w_value, w_window)
-    prev = lax.ppermute(rim, "ctx", [(b, b + 1) for b in range(63)])
-    in_x = [[4 * z + x for x in range(4)] for z in range(16)]
-    in_low = [[16 * h + 4 * l + x for l in range(4)] for h in range(4) for x in range(4)]
-    in_high = [[16 * h + 4 * l + x for h in range(4)] for l in range(4) for x in range(4)]
-    before_x, states = level(states, in_x, ctx % 4)
     numerator = call(inner_kernel, shape((count, 128), F32))(feats, v_lin)
-    states, numerator = lax.optimization_barrier((states, numerator))
-    before_low, states = level(states, in_low, (ctx // 4) % 4)
+    rim, numerator = lax.optimization_barrier((rim, numerator))
+    prev = lax.ppermute(rim, "ctx", [(b, b + 1) for b in range(PARTS - 1)])
+    pieces = lax.all_to_all(states, "ctx", 0, 0, tiled=True)
+    sums = call(prefix_kernel, shape((PARTS, DEEP, 128)))(pieces)
+    sums, prev = lax.optimization_barrier((sums, prev))
+    prefix = lax.all_to_all(sums, "ctx", 0, 0, tiled=True)
     win_out = call_with_scalar(attend_kernel, shape((count, 128)), 3)(ctx.astype(jnp.int32).reshape(1), q_win, rim, prev)
-    states, win_out, w_later = lax.optimization_barrier((states, win_out, w_out))
+    w_later, win_out = lax.optimization_barrier((w_out, win_out))
+    w_other = across(w_later)
     win_other = across(win_out)
-    w_other = across(w_later)
-    before_high, _ = level(states, in_high, ctx // 16)
-    prefix = (before_x + before_low + before_high).astype(BF)
     lin_out = call(linear_kernel, shape((count, 128)))(feats, numerator, prefix)
     lin_other = across(lin_out)
     summed = call_with_scalar(output_kernel, shape((4, count, 256)), 6)(

time: 120 us -> 119 us (level)
  waiting for transfers between devices: 21.5 us -> 29.6 us
  starting transfers between devices: 50.2 us -> 42.8 us
  local copies, waits for them, and re-layouts: 5.32 us -> 2.87 us
    all_to_all x3 -> x2, waiting for transfers between devices: 14.7 us -> 26.3 us  [the longest x1 14 us: shards(): pieces = lax.all_to_all(states, 'ctx', 0, 0, tiled=True)]
    all_to_all x3 -> x2, starting transfers between devices: 27.5 us -> 22.6 us  [the longest x1 18 us: shards(): pieces = lax.all_to_all(states, 'ctx', 0, 0, tiled=True)]
    ppermute x1, waiting for transfers between devices: 3.5 us -> 0.01 us  [shards(): prev = lax.ppermute(rim, 'ctx', [(b, b + 1) for b in range(PARTS - 1)])]
    ppermute x4, starting transfers between devices: 20.5 us -> 17.1 us  [across(): return lax.ppermute(value, 'head', [(h, h ^ 1) for h in range(8)])]
    broadcast_in_dim x2 -> x0, local copies, waits for them, and re-layouts: 1.39 us -> none  [level(): return (before, jnp.broadcast_to(total[None], states.shape))]
    unnamed x24 -> x16, local copies, waits for them, and re-layouts: 2.9 us -> 1.85 us
  transfers between devices with their start and end apart: 8 -> 7, of which waited for: 5 -> 4; matrix products, arithmetic and copies ran while one was open for 0% -> 0% of each run, Pallas kernels for 2% -> 1%
where the time goes in v3:
time: 119 us; the launch traced here: 118 us
  starting transfers between devices  42.8 us (36%)
  blocking collectives  32.9 us (28%)
  waiting for transfers between devices  29.6 us (25%)
  Pallas kernels  9.16 us (8%)
  local copies, waits for them, and re-layouts  2.87 us (2%)
    all_to_all x1, starting transfers between devices, shards(): pieces = lax.all_to_all(states, 'ctx', 0, 0, tiled=True)  18 us
    all_to_all x1, blocking collectives, shards(): lax.all_to_all(summed, 'head', 0, 0, tiled=True, axis_index_groups=along_y)  17.3 us
    ppermute x4, starting transfers between devices, across(): return lax.ppermute(value, 'head', [(h, h ^ 1) for h in range(8)])  17.1 us
    all_to_all x1, blocking collectives, shards(): lax.all_to_all(jnp.broadcast_to(tokens[None], (4,) + tokens.shape), 'head...  15.6 us
    all_to_all x1, waiting for transfers between devices, shards(): pieces = lax.all_to_all(states, 'ctx', 0, 0, tiled=True)  14 us
    all_to_all x1, waiting for transfers between devices, shards(): prefix = lax.all_to_all(sums, 'ctx', 0, 0, tiled=True)  12.3 us
    pallas_call x1, Pallas kernels, shards(): call_with_scalar(project_kernel, [shape((count, 32)), shape((count, 128))...  5.04 us
    all_to_all x1, starting transfers between devices, shards(): prefix = lax.all_to_all(sums, 'ctx', 0, 0, tiled=True)  4.61 us
  transfers between devices with their start and end apart: 7, of which 4 were waited for; matrix products, arithmetic and copies ran while one was open for 0% of the time, Pallas kernels for 1%

profile of v3, /device:TPU:1, one launch (start us, length us, event | category | flops | bytes accessed | tf_op | source)
XLA Modules:
  0.0 118.5 jit_solution(14721730319134792446)
XLA Ops:
  0.0 1.0 broadcast_in_dim.2
  1.0 0.0 copy-start
  1.0 0.0 copy-start.1
  1.0 15.6 %all_to_all.20.mine_ref = bf16[4,512,256]{2,1,0:T(8,128)(2,1)S(1)} all-to-all(bf16[4,512,256]{2,1,0:T(8,128)(2,1)S(1)} %broadcast_in_dim.2), channel_id=1, replica_groups={{0,2,4,6},{1,3,5,7},{8,10,12,14},{9,11,13,15},{16,18,20,22},{17,19,21,2..., dimensions={0} | all-to-all | bytes 2097152 | tf_op jit(solution)/shard_map/all_to_all | solution.py:193
  16.6 7.3 %collective-permute-start = (bf16[4,512,256]{2,1,0:T(8,128)(2,1)S(1)}, bf16[4,512,256]{2,1,0:T(8,128)(2,1)}, u32[]{:S(2)}, u32[]{:S(2)}) collective-permute-start(bf16[4,512,256]{2,1,0:T(8,128)(2,1)S(1)} %all_to_all.20.mine_ref), channel_id=1, source_target_pairs={{0,1},{1,0},{2,3},{3,2},{4,5},{5,4},{6,7},{7,6},{8,9},{9,8},{10,11... | collective-permute-start | bytes 3145736 | tf_op jit(solution)/shard_map/ppermute | solution.py:188
  24.0 0.0 copy-start.7
  24.0 2.4 %collective-permute-done.other_ref = bf16[4,512,256]{2,1,0:T(8,128)(2,1)} collective-permute-done((bf16[4,512,256]{2,1,0:T(8,128)(2,1)S(1)}, bf16[4,512,256]{2,1,0:T(8,128)(2,1)}, u32[]{:S(2)}, u32[]{:S(2)}) %collective-permute-start) | collective-permute-done | bytes 1048608 | tf_op jit(solution)/shard_map/ppermute | solution.py:188
  26.3 0.0 copy-done
  26.3 0.0 copy-done.1
  26.3 0.0 copy-done.7
  26.4 0.0 copy-start.3
  26.4 0.9 copy-done.3
  27.3 5.0 %shard_map.64 = (bf16[512,32]{1,0:T(8,128)(2,1)S(1)}, bf16[512,128]{1,0:T(8,128)(2,1)S(1)}, bf16[512,128]{1,0:T(8,128)(2,1)S(1)}, bf16[512,256]{1,0:T(8,128)(2,1)S(1)}, bf16[64,3,128]{2,1,0:T(4,128)(2,1)S(1)}) custom-call(s32[1]{0:T(128)} %bitcast.core_ref, bf16[4,512,256]{2,1,0:T(8,128)(2,1)S(1)} %all_to_all.20.mine_ref, ...), custom_call_target="tpu_custom_call" | custom-call | tf_op jit(solution)/shard_map/pallas_call | solution.py:196
  32.3 0.0 copy-start.4
  32.3 0.0 copy-start.6
  32.3 0.0 copy-start.2
  32.3 0.6 shard_map.65.num_ref
  32.9 0.0 copy-done.4
  33.0 0.0 copy-done.6
  33.0 3.1 %collective-permute-start.1 = (bf16[512,256]{1,0:T(8,128)(2,1)S(1)}, bf16[512,256]{1,0:T(8,128)(2,1)S(1)}, u32[]{:S(2)}, u32[]{:S(2)}) collective-permute-start(bf16[512,256]{1,0:T(8,128)(2,1)S(1)} %get-tuple-element.21.own_ref), channel_id=1, source_target_pairs={{0,8},{8,16},{16,24},{24,32},{32,40},{40,48},{48,56},{56,64},{64,7... | collective-permute-start | bytes 786440 | tf_op jit(solution)/shard_map/ppermute | solution.py:204
  36.1 18.0 %all-to-all-start.1 = ((bf16[64,3,128]{2,1,0:T(4,128)(2,1)}), bf16[64,3,128]{2,1,0:T(4,128)(2,1)S(1)}, u32[]{:S(2)}, u32[]{:S(2)}) async-start(bf16[64,3,128]{2,1,0:T(4,128)(2,1)} %copy-done.6), calls=%async_computation.1 | async-start | bytes 131072 | tf_op jit(solution)/shard_map/all_to_all | solution.py:205
  54.1 14.0 %all-to-all-done.1.got_ref = bf16[64,3,128]{2,1,0:T(4,128)(2,1)S(1)} async-done(((bf16[64,3,128]{2,1,0:T(4,128)(2,1)}), bf16[64,3,128]{2,1,0:T(4,128)(2,1)S(1)}, u32[]{:S(2)}, u32[]{:S(2)}) %all-to-all-start.1) | async-done | bytes 49184 | tf_op jit(solution)/shard_map/all_to_all | solution.py:205
  68.1 0.9 shard_map.66
  69.0 0.0 collective-permute-done.1.prev_ref
  69.0 0.0 copy-start.5
  69.0 0.9 copy-done.5
  69.9 1.3 %shard_map.68.win_ref = bf16[512,128]{1,0:T(8,128)(2,1)S(1)} custom-call(s32[1]{0:T(128)} %bitcast.3.first_ref, bf16[512,128]{1,0:T(8,128)(2,1)S(1)} %copy-done.5, bf16[512,256]{1,0:T(8,128)(2,1)S(1)} %get-tuple-element.21.own_ref, bf16[512,256]{1,0:T(8,128)(2,1)S(1)} %collective-permute-done.1.prev_ref), custom_call_target="tpu_custom_call" | custom-call | tf_op jit(solution)/shard_map/pallas_call | solution.py:209
  71.2 0.0 copy-done.2
  71.2 4.0 %collective-permute-start.4 = (bf16[256,2048]{1,0:T(8,128)(2,1)S(1)}, bf16[256,2048]{1,0:T(8,128)(2,1)S(1)}, u32[]{:S(2)}, u32[]{:S(2)}) collective-permute-start(bf16[256,2048]{1,0:T(8,128)(2,1)S(1)} %copy-done.2), channel_id=1, source_target_pairs={{0,1},{1,0},{2,3},{3,2},{4,5},{5,4},{6,7},{7,6},{8,9},{9,8},{10,11... | collective-permute-start | bytes 3145736 | tf_op jit(solution)/shard_map/ppermute | solution.py:188
  75.2 4.6 %all-to-all-start.2 = ((bf16[64,3,128]{2,1,0:T(4,128)(2,1)}), bf16[64,3,128]{2,1,0:T(4,128)(2,1)S(1)}, u32[]{:S(2)}, u32[]{:S(2)}) async-start(bf16[64,3,128]{2,1,0:T(4,128)(2,1)} %shard_map.66), calls=%async_computation.2 | async-start | bytes 131072 | tf_op jit(solution)/shard_map/all_to_all | solution.py:208
  79.9 1.9 %collective-permute-start.3 = (bf16[512,128]{1,0:T(8,128)(2,1)S(1)}, bf16[512,128]{1,0:T(8,128)(2,1)S(1)}, u32[]{:S(2)}, u32[]{:S(2)}) collective-permute-start(bf16[512,128]{1,0:T(8,128)(2,1)S(1)} %shard_map.68.win_ref), channel_id=1, source_target_pairs={{0,1},{1,0},{2,3},{3,2},{4,5},{5,4},{6,7},{7,6},{8,9},{9,8},{10,11... | collective-permute-start | bytes 393224 | tf_op jit(solution)/shard_map/ppermute | solution.py:188
  81.8 12.3 %all-to-all-done.2.prefix_ref = bf16[64,3,128]{2,1,0:T(4,128)(2,1)S(1)} async-done(((bf16[64,3,128]{2,1,0:T(4,128)(2,1)}), bf16[64,3,128]{2,1,0:T(4,128)(2,1)S(1)}, u32[]{:S(2)}, u32[]{:S(2)}) %all-to-all-start.2) | async-done | bytes 49184 | tf_op jit(solution)/shard_map/all_to_all | solution.py:208
  94.1 0.6 shard_map.67.lin_ref
  94.7 3.9 %collective-permute-start.2 = (bf16[512,128]{1,0:T(8,128)(2,1)S(1)}, bf16[512,128]{1,0:T(8,128)(2,1)S(1)}, u32[]{:S(2)}, u32[]{:S(2)}) collective-permute-start(bf16[512,128]{1,0:T(8,128)(2,1)S(1)} %shard_map.67.lin_ref), channel_id=1, source_target_pairs={{0,1},{1,0},{2,3},{3,2},{4,5},{5,4},{6,7},{7,6},{8,9},{9,8},{10,11... | collective-permute-start | bytes 393224 | tf_op jit(solution)/shard_map/ppermute | solution.py:188
  98.6 0.0 collective-permute-done.3.win2_ref
  98.6 1.0 collective-permute-done.2.lin2_ref
  99.6 0.0 collective-permute-done.4.w2_ref
  99.6 0.7 shard_map.69
  100.3 17.3 %all_to_all.21 = bf16[4,512,256]{2,1,0:T(8,128)(2,1)S(1)} all-to-all(bf16[4,512,256]{2,1,0:T(8,128)(2,1)S(1)} %shard_map.69), channel_id=1, replica_groups={{0,2,4,6},{1,3,5,7},{8,10,12,14},{9,11,13,15},{16,18,20,22},{17,19,21,2..., dimensions={0} | all-to-all | bytes 2097152 | tf_op jit(solution)/shard_map/all_to_all | solution.py:218
  117.6 0.9 reduce_sum.12
Async XLA Ops:
  1.0 25.3 %copy-start = (bf16[2048,256]{1,0:T(8,128)(2,1)S(1)}, bf16[2048,256]{1,0:T(8,128)(2,1)}, u32[]{:S(2)}) copy-start(bf16[2048,256]{1,0:T(8,128)(2,1)} %wv_ref.1) | copy-start | bytes 3145732
  1.0 25.3 %copy-start.1 = (bf16[2048,256]{1,0:T(8,128)(2,1)S(1)}, bf16[2048,256]{1,0:T(8,128)(2,1)}, u32[]{:S(2)}) copy-start(bf16[2048,256]{1,0:T(8,128)(2,1)} %ww_ref.1) | copy-start | bytes 3145732
  16.6 9.7 %collective-permute-start = (bf16[4,512,256]{2,1,0:T(8,128)(2,1)S(1)}, bf16[4,512,256]{2,1,0:T(8,128)(2,1)}, u32[]{:S(2)}, u32[]{:S(2)}) collective-permute-start(bf16[4,512,256]{2,1,0:T(8,128)(2,1)S(1)} %all_to_all.20.mine_ref), channel_id=1, source_target_pairs={{0,1},{1,0},{2,3},{3,2},{4,5},{5,4},{6,7},{7,6},{8,9},{9,8},{10,11... | collective-permute-start | bytes 3145736 | tf_op jit(solution)/shard_map/ppermute | solution.py:188
  24.0 2.4 %copy-start.7 = (f32[2048]{0:T(1024)S(1)}, f32[2048]{0:T(1024)}, u32[]{:S(2)}) copy-start(f32[2048]{0:T(1024)} %param.7) | copy-start | bytes 24580
  26.4 0.9 copy-start.3
  32.3 0.7 copy-start.4
  32.3 0.7 copy-start.6
  32.3 38.9 %copy-start.2 = (bf16[256,2048]{1,0:T(8,128)(2,1)S(1)}, bf16[256,2048]{1,0:T(8,128)(2,1)}, u32[]{:S(2)}) copy-start(bf16[256,2048]{1,0:T(8,128)(2,1)} %w_ref.1) | copy-start | bytes 3145732
  33.0 36.1 %collective-permute-start.1 = (bf16[512,256]{1,0:T(8,128)(2,1)S(1)}, bf16[512,256]{1,0:T(8,128)(2,1)S(1)}, u32[]{:S(2)}, u32[]{:S(2)}) collective-permute-start(bf16[512,256]{1,0:T(8,128)(2,1)S(1)} %get-tuple-element.21.own_ref), channel_id=1, source_target_pairs={{0,8},{8,16},{16,24},{24,32},{32,40},{40,48},{48,56},{56,64},{64,7... | collective-permute-start | bytes 786440 | tf_op jit(solution)/shard_map/ppermute | solution.py:204
  36.1 32.0 %all-to-all-start.1 = ((bf16[64,3,128]{2,1,0:T(4,128)(2,1)}), bf16[64,3,128]{2,1,0:T(4,128)(2,1)S(1)}, u32[]{:S(2)}, u32[]{:S(2)}) async-start(bf16[64,3,128]{2,1,0:T(4,128)(2,1)} %copy-done.6), calls=%async_computation.1 | async-start | bytes 131072 | tf_op jit(solution)/shard_map/all_to_all | solution.py:205
  69.0 0.9 copy-start.5
  71.2 28.3 %collective-permute-start.4 = (bf16[256,2048]{1,0:T(8,128)(2,1)S(1)}, bf16[256,2048]{1,0:T(8,128)(2,1)S(1)}, u32[]{:S(2)}, u32[]{:S(2)}) collective-permute-start(bf16[256,2048]{1,0:T(8,128)(2,1)S(1)} %copy-done.2), channel_id=1, source_target_pairs={{0,1},{1,0},{2,3},{3,2},{4,5},{5,4},{6,7},{7,6},{8,9},{9,8},{10,11... | collective-permute-start | bytes 3145736 | tf_op jit(solution)/shard_map/ppermute | solution.py:188
  75.2 18.9 %all-to-all-start.2 = ((bf16[64,3,128]{2,1,0:T(4,128)(2,1)}), bf16[64,3,128]{2,1,0:T(4,128)(2,1)S(1)}, u32[]{:S(2)}, u32[]{:S(2)}) async-start(bf16[64,3,128]{2,1,0:T(4,128)(2,1)} %shard_map.66), calls=%async_computation.2 | async-start | bytes 131072 | tf_op jit(solution)/shard_map/all_to_all | solution.py:208
  79.9 18.7 %collective-permute-start.3 = (bf16[512,128]{1,0:T(8,128)(2,1)S(1)}, bf16[512,128]{1,0:T(8,128)(2,1)S(1)}, u32[]{:S(2)}, u32[]{:S(2)}) collective-permute-start(bf16[512,128]{1,0:T(8,128)(2,1)S(1)} %shard_map.68.win_ref), channel_id=1, source_target_pairs={{0,1},{1,0},{2,3},{3,2},{4,5},{5,4},{6,7},{7,6},{8,9},{9,8},{10,11... | collective-permute-start | bytes 393224 | tf_op jit(solution)/shard_map/ppermute | solution.py:188
  94.7 4.9 %collective-permute-start.2 = (bf16[512,128]{1,0:T(8,128)(2,1)S(1)}, bf16[512,128]{1,0:T(8,128)(2,1)S(1)}, u32[]{:S(2)}, u32[]{:S(2)}) collective-permute-start(bf16[512,128]{1,0:T(8,128)(2,1)S(1)} %shard_map.67.lin_ref), channel_id=1, source_target_pairs={{0,1},{1,0},{2,3},{3,2},{4,5},{5,4},{6,7},{7,6},{8,9},{9,8},{10,11... | collective-permute-start | bytes 393224 | tf_op jit(solution)/shard_map/ppermute | solution.py:188

commit v4 on v3

v4 whole, which is shorter than its diff:
```python
import functools
import math

import jax
import jax.numpy as jnp
from jax import lax
from jax.experimental import pallas as pl
from jax.experimental.pallas import tpu as pltpu
from jax.sharding import PartitionSpec as P

EPS = 1e-05
FEAT = 16
QUARTER = 40
ROWS = 4 * QUARTER
BF = jnp.bfloat16
F32 = jnp.float32
VMEM = 12 * 1024 * 1024


def call(kernel, outs, scratch=()):
    return pl.pallas_call(
        kernel,
        out_shape=outs,
        scratch_shapes=scratch,
        compiler_params=pltpu.CompilerParams(vmem_limit_bytes=VMEM),
    )


def call_with_scalar(kernel, outs, count, scratch=(), in_place=None):
    return pl.pallas_call(
        kernel,
        out_shape=outs,
        in_specs=[pl.BlockSpec(memory_space=pltpu.SMEM)]
        + [pl.BlockSpec(memory_space=pltpu.HBM if i + 1 == in_place else pltpu.VMEM) for i in range(count)],
        scratch_shapes=scratch,
        compiler_params=pltpu.CompilerParams(vmem_limit_bytes=VMEM),
    )


def pick(shape, axis):
    r = lax.broadcasted_iota(jnp.int32, shape, axis)
    u = lax.broadcasted_iota(jnp.int32, shape, 1 - axis)
    first = (r >= 1) & (r <= FEAT) & (u == r - 1)
    second = jnp.zeros(shape, jnp.bool_)
    base = 1 + FEAT
    for i in range(FEAT):
        width = FEAT - i
        inside = (r >= base) & (r < base + width)
        first = first | (inside & (u == i))
        second = second | (inside & (u == i + r - base))
        base += width
    return first.astype(F32).astype(BF), second.astype(F32).astype(BF)


def weights_of(shape, axis, twice):
    r = lax.broadcasted_iota(jnp.int32, shape, axis)
    scale = jnp.where(r == 0, 1.0, jnp.where(r <= FEAT, 0.5, 1.0 / (4.0 * math.sqrt(2.0))))
    if twice:
        base = 1 + FEAT
        square = jnp.zeros(shape, jnp.bool_)
        for i in range(FEAT):
            square = square | (r == base)
            base += FEAT - i
        scale = jnp.where((r > FEAT) & ~square, 2.0 * scale, scale)
    one_first = jnp.where(r == 0, 1.0, 0.0)
    one_second = jnp.where(r <= FEAT, 1.0, 0.0)
    return scale, one_first, one_second


NT = (((1,), (1,)), ((), ()))
NN = (((1,), (0,)), ((), ()))


def dot(a, b, dims=NN):
    return lax.dot_general(a, b, dims, preferred_element_type=F32)


def project_kernel(
    core_ref, mine_ref, other_ref, gain_ref, wf_hbm, wv_ref, ww_ref, pack_ref, rim_ref, state_ref, normed, wf_ref, wf_sem
):
    load = pltpu.make_async_copy(wf_hbm, wf_ref, wf_sem)
    load.start()
    count = mine_ref.shape[1]
    step = 128
    core = core_ref[0]
    for r in range(0, count, step):
        total = jnp.zeros((step, 256), F32)
        for source in (mine_ref, other_ref):
            for y in range(4):
                x = source[y, r : r + step, :].astype(F32)
                total = total + x * x
        scale = lax.rsqrt(jnp.sum(total, axis=1, keepdims=True) * (1.0 / 2048.0) + EPS)
        for flip, source in enumerate((mine_ref, other_ref)):
            for y in range(4):
                at = pl.multiple_of((2 * y + (core + flip) % 2) * 256, 256)
                x = source[y, r : r + step, :].astype(F32)
                normed[r : r + step, pl.ds(at, 256)] = (x * scale * gain_ref[0:1, pl.ds(at, 256)]).astype(BF)
    n = normed[...]
    load.wait()
    feats = dot(n, wf_ref[...], NT).astype(BF)
    values = dot(n, wv_ref[...]).astype(BF)
    pack_ref[:, 256:288] = feats
    pack_ref[:, 288:] = jnp.zeros((count, 96), BF)
    vlin = values[:, :128]
    pack_ref[:, 128:256] = vlin
    first, second = pick((ROWS, FEAT), 0)
    scale, add_first, add_second = weights_of((ROWS, 1), 0, False)
    k = feats[:, FEAT:]
    phi = (dot(first, k, NT) + add_first) * (dot(second, k, NT) + add_second) * scale
    state = dot(phi.astype(BF), vlin)
    for i in range(4):
        state_ref[i, :, :] = state[QUARTER * i : QUARTER * (i + 1), :].astype(BF)
    windowed = dot(n, ww_ref[...]).astype(BF)
    pack_ref[:, :128] = windowed[:, :128]
    rim_ref[:, :128] = windowed[:, 128:]
    rim_ref[:, 128:] = values[:, 128:]


def inner_kernel(pack_ref, num_ref):
    count = pack_ref.shape[0]
    tile = 256
    for t in range(count // tile):
        ql = pack_ref[t * tile : (t + 1) * tile, 256 : 256 + FEAT]
        kl = pack_ref[: (t + 1) * tile, 256 + FEAT : 256 + 2 * FEAT]
        inner = dot(ql, kl, NT)
        width = kl.shape[0]
        row = lax.broadcasted_iota(jnp.int32, (tile, width), 0) + t * tile
        col = lax.broadcasted_iota(jnp.int32, (tile, width), 1)
        series = 1.0 + inner * 0.25 + inner * inner * (1.0 / 32.0)
        weight = jnp.where(row >= col, series, 0.0).astype(BF)
        num_ref[t * tile : (t + 1) * tile, :] = dot(weight, pack_ref[: (t + 1) * tile, 128:256])


def attend_kernel(first_ref, pack_ref, own_ref, prev_ref, win_ref):
    count = pack_ref.shape[0]
    tile = 256
    no_prev = first_ref[0] == 0
    for t in range(count // tile):
        q = pack_ref[t * tile : (t + 1) * tile, :128]
        old = prev_ref[t * tile :, :]
        new = own_ref[: (t + 1) * tile, :]
        keys = jnp.concatenate([old[:, :128], new[:, :128]], axis=0)
        vals = jnp.concatenate([old[:, 128:], new[:, 128:]], axis=0)
        width = keys.shape[0]
        scores = dot(q, keys, NT) * (1.0 / math.sqrt(128.0))
        at = lax.broadcasted_iota(jnp.int32, (tile, width), 0) + count
        key = lax.broadcasted_iota(jnp.int32, (tile, width), 1)
        least = jnp.where(no_prev, count - t * tile, 0)
        allowed = (key <= at) & (key > at - count) & (key >= least)
        scores = jnp.where(allowed, scores, -1e30)
        lifted = jnp.exp(scores - jnp.max(scores, axis=1, keepdims=True))
        probs = (lifted / jnp.sum(lifted, axis=1, keepdims=True)).astype(BF)
        win_ref[t * tile : (t + 1) * tile, :] = dot(probs, vals).astype(BF)


def linear_kernel(pack_ref, num_ref, prefix_ref, win_ref, mix_ref):
    first, second = pick((FEAT, ROWS), 1)
    scale, add_first, add_second = weights_of((1, ROWS), 1, True)
    q = pack_ref[:, 256 : 256 + FEAT]
    phi = (dot(q, first) + add_first) * (dot(q, second) + add_second) * scale
    prefix = jnp.concatenate([prefix_ref[i, :, :].astype(F32) for i in range(4)], axis=0).astype(BF)
    numerator = num_ref[...] + dot(phi.astype(BF), prefix)
    mean = jnp.mean(numerator * numerator, axis=1, keepdims=True)
    mix_ref[:, :128] = (numerator * lax.rsqrt(mean + EPS)).astype(BF)
    mix_ref[:, 128:] = win_ref[...]


def output_kernel(core_ref, mix_ref, w_ref, mix2_ref, w2_ref, sum_ref):
    for y in range(4):
        at = pl.multiple_of((2 * y + core_ref[0]) * 256, 256)
        total = dot(mix_ref[...], w_ref[:, pl.ds(at, 256)]) + dot(mix2_ref[...], w2_ref[:, pl.ds(at, 256)])
        sum_ref[y, :, :] = total.astype(BF)


def total_kernel(got_ref, out_ref):
    total = got_ref[0, :, :].astype(F32)
    for i in range(1, 4):
        total = total + got_ref[i, :, :].astype(F32)
    total = total.astype(BF)
    for z in range(16):
        out_ref[z, :, :] = total


def prefix_kernel(place_ref, got_ref, totals_ref, out_ref):
    state = jnp.zeros((QUARTER, 128), F32)
    for z in range(15):
        state = state + jnp.where(z < place_ref[0], totals_ref[z, :, :].astype(F32), 0.0)
    for i in range(4):
        out_ref[i, :, :] = state.astype(BF)
        state = state + got_ref[i, :, :].astype(F32)


def shards(tokens, gain, w_feat, w_value, w_window, w_out):
    count = tokens.shape[0]
    head = lax.axis_index("head")
    ctx = lax.axis_index("ctx")
    core = (head % 2).astype(jnp.int32).reshape(1)
    along_y = [[2 * y + c for y in range(4)] for c in range(2)]

    def across(value):
        return lax.ppermute(value, "head", [(h, h ^ 1) for h in range(8)])

    def shape(dims, kind=BF):
        return jax.ShapeDtypeStruct(dims, kind)

    spread = lax.all_to_all(
        jnp.broadcast_to(tokens[None], (4,) + tokens.shape), "head", 0, 0, tiled=True, axis_index_groups=along_y
    )
    spread, w_later = lax.optimization_barrier((spread, w_out))
    other = across(spread)
    w_other = across(w_later)
    pack, rim, states = call_with_scalar(
        project_kernel,
        [shape((count, 384)), shape((count, 256)), shape((4, QUARTER, 128))],
        6,
        [pltpu.VMEM((count, 2048), BF), pltpu.VMEM((32, 2048), BF), pltpu.SemaphoreType.DMA],
        4,
    )(core, spread, other, gain.reshape(1, -1), w_feat.T, w_value, w_window)
    in_x = [[4 * z + x for x in range(4)] for z in range(16)]
    in_z = [[4 * z + x for z in range(16)] for x in range(4)]
    quarters = lax.all_to_all(states, "ctx", 0, 0, tiled=True, axis_index_groups=in_x)
    rim, quarters = lax.optimization_barrier((rim, quarters))
    totals = lax.all_to_all(
        call(total_kernel, shape((16, QUARTER, 128)))(quarters), "ctx", 0, 0, tiled=True, axis_index_groups=in_z
    )
    prev = lax.ppermute(rim, "ctx", [(b, b + 1) for b in range(63)])
    numerator = call(inner_kernel, shape((count, 128), F32))(pack)
    win_out = call_with_scalar(attend_kernel, shape((count, 128)), 3)(ctx.astype(jnp.int32).reshape(1), pack, rim, prev)
    sums = call_with_scalar(prefix_kernel, shape((4, QUARTER, 128)), 2)(
        (ctx // 4).astype(jnp.int32).reshape(1), quarters, totals
    )
    sums, numerator, win_out = lax.optimization_barrier((sums, numerator, win_out))
    prefix = lax.all_to_all(sums, "ctx", 0, 0, tiled=True, axis_index_groups=in_x)
    mix = call(linear_kernel, shape((count, 256)))(pack, numerator, prefix, win_out)
    summed = call_with_scalar(output_kernel, shape((4, count, 256)), 4)(core, mix, w_out, across(mix), w_other)
    parts = lax.all_to_all(summed, "head", 0, 0, tiled=True, axis_index_groups=along_y)
    return jnp.sum(parts.astype(F32), axis=0).astype(BF)


def solution(mesh):
    placed = (P("ctx", "head"), P(), P(None, "head"), P(None, "head"), P(None, "head"), P("head", None))
    return jax.shard_map(shards, mesh=mesh, in_specs=placed, out_specs=P("ctx", "head"), check_vma=False)
```

time: 119 us -> 108 us (0.908)
  waiting for transfers between devices: 29.6 us -> 9.6 us
  blocking collectives: 32.9 us -> 50.5 us
  starting transfers between devices: 42.8 us -> 32.3 us
  Pallas kernels: 9.16 us -> 10.8 us
    all_to_all x2 -> x1, waiting for transfers between devices: 26.3 us -> 5.38 us  [shards(): lax.all_to_all(call(total_kernel, shape((16, QUARTER, 128)))(quarters), '...]
    all_to_all x0 -> x2, blocking collectives: none -> 17.7 us  [the longest x1 9.51 us: shards(): lax.all_to_all(sums, 'ctx', 0, 0, tiled=True, axis_index_groups=in_x)]
    all_to_all x2 -> x1, starting transfers between devices: 22.6 us -> 14.9 us  [shards(): lax.all_to_all(call(total_kernel, shape((16, QUARTER, 128)))(quarters), '...]
    ppermute x1, waiting for transfers between devices: 0.01 us -> 2.65 us  [shards(): prev = lax.ppermute(rim, 'ctx', [(b, b + 1) for b in range(63)])]
    ppermute x4 -> x3, starting transfers between devices: 17.1 us -> 15.2 us  [across(): return lax.ppermute(value, 'head', [(h, h ^ 1) for h in range(8)])]
    ppermute x4 -> x3, waiting for transfers between devices: 3.33 us -> 1.57 us  [across(): return lax.ppermute(value, 'head', [(h, h ^ 1) for h in range(8)])]
    pallas_call x5 -> x6, Pallas kernels: 7.89 us -> 9.57 us  [the longest x1 5.37 us: shards(): call_with_scalar(project_kernel, [shape((count, 384)), shape((count, 256)...]
  transfers between devices with their start and end apart: 7 -> 5, of which waited for: 4 -> 4; matrix products, arithmetic and copies ran while one was open for 0% -> 0% of each run, Pallas kernels for 1% -> 8%
where the time goes in v4:
time: 108 us; the launch traced here: 107 us
  blocking collectives  50.5 us (47%)
  starting transfers between devices  32.3 us (30%)
  Pallas kernels  10.8 us (10%)
  waiting for transfers between devices  9.6 us (9%)
  local copies, waits for them, and re-layouts  2.87 us (3%)
    all_to_all x1, blocking collectives, shards(): lax.all_to_all(summed, 'head', 0, 0, tiled=True, axis_index_groups=along_y)  17.3 us
    all_to_all x1, blocking collectives, shards(): lax.all_to_all(jnp.broadcast_to(tokens[None], (4,) + tokens.shape), 'head...  15.6 us
    ppermute x3, starting transfers between devices, across(): return lax.ppermute(value, 'head', [(h, h ^ 1) for h in range(8)])  15.2 us
    all_to_all x1, starting transfers between devices, shards(): lax.all_to_all(call(total_kernel, shape((16, QUARTER, 128)))(quarters), '...  14.9 us
    all_to_all x1, blocking collectives, shards(): lax.all_to_all(sums, 'ctx', 0, 0, tiled=True, axis_index_groups=in_x)  9.51 us
    all_to_all x1, blocking collectives, shards(): lax.all_to_all(states, 'ctx', 0, 0, tiled=True, axis_index_groups=in_x)  8.15 us
    all_to_all x1, waiting for transfers between devices, shards(): lax.all_to_all(call(total_kernel, shape((16, QUARTER, 128)))(quarters), '...  5.38 us
    pallas_call x1, Pallas kernels, shards(): call_with_scalar(project_kernel, [shape((count, 384)), shape((count, 256)...  5.37 us
  transfers between devices with their start and end apart: 5, of which 4 were waited for; matrix products, arithmetic and copies ran while one was open for 0% of the time, Pallas kernels for 8%

profile of v4, /device:TPU:1, one launch (start us, length us, event | category | flops | bytes accessed | tf_op | source)
XLA Modules:
  0.0 107.2 jit_solution(2601138021413370111)
XLA Ops:
  0.0 1.0 broadcast_in_dim.2
  1.0 0.0 copy-start
  1.0 0.0 copy-start.1
  1.0 15.6 %all_to_all.25.mine_ref = bf16[4,512,256]{2,1,0:T(8,128)(2,1)S(1)} all-to-all(bf16[4,512,256]{2,1,0:T(8,128)(2,1)S(1)} %broadcast_in_dim.2), channel_id=1, replica_groups={{0,2,4,6},{1,3,5,7},{8,10,12,14},{9,11,13,15},{16,18,20,22},{17,19,21,2..., dimensions={0} | all-to-all | bytes 2097152 | tf_op jit(solution)/shard_map/all_to_all | solution.py:206
  16.6 7.3 %collective-permute-start = (bf16[4,512,256]{2,1,0:T(8,128)(2,1)S(1)}, bf16[4,512,256]{2,1,0:T(8,128)(2,1)}, u32[]{:S(2)}, u32[]{:S(2)}) collective-permute-start(bf16[4,512,256]{2,1,0:T(8,128)(2,1)S(1)} %all_to_all.25.mine_ref), channel_id=1, source_target_pairs={{0,1},{1,0},{2,3},{3,2},{4,5},{5,4},{6,7},{7,6},{8,9},{9,8},{10,11... | collective-permute-start | bytes 3145736 | tf_op jit(solution)/shard_map/ppermute | solution.py:201
  23.9 1.9 %collective-permute-start.3 = (bf16[256,2048]{1,0:T(8,128)(2,1)}, bf16[256,2048]{1,0:T(8,128)(2,1)}, u32[]{:S(2)}, u32[]{:S(2)}) collective-permute-start(bf16[256,2048]{1,0:T(8,128)(2,1)} %w_ref.1), channel_id=1, source_target_pairs={{0,1},{1,0},{2,3},{3,2},{4,5},{5,4},{6,7},{7,6},{8,9},{9,8},{10,11... | collective-permute-start | bytes 3145736 | tf_op jit(solution)/shard_map/ppermute | solution.py:201
  25.9 0.0 copy-start.5
  25.9 0.4 collective-permute-done.other_ref
  26.3 0.0 copy-done
  26.3 0.0 copy-done.1
  26.3 0.2 copy-done.5
  26.6 0.0 copy-start.4
  26.6 0.9 copy-done.4
  27.5 5.4 %shard_map.64 = (bf16[512,384]{1,0:T(8,128)(2,1)S(1)}, bf16[512,256]{1,0:T(8,128)(2,1)S(1)}, bf16[4,40,128]{2,1,0:T(8,128)(2,1)S(1)}) custom-call(s32[1]{0:T(128)} %bitcast.core_ref, bf16[4,512,256]{2,1,0:T(8,128)(2,1)S(1)} %all_to_all.25.mine_ref, bf16[4,512,256]{2,1,0:T(8,128)(2,1)} %collective-permute-done.other_ref, f32[1,2048]{1,0:T(1,128)S(1)} %bitcast.6, ...), custom_call_target="tpu_custom_call" | custom-call | tf_op jit(solution)/shard_map/pallas_call | solution.py:212
  32.9 0.0 copy-start.2
  32.9 0.7 copy-done.2
  33.6 8.1 %all_to_all.26.got_ref = bf16[4,40,128]{2,1,0:T(8,128)(2,1)S(1)} all-to-all(bf16[4,40,128]{2,1,0:T(8,128)(2,1)S(1)} %get-tuple-element.18), channel_id=1, replica_groups={{0,8,16,24},{32,40,48,56},{64,72,80,88},{96,104,112,120},{128,136,144,1..., dimensions={0} | all-to-all | bytes 81920 | tf_op jit(solution)/shard_map/all_to_all | solution.py:221
  41.7 0.0 copy-start.3
  41.7 0.7 shard_map.65
  42.4 14.9 %all-to-all-start.2 = ((bf16[16,40,128]{2,1,0:T(8,128)(2,1)}), bf16[16,40,128]{2,1,0:T(8,128)(2,1)S(1)}, u32[]{:S(2)}, u32[]{:S(2)}) async-start(bf16[16,40,128]{2,1,0:T(8,128)(2,1)} %shard_map.65), calls=%async_computation.2 | async-start | bytes 327680 | tf_op jit(solution)/shard_map/all_to_all | solution.py:223
  57.3 0.0 copy-done.3
  57.3 2.2 %collective-permute-start.1 = (bf16[512,256]{1,0:T(8,128)(2,1)S(1)}, bf16[512,256]{1,0:T(8,128)(2,1)S(1)}, u32[]{:S(2)}, u32[]{:S(2)}) collective-permute-start(bf16[512,256]{1,0:T(8,128)(2,1)S(1)} %copy-done.3), channel_id=1, source_target_pairs={{0,8},{8,16},{16,24},{24,32},{32,40},{40,48},{48,56},{56,64},{64,7... | collective-permute-start | bytes 786440 | tf_op jit(solution)/shard_map/ppermute | solution.py:226
  59.6 0.6 shard_map.67.num_ref
  60.2 2.6 %collective-permute-done.1.prev_ref = bf16[512,256]{1,0:T(8,128)(2,1)S(1)} collective-permute-done((bf16[512,256]{1,0:T(8,128)(2,1)S(1)}, bf16[512,256]{1,0:T(8,128)(2,1)S(1)}, u32[]{:S(2)}, u32[]{:S(2)}) %collective-permute-start.1) | collective-permute-done | bytes 262176 | tf_op jit(solution)/shard_map/ppermute | solution.py:226
  62.8 1.3 %shard_map.68.win_ref = bf16[512,128]{1,0:T(8,128)(2,1)S(1)} custom-call(s32[1]{0:T(128)} %bitcast.4.first_ref, bf16[512,384]{1,0:T(8,128)(2,1)S(1)} %get-tuple-element.16.pack_ref, bf16[512,256]{1,0:T(8,128)(2,1)S(1)} %copy-done.3, bf16[512,256]{1,0:T(8,128)(2,1)S(1)} %collective-permute-done.1.prev_ref), custom_call_target="tpu_custom_call" | custom-call | tf_op jit(solution)/shard_map/pallas_call | solution.py:228
  64.1 5.4 %all-to-all-done.2.totals_ref = bf16[16,40,128]{2,1,0:T(8,128)(2,1)S(1)} async-done(((bf16[16,40,128]{2,1,0:T(8,128)(2,1)}), bf16[16,40,128]{2,1,0:T(8,128)(2,1)S(1)}, u32[]{:S(2)}, u32[]{:S(2)}) %all-to-all-start.2) | async-done | bytes 163872 | tf_op jit(solution)/shard_map/all_to_all | solution.py:223
  69.5 9.5 %all_to_all.27.prefix_ref = bf16[4,40,128]{2,1,0:T(8,128)(2,1)S(1)} all-to-all(bf16[4,40,128]{2,1,0:T(8,128)(2,1)S(1)} %shard_map.66), channel_id=1, replica_groups={{0,8,16,24},{32,40,48,56},{64,72,80,88},{96,104,112,120},{128,136,144,1..., dimensions={0} | all-to-all | bytes 81920 | tf_op jit(solution)/shard_map/all_to_all | solution.py:233
  79.1 0.6 shard_map.69.mix_ref
  79.7 5.9 %collective-permute-start.2 = (bf16[512,256]{1,0:T(8,128)(2,1)S(1)}, bf16[512,256]{1,0:T(8,128)(2,1)S(1)}, u32[]{:S(2)}, u32[]{:S(2)}) collective-permute-start(bf16[512,256]{1,0:T(8,128)(2,1)S(1)} %shard_map.69.mix_ref), channel_id=1, source_target_pairs={{0,1},{1,0},{2,3},{3,2},{4,5},{5,4},{6,7},{7,6},{8,9},{9,8},{10,11... | collective-permute-start | bytes 786440 | tf_op jit(solution)/shard_map/ppermute | solution.py:201
  85.6 0.0 collective-permute-done.3.w2_ref
  85.6 1.1 %collective-permute-done.2.mix2_ref = bf16[512,256]{1,0:T(8,128)(2,1)S(1)} collective-permute-done((bf16[512,256]{1,0:T(8,128)(2,1)S(1)}, bf16[512,256]{1,0:T(8,128)(2,1)S(1)}, u32[]{:S(2)}, u32[]{:S(2)}) %collective-permute-start.2) | collective-permute-done | bytes 262176 | tf_op jit(solution)/shard_map/ppermute | solution.py:201
  86.7 2.3 %shard_map.70 = bf16[4,512,256]{2,1,0:T(8,128)(2,1)S(1)} custom-call(s32[1]{0:T(128)} %bitcast.core_ref, bf16[512,256]{1,0:T(8,128)(2,1)S(1)} %shard_map.69.mix_ref, bf16[256,2048]{1,0:T(8,128)(2,1)} %w_ref.1, bf16[512,256]{1,0:T(8,128)(2,1)S(1)} %collective-permute-done.2.mix2_ref, bf16[256,2048]{1,0:T(8,128)(2,1)} %collective-permute-done.3.w2_ref), custom_call_target="tpu_custom_call" | custom-call | tf_op jit(solution)/shard_map/pallas_call | solution.py:235
  89.0 17.3 %all_to_all.28 = bf16[4,512,256]{2,1,0:T(8,128)(2,1)S(1)} all-to-all(bf16[4,512,256]{2,1,0:T(8,128)(2,1)S(1)} %shard_map.70), channel_id=1, replica_groups={{0,2,4,6},{1,3,5,7},{8,10,12,14},{9,11,13,15},{16,18,20,22},{17,19,21,2..., dimensions={0} | all-to-all | bytes 2097152 | tf_op jit(solution)/shard_map/all_to_all | solution.py:236
  106.3 0.9 reduce_sum.12
  (1 shorter events, 0.0 us)
Async XLA Ops:
  1.0 25.3 %copy-start = (bf16[2048,256]{1,0:T(8,128)(2,1)S(1)}, bf16[2048,256]{1,0:T(8,128)(2,1)}, u32[]{:S(2)}) copy-start(bf16[2048,256]{1,0:T(8,128)(2,1)} %wv_ref.1) | copy-start | bytes 3145732
  1.0 25.3 %copy-start.1 = (bf16[2048,256]{1,0:T(8,128)(2,1)S(1)}, bf16[2048,256]{1,0:T(8,128)(2,1)}, u32[]{:S(2)}) copy-start(bf16[2048,256]{1,0:T(8,128)(2,1)} %ww_ref.1) | copy-start | bytes 3145732
  16.6 9.7 %collective-permute-start = (bf16[4,512,256]{2,1,0:T(8,128)(2,1)S(1)}, bf16[4,512,256]{2,1,0:T(8,128)(2,1)}, u32[]{:S(2)}, u32[]{:S(2)}) collective-permute-start(bf16[4,512,256]{2,1,0:T(8,128)(2,1)S(1)} %all_to_all.25.mine_ref), channel_id=1, source_target_pairs={{0,1},{1,0},{2,3},{3,2},{4,5},{5,4},{6,7},{7,6},{8,9},{9,8},{10,11... | collective-permute-start | bytes 3145736 | tf_op jit(solution)/shard_map/ppermute | solution.py:201
  23.9 61.7 %collective-permute-start.3 = (bf16[256,2048]{1,0:T(8,128)(2,1)}, bf16[256,2048]{1,0:T(8,128)(2,1)}, u32[]{:S(2)}, u32[]{:S(2)}) collective-permute-start(bf16[256,2048]{1,0:T(8,128)(2,1)} %w_ref.1), channel_id=1, source_target_pairs={{0,1},{1,0},{2,3},{3,2},{4,5},{5,4},{6,7},{7,6},{8,9},{9,8},{10,11... | collective-permute-start | bytes 3145736 | tf_op jit(solution)/shard_map/ppermute | solution.py:201
  25.9 0.7 copy-start.5
  26.6 0.9 copy-start.4
  32.9 0.7 copy-start.2
  41.7 15.6 %copy-start.3 = (bf16[512,256]{1,0:T(8,128)(2,1)S(1)}, bf16[512,256]{1,0:T(8,128)(2,1)}, u32[]{:S(2)}) copy-start(bf16[512,256]{1,0:T(8,128)(2,1)} %copy-done.2) | copy-start | bytes 786436
  42.4 27.1 %all-to-all-start.2 = ((bf16[16,40,128]{2,1,0:T(8,128)(2,1)}), bf16[16,40,128]{2,1,0:T(8,128)(2,1)S(1)}, u32[]{:S(2)}, u32[]{:S(2)}) async-start(bf16[16,40,128]{2,1,0:T(8,128)(2,1)} %shard_map.65), calls=%async_computation.2 | async-start | bytes 327680 | tf_op jit(solution)/shard_map/all_to_all | solution.py:223
  57.3 5.5 %collective-permute-start.1 = (bf16[512,256]{1,0:T(8,128)(2,1)S(1)}, bf16[512,256]{1,0:T(8,128)(2,1)S(1)}, u32[]{:S(2)}, u32[]{:S(2)}) collective-permute-start(bf16[512,256]{1,0:T(8,128)(2,1)S(1)} %copy-done.3), channel_id=1, source_target_pairs={{0,8},{8,16},{16,24},{24,32},{32,40},{40,48},{48,56},{56,64},{64,7... | collective-permute-start | bytes 786440 | tf_op jit(solution)/shard_map/ppermute | solution.py:226
  79.7 7.1 %collective-permute-start.2 = (bf16[512,256]{1,0:T(8,128)(2,1)S(1)}, bf16[512,256]{1,0:T(8,128)(2,1)S(1)}, u32[]{:S(2)}, u32[]{:S(2)}) collective-permute-start(bf16[512,256]{1,0:T(8,128)(2,1)S(1)} %shard_map.69.mix_ref), channel_id=1, source_target_pairs={{0,1},{1,0},{2,3},{3,2},{4,5},{5,4},{6,7},{7,6},{8,9},{9,8},{10,11... | collective-permute-start | bytes 786440 | tf_op jit(solution)/shard_map/ppermute | solution.py:201

commit v5 on v4

--- a/solution.py
+++ b/solution.py
@@ -26,13 +26,12 @@
     )
 
 
-def call_with_scalar(kernel, outs, count, scratch=(), in_place=None):
+def call_with_scalar(kernel, outs, count):
     return pl.pallas_call(
         kernel,
         out_shape=outs,
         in_specs=[pl.BlockSpec(memory_space=pltpu.SMEM)]
-        + [pl.BlockSpec(memory_space=pltpu.HBM if i + 1 == in_place else pltpu.VMEM) for i in range(count)],
-        scratch_shapes=scratch,
+        + [pl.BlockSpec(memory_space=pltpu.VMEM)] * count,
         compiler_params=pltpu.CompilerParams(vmem_limit_bytes=VMEM),
     )
 
@@ -76,9 +75,10 @@
 
 
 def project_kernel(
-    core_ref, mine_ref, other_ref, gain_ref, wf_hbm, wv_ref, ww_ref, pack_ref, rim_ref, state_ref, normed, wf_ref, wf_sem
+    core_ref, mine_ref, other_ref, gain_ref, wf_hbm, wv_ref, ww_ref, *rest
 ):
-    load = pltpu.make_async_copy(wf_hbm, wf_ref, wf_sem)
+    *before, pack_hbm, rim_hbm, state_ref, flag_ref, normed, wf_ref, pack_ref, rim_ref, sems = rest
+    load = pltpu.make_async_copy(wf_hbm, wf_ref, sems.at[0])
     load.start()
     count = mine_ref.shape[1]
     step = 128
@@ -95,25 +95,38 @@
                 at = pl.multiple_of((2 * y + (core + flip) % 2) * 256, 256)
                 x = source[y, r : r + step, :].astype(F32)
                 normed[r : r + step, pl.ds(at, 256)] = (x * scale * gain_ref[0:1, pl.ds(at, 256)]).astype(BF)
+    low = count if before else 0
     n = normed[...]
+    windowed = dot(n, ww_ref[...]).astype(BF)
+    values = dot(n, wv_ref[...]).astype(BF)
+    rim_ref[:, :128] = windowed[:, 128:]
+    rim_ref[:, 128:] = values[:, 128:]
+    store_rim = pltpu.make_async_copy(rim_ref, rim_hbm.at[low : low + count, :], sems.at[1])
+    store_rim.start()
     load.wait()
     feats = dot(n, wf_ref[...], NT).astype(BF)
-    values = dot(n, wv_ref[...]).astype(BF)
+    vlin = values[:, :128]
+    pack_ref[:, :128] = windowed[:, :128]
+    pack_ref[:, 128:256] = vlin
     pack_ref[:, 256:288] = feats
     pack_ref[:, 288:] = jnp.zeros((count, 96), BF)
-    vlin = values[:, :128]
-    pack_ref[:, 128:256] = vlin
+    store_pack = pltpu.make_async_copy(pack_ref, pack_hbm.at[low : low + count, :], sems.at[2])
+    store_pack.start()
     first, second = pick((ROWS, FEAT), 0)
     scale, add_first, add_second = weights_of((ROWS, 1), 0, False)
     k = feats[:, FEAT:]
     phi = (dot(first, k, NT) + add_first) * (dot(second, k, NT) + add_second) * scale
     state = dot(phi.astype(BF), vlin)
-    for i in range(4):
-        state_ref[i, :, :] = state[QUARTER * i : QUARTER * (i + 1), :].astype(BF)
-    windowed = dot(n, ww_ref[...]).astype(BF)
-    pack_ref[:, :128] = windowed[:, :128]
-    rim_ref[:, :128] = windowed[:, 128:]
-    rim_ref[:, 128:] = values[:, 128:]
+    if not before:
+        state_ref[...] = state
+        flag_ref[...] = jnp.zeros(flag_ref.shape, F32)
+    else:
+        state = state + before[2][...]
+        flag_ref[...] = before[3][...]
+        for i in range(4):
+            state_ref[i, :, :] = state[QUARTER * i : QUARTER * (i + 1), :].astype(BF)
+    store_rim.wait()
+    store_pack.wait()
 
 
 def inner_kernel(pack_ref, num_ref):
@@ -203,19 +216,41 @@
     def shape(dims, kind=BF):
         return jax.ShapeDtypeStruct(dims, kind)
 
-    spread = lax.all_to_all(
-        jnp.broadcast_to(tokens[None], (4,) + tokens.shape), "head", 0, 0, tiled=True, axis_index_groups=along_y
-    )
-    spread, w_later = lax.optimization_barrier((spread, w_out))
-    other = across(spread)
-    w_other = across(w_later)
-    pack, rim, states = call_with_scalar(
-        project_kernel,
-        [shape((count, 384)), shape((count, 256)), shape((4, QUARTER, 128))],
-        6,
-        [pltpu.VMEM((count, 2048), BF), pltpu.VMEM((32, 2048), BF), pltpu.SemaphoreType.DMA],
-        4,
-    )(core, spread, other, gain.reshape(1, -1), w_feat.T, w_value, w_window)
+    half = count // 2
+    vmem, hbm = pl.BlockSpec(memory_space=pltpu.VMEM), pl.BlockSpec(memory_space=pltpu.HBM)
+    done = []
+    for part in range(2):
+        rows = tokens[half * part : half * (part + 1)]
+        spread = lax.all_to_all(
+            jnp.broadcast_to(rows[None], (4,) + rows.shape), "head", 0, 0, tiled=True, axis_index_groups=along_y
+        )
+        if part == 1:
+            w_later, done[3] = lax.optimization_barrier((w_out, done[3]))
+            w_other = across(w_later)
+            spread, done[3] = lax.optimization_barrier((spread, done[3]))
+        other = across(spread)
+        done = list(pl.pallas_call(
+            project_kernel,
+            out_shape=[
+                shape((count, 384)),
+                shape((count, 256)),
+                shape((4, QUARTER, 128)) if part else shape((ROWS, 128), F32),
+                shape((8, 128), F32),
+            ],
+            in_specs=[pl.BlockSpec(memory_space=pltpu.SMEM), vmem, vmem, vmem, hbm, vmem, vmem]
+            + ([hbm, hbm, vmem, vmem] if part else []),
+            out_specs=[hbm, hbm, vmem, vmem],
+            input_output_aliases={7: 0, 8: 1} if part else {},
+            scratch_shapes=[
+                pltpu.VMEM((half, 2048), BF),
+                pltpu.VMEM((32, 2048), BF),
+                pltpu.VMEM((half, 384), BF),
+                pltpu.VMEM((half, 256), BF),
+                pltpu.SemaphoreType.DMA((3,)),
+            ],
+            compiler_params=pltpu.CompilerParams(vmem_limit_bytes=VMEM),
+        )(core, spread, other, gain.reshape(1, -1), w_feat.T, w_value, w_window, *done))
+    pack, rim, states, _ = done
     in_x = [[4 * z + x for x in range(4)] for z in range(16)]
     in_z = [[4 * z + x for z in range(16)] for x in range(4)]
     quarters = lax.all_to_all(states, "ctx", 0, 0, tiled=True, axis_index_groups=in_x)

time: 108 us -> 118 us (1.093)
  starting transfers between devices: 32.3 us -> 38.2 us
  local copies, waits for them, and re-layouts: 2.87 us -> 8.2 us
  blocking collectives: 50.5 us -> 45.4 us
  waiting for transfers between devices: 9.6 us -> 11.8 us
  Pallas kernels: 10.8 us -> 12.8 us
    unnamed x12 -> x24, local copies, waits for them, and re-layouts: 1.86 us -> 6.34 us
    all_to_all x1, blocking collectives: 15.6 us -> 11.9 us  [shards(): lax.all_to_all(jnp.broadcast_to(rows[None], (4,) + rows.shape), 'head', 0...]
    all_to_all x0 -> x1, starting transfers between devices: none -> 3.47 us  [shards(): lax.all_to_all(jnp.broadcast_to(rows[None], (4,) + rows.shape), 'head', 0...]
    ppermute x3 -> x4, starting transfers between devices: 15.2 us -> 18.3 us  [across(): return lax.ppermute(value, 'head', [(h, h ^ 1) for h in range(8)])]
    all_to_all x0 -> x1, waiting for transfers between devices: none -> 2.62 us  [shards(): lax.all_to_all(jnp.broadcast_to(rows[None], (4,) + rows.shape), 'head', 0...]
    pallas_call x1 -> x2, Pallas kernels: 5.37 us -> 7.61 us  [shards(): pl.pallas_call(project_kernel, out_shape=[shape((count, 384)), shape((cou...]
    all_to_all x1, blocking collectives: 8.15 us -> 6.69 us  [shards(): lax.all_to_all(states, 'ctx', 0, 0, tiled=True, axis_index_groups=in_x)]
  transfers between devices with their start and end apart: 5 -> 7, of which waited for: 4 -> 4; matrix products, arithmetic and copies ran while one was open for 0% -> 1% of each run, Pallas kernels for 8% -> 9%
where the time goes in v5:
time: 118 us; the launch traced here: 117 us
  blocking collectives  45.4 us (38%)
  starting transfers between devices  38.2 us (32%)
  Pallas kernels  12.8 us (11%)
  waiting for transfers between devices  11.8 us (10%)
  local copies, waits for them, and re-layouts  8.2 us (7%)
    ppermute x4, starting transfers between devices, across(): return lax.ppermute(value, 'head', [(h, h ^ 1) for h in range(8)])  18.3 us
    all_to_all x1, blocking collectives, shards(): lax.all_to_all(summed, 'head', 0, 0, tiled=True, axis_index_groups=along_y)  17.3 us
    all_to_all x1, starting transfers between devices, shards(): lax.all_to_all(call(total_kernel, shape((16, QUARTER, 128)))(quarters), '...  14.3 us
    all_to_all x1, blocking collectives, shards(): lax.all_to_all(jnp.broadcast_to(rows[None], (4,) + rows.shape), 'head', 0...  11.9 us
    all_to_all x1, blocking collectives, shards(): lax.all_to_all(sums, 'ctx', 0, 0, tiled=True, axis_index_groups=in_x)  9.52 us
    pallas_call x2, Pallas kernels, shards(): pl.pallas_call(project_kernel, out_shape=[shape((count, 384)), shape((cou...  7.61 us
    all_to_all x1, blocking collectives, shards(): lax.all_to_all(states, 'ctx', 0, 0, tiled=True, axis_index_groups=in_x)  6.69 us
    unnamed x24, local copies, waits for them, and re-layouts  6.34 us
  transfers between devices with their start and end apart: 7, of which 4 were waited for; matrix products, arithmetic and copies ran while one was open for 1% of the time, Pallas kernels for 9%

profile of v5, /device:TPU:1, one launch (start us, length us, event | category | flops | bytes accessed | tf_op | source)
XLA Modules:
  0.0 117.5 jit_solution(387707448905317947)
XLA Ops:
  0.0 1.0 fusion
  1.0 0.0 copy-start.1
  1.0 11.9 %all_to_all.30.mine_ref = bf16[4,256,256]{2,1,0:T(8,128)(2,1)S(1)} all-to-all(bf16[4,256,256]{2,1,0:T(8,128)(2,1)S(1)} %broadcast_in_dim.5), channel_id=1, replica_groups={{0,2,4,6},{1,3,5,7},{8,10,12,14},{9,11,13,15},{16,18,20,22},{17,19,21,2..., dimensions={0} | all-to-all | bytes 1048576 | tf_op jit(solution)/shard_map/all_to_all | solution.py:224
  12.9 0.0 copy-start
  12.9 7.6 %collective-permute-start = (bf16[4,256,256]{2,1,0:T(8,128)(2,1)S(1)}, bf16[4,256,256]{2,1,0:T(8,128)(2,1)}, u32[]{:S(2)}, u32[]{:S(2)}) collective-permute-start(bf16[4,256,256]{2,1,0:T(8,128)(2,1)S(1)} %all_to_all.30.mine_ref), channel_id=1, source_target_pairs={{0,1},{1,0},{2,3},{3,2},{4,5},{5,4},{6,7},{7,6},{8,9},{9,8},{10,11... | collective-permute-start | bytes 1572872 | tf_op jit(solution)/shard_map/ppermute | solution.py:214
  20.6 0.8 broadcast_in_dim.4
  21.4 3.5 %all-to-all-start = ((bf16[4,256,256]{2,1,0:T(8,128)(2,1)}), bf16[4,256,256]{2,1,0:T(8,128)(2,1)S(1)}, u32[]{:S(2)}, u32[]{:S(2)}) async-start(bf16[4,256,256]{2,1,0:T(8,128)(2,1)} %broadcast_in_dim.4), calls=%async_computation | async-start | bytes 1048576 | tf_op jit(solution)/shard_map/all_to_all | solution.py:224
  24.9 0.0 copy-start.11
  24.9 0.0 collective-permute-done.other_ref
  24.9 0.0 copy-done.1
  24.9 0.0 copy-done
  24.9 0.7 copy-done.11
  25.6 0.0 copy-start.7
  25.6 0.9 copy-done.7
  26.5 4.0 %shard_map.64 = (bf16[512,384]{1,0:T(8,128)(2,1)S(1)}, bf16[512,256]{1,0:T(8,128)(2,1)S(1)}, f32[160,128]{1,0:T(8,128)S(1)}, f32[8,128]{1,0:T(8,128)S(1)}) custom-call(s32[1]{0:T(128)} %bitcast.core_ref, bf16[4,256,256]{2,1,0:T(8,128)(2,1)S(1)} %all_to_all.30.mine_ref, bf16[4,256,256]{2,1,0:T(8,128)(2,1)} %collective-permute-done.other_ref, ...), custom_call_target="tpu_custom_call" | custom-call | tf_op jit(solution)/shard_map/pallas_call | solution.py:232
  30.5 0.0 copy-start.2
  30.5 0.7 copy-done.2
  31.2 0.0 copy-start.9
  31.2 0.6 copy-done.9
  31.9 2.6 %all-to-all-done.mine_ref = bf16[4,256,256]{2,1,0:T(8,128)(2,1)S(1)} async-done(((bf16[4,256,256]{2,1,0:T(8,128)(2,1)}), bf16[4,256,256]{2,1,0:T(8,128)(2,1)S(1)}, u32[]{:S(2)}, u32[]{:S(2)}) %all-to-all-start) | async-done | bytes 524320 | tf_op jit(solution)/shard_map/all_to_all | solution.py:224
  34.5 2.7 %collective-permute-start.1 = (bf16[4,256,256]{2,1,0:T(8,128)(2,1)S(1)}, bf16[4,256,256]{2,1,0:T(8,128)(2,1)S(1)}, u32[]{:S(2)}, u32[]{:S(2)}) collective-permute-start(bf16[4,256,256]{2,1,0:T(8,128)(2,1)S(1)} %all-to-all-done.mine_ref), channel_id=1, source_target_pairs={{0,1},{1,0},{2,3},{3,2},{4,5},{5,4},{6,7},{7,6},{8,9},{9,8},{10,11... | collective-permute-start | bytes 1572872 | tf_op jit(solution)/shard_map/ppermute | solution.py:214
  37.2 1.9 %collective-permute-start.4 = (bf16[256,2048]{1,0:T(8,128)(2,1)}, bf16[256,2048]{1,0:T(8,128)(2,1)}, u32[]{:S(2)}, u32[]{:S(2)}) collective-permute-start(bf16[256,2048]{1,0:T(8,128)(2,1)} %w_ref.1), channel_id=1, source_target_pairs={{0,1},{1,0},{2,3},{3,2},{4,5},{5,4},{6,7},{7,6},{8,9},{9,8},{10,11... | collective-permute-start | bytes 3145736 | tf_op jit(solution)/shard_map/ppermute | solution.py:214
  39.1 0.0 collective-permute-done.1.other_ref
  39.1 0.0 copy-start.3
  39.1 0.9 copy-done.3
  40.1 0.9 copy-done.8
  41.0 0.9 copy-done.10
  41.9 3.6 %shard_map.65 = (bf16[512,384]{1,0:T(8,128)(2,1)S(1)}, bf16[512,256]{1,0:T(8,128)(2,1)S(1)}, bf16[4,40,128]{2,1,0:T(8,128)(2,1)S(1)}, f32[8,128]{1,0:T(8,128)}) custom-call(s32[1]{0:T(128)} %bitcast.core_ref, bf16[4,256,256]{2,1,0:T(8,128)(2,1)S(1)} %all-to-all-done.mine_ref, ...), custom_call_target="tpu_custom_call", output_to_operand_aliasing={{0}: (7, {}), {1}: (8, {})} | custom-call | tf_op jit(solution)/shard_map/pallas_call | solution.py:232
  45.5 0.0 copy-start.4
  45.5 0.7 copy-done.4
  46.2 6.7 %all_to_all.31.got_ref = bf16[4,40,128]{2,1,0:T(8,128)(2,1)S(1)} all-to-all(bf16[4,40,128]{2,1,0:T(8,128)(2,1)S(1)} %get-tuple-element.30), channel_id=1, replica_groups={{0,8,16,24},{32,40,48,56},{64,72,80,88},{96,104,112,120},{128,136,144,1..., dimensions={0} | all-to-all | bytes 81920 | tf_op jit(solution)/shard_map/all_to_all | solution.py:256
  52.9 0.7 shard_map.66
  53.6 14.3 %all-to-all-start.3 = ((bf16[16,40,128]{2,1,0:T(8,128)(2,1)}), bf16[16,40,128]{2,1,0:T(8,128)(2,1)S(1)}, u32[]{:S(2)}, u32[]{:S(2)}) async-start(bf16[16,40,128]{2,1,0:T(8,128)(2,1)} %shard_map.66), calls=%async_computation.3 | async-start | bytes 327680 | tf_op jit(solution)/shard_map/all_to_all | solution.py:258
  67.8 0.0 copy-done.5
  67.8 2.2 %collective-permute-start.2 = (bf16[512,256]{1,0:T(8,128)(2,1)S(1)}, bf16[512,256]{1,0:T(8,128)(2,1)S(1)}, u32[]{:S(2)}, u32[]{:S(2)}) collective-permute-start(bf16[512,256]{1,0:T(8,128)(2,1)S(1)} %copy-done.5), channel_id=1, source_target_pairs={{0,8},{8,16},{16,24},{24,32},{32,40},{40,48},{48,56},{56,64},{64,7... | collective-permute-start | bytes 786440 | tf_op jit(solution)/shard_map/ppermute | solution.py:261
  70.1 0.6 shard_map.68.num_ref
  70.7 2.7 %collective-permute-done.2.prev_ref = bf16[512,256]{1,0:T(8,128)(2,1)S(1)} collective-permute-done((bf16[512,256]{1,0:T(8,128)(2,1)S(1)}, bf16[512,256]{1,0:T(8,128)(2,1)S(1)}, u32[]{:S(2)}, u32[]{:S(2)}) %collective-permute-start.2) | collective-permute-done | bytes 262176 | tf_op jit(solution)/shard_map/ppermute | solution.py:261
  73.3 1.3 %shard_map.69.win_ref = bf16[512,128]{1,0:T(8,128)(2,1)S(1)} custom-call(s32[1]{0:T(128)} %bitcast.4.first_ref, bf16[512,384]{1,0:T(8,128)(2,1)S(1)} %get-tuple-element.28.pack_ref, bf16[512,256]{1,0:T(8,128)(2,1)S(1)} %copy-done.5, bf16[512,256]{1,0:T(8,128)(2,1)S(1)} %collective-permute-done.2.prev_ref), custom_call_target="tpu_custom_call" | custom-call | tf_op jit(solution)/shard_map/pallas_call | solution.py:263
  74.6 5.4 %all-to-all-done.3.totals_ref = bf16[16,40,128]{2,1,0:T(8,128)(2,1)S(1)} async-done(((bf16[16,40,128]{2,1,0:T(8,128)(2,1)}), bf16[16,40,128]{2,1,0:T(8,128)(2,1)S(1)}, u32[]{:S(2)}, u32[]{:S(2)}) %all-to-all-start.3) | async-done | bytes 163872 | tf_op jit(solution)/shard_map/all_to_all | solution.py:258
  80.0 9.5 %all_to_all.32.prefix_ref = bf16[4,40,128]{2,1,0:T(8,128)(2,1)S(1)} all-to-all(bf16[4,40,128]{2,1,0:T(8,128)(2,1)S(1)} %shard_map.67), channel_id=1, replica_groups={{0,8,16,24},{32,40,48,56},{64,72,80,88},{96,104,112,120},{128,136,144,1..., dimensions={0} | all-to-all | bytes 81920 | tf_op jit(solution)/shard_map/all_to_all | solution.py:268
  89.6 0.6 shard_map.70.mix_ref
  90.1 6.0 %collective-permute-start.3 = (bf16[512,256]{1,0:T(8,128)(2,1)S(1)}, bf16[512,256]{1,0:T(8,128)(2,1)S(1)}, u32[]{:S(2)}, u32[]{:S(2)}) collective-permute-start(bf16[512,256]{1,0:T(8,128)(2,1)S(1)} %shard_map.70.mix_ref), channel_id=1, source_target_pairs={{0,1},{1,0},{2,3},{3,2},{4,5},{5,4},{6,7},{7,6},{8,9},{9,8},{10,11... | collective-permute-start | bytes 786440 | tf_op jit(solution)/shard_map/ppermute | solution.py:214
  96.2 0.0 collective-permute-done.4.w2_ref
  96.2 1.1 collective-permute-done.3.mix2_ref
  97.3 0.0 copy-done.6
  97.3 1.9 %shard_map.71 = bf16[4,512,256]{2,1,0:T(8,128)(2,1)S(1)} custom-call(s32[1]{0:T(128)} %bitcast.core_ref, bf16[512,256]{1,0:T(8,128)(2,1)S(1)} %shard_map.70.mix_ref, bf16[256,2048]{1,0:T(8,128)(2,1)S(1)} %copy-done.6, bf16[512,256]{1,0:T(8,128)(2,1)S(1)} %collective-permute-done.3.mix2_ref, bf16[256,2048]{1,0:T(8,128)(2,1)} %collective-permute-done.4.w2_ref), custom_call_target="tpu_custom_call" | custom-call | tf_op jit(solution)/shard_map/pallas_call | solution.py:270
  99.3 17.3 %all_to_all.33 = bf16[4,512,256]{2,1,0:T(8,128)(2,1)S(1)} all-to-all(bf16[4,512,256]{2,1,0:T(8,128)(2,1)S(1)} %shard_map.71), channel_id=1, replica_groups={{0,2,4,6},{1,3,5,7},{8,10,12,14},{9,11,13,15},{16,18,20,22},{17,19,21,2..., dimensions={0} | all-to-all | bytes 2097152 | tf_op jit(solution)/shard_map/all_to_all | solution.py:271
  116.6 0.9 reduce_sum.12
  (6 shorter events, 0.1 us)
Async XLA Ops:
  1.0 23.9 %copy-start.1 = (bf16[2048,256]{1,0:T(8,128)(2,1)S(1)}, bf16[2048,256]{1,0:T(8,128)(2,1)}, u32[]{:S(2)}) copy-start(bf16[2048,256]{1,0:T(8,128)(2,1)} %ww_ref.3) | copy-start | bytes 3145732
  12.9 12.0 %copy-start = (bf16[2048,256]{1,0:T(8,128)(2,1)S(1)}, bf16[2048,256]{1,0:T(8,128)(2,1)}, u32[]{:S(2)}) copy-start(bf16[2048,256]{1,0:T(8,128)(2,1)} %wv_ref.3) | copy-start | bytes 3145732
  12.9 12.0 %collective-permute-start = (bf16[4,256,256]{2,1,0:T(8,128)(2,1)S(1)}, bf16[4,256,256]{2,1,0:T(8,128)(2,1)}, u32[]{:S(2)}, u32[]{:S(2)}) collective-permute-start(bf16[4,256,256]{2,1,0:T(8,128)(2,1)S(1)} %all_to_all.30.mine_ref), channel_id=1, source_target_pairs={{0,1},{1,0},{2,3},{3,2},{4,5},{5,4},{6,7},{7,6},{8,9},{9,8},{10,11... | collective-permute-start | bytes 1572872 | tf_op jit(solution)/shard_map/ppermute | solution.py:214
  21.4 13.1 %all-to-all-start = ((bf16[4,256,256]{2,1,0:T(8,128)(2,1)}), bf16[4,256,256]{2,1,0:T(8,128)(2,1)S(1)}, u32[]{:S(2)}, u32[]{:S(2)}) async-start(bf16[4,256,256]{2,1,0:T(8,128)(2,1)} %broadcast_in_dim.4), calls=%async_computation | async-start | bytes 1048576 | tf_op jit(solution)/shard_map/all_to_all | solution.py:224
  24.9 0.7 copy-start.11
  25.6 0.9 copy-start.7
  30.5 0.7 copy-start.2
  31.2 0.6 copy-start.9
  34.5 4.6 %collective-permute-start.1 = (bf16[4,256,256]{2,1,0:T(8,128)(2,1)S(1)}, bf16[4,256,256]{2,1,0:T(8,128)(2,1)S(1)}, u32[]{:S(2)}, u32[]{:S(2)}) collective-permute-start(bf16[4,256,256]{2,1,0:T(8,128)(2,1)S(1)} %all-to-all-done.mine_ref), channel_id=1, source_target_pairs={{0,1},{1,0},{2,3},{3,2},{4,5},{5,4},{6,7},{7,6},{8,9},{9,8},{10,11... | collective-permute-start | bytes 1572872 | tf_op jit(solution)/shard_map/ppermute | solution.py:214
  37.2 59.0 %collective-permute-start.4 = (bf16[256,2048]{1,0:T(8,128)(2,1)}, bf16[256,2048]{1,0:T(8,128)(2,1)}, u32[]{:S(2)}, u32[]{:S(2)}) collective-permute-start(bf16[256,2048]{1,0:T(8,128)(2,1)} %w_ref.1), channel_id=1, source_target_pairs={{0,1},{1,0},{2,3},{3,2},{4,5},{5,4},{6,7},{7,6},{8,9},{9,8},{10,11... | collective-permute-start | bytes 3145736 | tf_op jit(solution)/shard_map/ppermute | solution.py:214
  39.1 1.0 copy-start.3
  40.1 0.9 copy-start.8
  41.0 0.9 copy-start.10
  45.5 0.7 copy-start.4
  52.9 15.0 %copy-start.5 = (bf16[512,256]{1,0:T(8,128)(2,1)S(1)}, bf16[512,256]{1,0:T(8,128)(2,1)}, u32[]{:S(2)}) copy-start(bf16[512,256]{1,0:T(8,128)(2,1)} %copy-done.4) | copy-start | bytes 786436
  53.6 26.4 %all-to-all-start.3 = ((bf16[16,40,128]{2,1,0:T(8,128)(2,1)}), bf16[16,40,128]{2,1,0:T(8,128)(2,1)S(1)}, u32[]{:S(2)}, u32[]{:S(2)}) async-start(bf16[16,40,128]{2,1,0:T(8,128)(2,1)} %shard_map.66), calls=%async_computation.3 | async-start | bytes 327680 | tf_op jit(solution)/shard_map/all_to_all | solution.py:258
  67.8 5.5 %collective-permute-start.2 = (bf16[512,256]{1,0:T(8,128)(2,1)S(1)}, bf16[512,256]{1,0:T(8,128)(2,1)S(1)}, u32[]{:S(2)}, u32[]{:S(2)}) collective-permute-start(bf16[512,256]{1,0:T(8,128)(2,1)S(1)} %copy-done.5), channel_id=1, source_target_pairs={{0,8},{8,16},{16,24},{24,32},{32,40},{40,48},{48,56},{56,64},{64,7... | collective-permute-start | bytes 786440 | tf_op jit(solution)/shard_map/ppermute | solution.py:261
  73.3 24.0 %copy-start.6 = (bf16[256,2048]{1,0:T(8,128)(2,1)S(1)}, bf16[256,2048]{1,0:T(8,128)(2,1)}, u32[]{:S(2)}) copy-start(bf16[256,2048]{1,0:T(8,128)(2,1)} %w_ref.1) | copy-start | bytes 3145732
  90.1 7.2 %collective-permute-start.3 = (bf16[512,256]{1,0:T(8,128)(2,1)S(1)}, bf16[512,256]{1,0:T(8,128)(2,1)S(1)}, u32[]{:S(2)}, u32[]{:S(2)}) collective-permute-start(bf16[512,256]{1,0:T(8,128)(2,1)S(1)} %shard_map.70.mix_ref), channel_id=1, source_target_pairs={{0,1},{1,0},{2,3},{3,2},{4,5},{5,4},{6,7},{7,6},{8,9},{9,8},{10,11... | collective-permute-start | bytes 786440 | tf_op jit(solution)/shard_map/ppermute | solution.py:214

commit v6 on v4

--- a/solution.py
+++ b/solution.py
@@ -26,13 +26,11 @@
     )
 
 
-def call_with_scalar(kernel, outs, count, scratch=(), in_place=None):
+def call_with_scalar(kernel, outs, count):
     return pl.pallas_call(
         kernel,
         out_shape=outs,
-        in_specs=[pl.BlockSpec(memory_space=pltpu.SMEM)]
-        + [pl.BlockSpec(memory_space=pltpu.HBM if i + 1 == in_place else pltpu.VMEM) for i in range(count)],
-        scratch_shapes=scratch,
+        in_specs=[pl.BlockSpec(memory_space=pltpu.SMEM)] + [pl.BlockSpec(memory_space=pltpu.VMEM)] * count,
         compiler_params=pltpu.CompilerParams(vmem_limit_bytes=VMEM),
     )
 
@@ -75,34 +73,41 @@
     return lax.dot_general(a, b, dims, preferred_element_type=F32)
 
 
-def project_kernel(
-    core_ref, mine_ref, other_ref, gain_ref, wf_hbm, wv_ref, ww_ref, pack_ref, rim_ref, state_ref, normed, wf_ref, wf_sem
-):
-    load = pltpu.make_async_copy(wf_hbm, wf_ref, wf_sem)
-    load.start()
-    count = mine_ref.shape[1]
-    step = 128
-    core = core_ref[0]
-    for r in range(0, count, step):
-        total = jnp.zeros((step, 256), F32)
-        for source in (mine_ref, other_ref):
-            for y in range(4):
-                x = source[y, r : r + step, :].astype(F32)
-                total = total + x * x
-        scale = lax.rsqrt(jnp.sum(total, axis=1, keepdims=True) * (1.0 / 2048.0) + EPS)
-        for flip, source in enumerate((mine_ref, other_ref)):
-            for y in range(4):
-                at = pl.multiple_of((2 * y + (core + flip) % 2) * 256, 256)
-                x = source[y, r : r + step, :].astype(F32)
-                normed[r : r + step, pl.ds(at, 256)] = (x * scale * gain_ref[0:1, pl.ds(at, 256)]).astype(BF)
-    n = normed[...]
-    load.wait()
-    feats = dot(n, wf_ref[...], NT).astype(BF)
-    values = dot(n, wv_ref[...]).astype(BF)
+def gather_products(flip, core_ref, x_ref, gain_ref, wf_ref, wv_ref, ww_ref):
+    squares = feats = values = windowed = 0.0
+    for y in range(4):
+        at = pl.multiple_of((2 * y + (core_ref[0] + flip) % 2) * 256, 256)
+        x = x_ref[y, :, :].astype(F32)
+        squares = squares + x * x
+        scaled = (x * gain_ref[0:1, pl.ds(at, 256)]).astype(BF)
+        feats = feats + dot(scaled, wf_ref[:, pl.ds(at, 256)], NT)
+        values = values + dot(scaled, wv_ref[pl.ds(at, 256), :])
+        windowed = windowed + dot(scaled, ww_ref[pl.ds(at, 256), :])
+    return jnp.sum(squares, axis=1, keepdims=True), feats, values, windowed
+
+
+def begin_kernel(core_ref, x_ref, gain_ref, wf_ref, wv_ref, ww_ref, held_ref):
+    squares, feats, values, windowed = gather_products(0, core_ref, x_ref, gain_ref, wf_ref, wv_ref, ww_ref)
+    held_ref[:, :256] = values
+    held_ref[:, 256:512] = windowed
+    held_ref[:, 512:544] = feats
+    held_ref[:, 544:] = jnp.broadcast_to(squares, (squares.shape[0], 96))
+
+
+def project_kernel(core_ref, x_ref, gain_ref, wf_ref, wv_ref, ww_ref, held_ref, pack_ref, rim_ref, state_ref):
+    count = x_ref.shape[1]
+    squares, feats, values, windowed = gather_products(1, core_ref, x_ref, gain_ref, wf_ref, wv_ref, ww_ref)
+    scale = lax.rsqrt((squares + held_ref[:, 544:545]) * (1.0 / 2048.0) + EPS)
+    values = ((values + held_ref[:, :256]) * scale).astype(BF)
+    windowed = ((windowed + held_ref[:, 256:512]) * scale).astype(BF)
+    feats = ((feats + held_ref[:, 512:544]) * scale).astype(BF)
+    rim_ref[:, :128] = windowed[:, 128:]
+    rim_ref[:, 128:] = values[:, 128:]
+    vlin = values[:, :128]
+    pack_ref[:, :128] = windowed[:, :128]
+    pack_ref[:, 128:256] = vlin
     pack_ref[:, 256:288] = feats
     pack_ref[:, 288:] = jnp.zeros((count, 96), BF)
-    vlin = values[:, :128]
-    pack_ref[:, 128:256] = vlin
     first, second = pick((ROWS, FEAT), 0)
     scale, add_first, add_second = weights_of((ROWS, 1), 0, False)
     k = feats[:, FEAT:]
@@ -110,13 +115,9 @@
     state = dot(phi.astype(BF), vlin)
     for i in range(4):
         state_ref[i, :, :] = state[QUARTER * i : QUARTER * (i + 1), :].astype(BF)
-    windowed = dot(n, ww_ref[...]).astype(BF)
-    pack_ref[:, :128] = windowed[:, :128]
-    rim_ref[:, :128] = windowed[:, 128:]
-    rim_ref[:, 128:] = values[:, 128:]
-
-
-def inner_kernel(pack_ref, num_ref):
+
+
+def inner_kernel(pack_ref, after_ref, num_ref):
     count = pack_ref.shape[0]
     tile = 256
     for t in range(count // tile):
@@ -165,11 +166,16 @@
     mix_ref[:, 128:] = win_ref[...]
 
 
-def output_kernel(core_ref, mix_ref, w_ref, mix2_ref, w2_ref, sum_ref):
+def own_kernel(core_ref, mix_ref, w_ref, sum_ref):
     for y in range(4):
         at = pl.multiple_of((2 * y + core_ref[0]) * 256, 256)
-        total = dot(mix_ref[...], w_ref[:, pl.ds(at, 256)]) + dot(mix2_ref[...], w2_ref[:, pl.ds(at, 256)])
-        sum_ref[y, :, :] = total.astype(BF)
+        sum_ref[y, :, :] = dot(mix_ref[...], w_ref[:, pl.ds(at, 256)])
+
+
+def output_kernel(core_ref, mix_ref, w_ref, own_ref, sum_ref):
+    for y in range(4):
+        at = pl.multiple_of((2 * y + core_ref[0]) * 256, 256)
+        sum_ref[y, :, :] = (own_ref[y, :, :] + dot(mix_ref[...], w_ref[:, pl.ds(at, 256)])).astype(BF)
 
 
 def total_kernel(got_ref, out_ref):
@@ -206,16 +212,12 @@
     spread = lax.all_to_all(
         jnp.broadcast_to(tokens[None], (4,) + tokens.shape), "head", 0, 0, tiled=True, axis_index_groups=along_y
     )
-    spread, w_later = lax.optimization_barrier((spread, w_out))
     other = across(spread)
-    w_other = across(w_later)
+    weights = (gain.reshape(1, -1), w_feat.T, w_value, w_window)
+    held = call_with_scalar(begin_kernel, shape((count, 640), F32), 5)(core, spread, *weights)
     pack, rim, states = call_with_scalar(
-        project_kernel,
-        [shape((count, 384)), shape((count, 256)), shape((4, QUARTER, 128))],
-        6,
-        [pltpu.VMEM((count, 2048), BF), pltpu.VMEM((32, 2048), BF), pltpu.SemaphoreType.DMA],
-        4,
-    )(core, spread, other, gain.reshape(1, -1), w_feat.T, w_value, w_window)
+        project_kernel, [shape((count, 384)), shape((count, 256)), shape((4, QUARTER, 128))], 6
+    )(core, other, *weights, held)
     in_x = [[4 * z + x for x in range(4)] for z in range(16)]
     in_z = [[4 * z + x for z in range(16)] for x in range(4)]
     quarters = lax.all_to_all(states, "ctx", 0, 0, tiled=True, axis_index_groups=in_x)
@@ -224,7 +226,9 @@
         call(total_kernel, shape((16, QUARTER, 128)))(quarters), "ctx", 0, 0, tiled=True, axis_index_groups=in_z
     )
     prev = lax.ppermute(rim, "ctx", [(b, b + 1) for b in range(63)])
-    numerator = call(inner_kernel, shape((count, 128), F32))(pack)
+    numerator = call(inner_kernel, shape((count, 128), F32))(pack, quarters)
+    w_later, prev = lax.optimization_barrier((w_out, prev))
+    w_other = across(w_later)
     win_out = call_with_scalar(attend_kernel, shape((count, 128)), 3)(ctx.astype(jnp.int32).reshape(1), pack, rim, prev)
     sums = call_with_scalar(prefix_kernel, shape((4, QUARTER, 128)), 2)(
         (ctx // 4).astype(jnp.int32).reshape(1), quarters, totals
@@ -232,7 +236,8 @@
     sums, numerator, win_out = lax.optimization_barrier((sums, numerator, win_out))
     prefix = lax.all_to_all(sums, "ctx", 0, 0, tiled=True, axis_index_groups=in_x)
     mix = call(linear_kernel, shape((count, 256)))(pack, numerator, prefix, win_out)
-    summed = call_with_scalar(output_kernel, shape((4, count, 256)), 4)(core, mix, w_out, across(mix), w_other)
+    own = call_with_scalar(own_kernel, shape((4, count, 256), F32), 2)(core, mix, w_out)
+    summed = call_with_scalar(output_kernel, shape((4, count, 256)), 3)(core, across(mix), w_other, own)
     parts = lax.all_to_all(summed, "head", 0, 0, tiled=True, axis_index_groups=along_y)
     return jnp.sum(parts.astype(F32), axis=0).astype(BF)
 

time: 108 us -> 115 us (1.065)
  starting transfers between devices: 32.3 us -> 39.4 us
  waiting for transfers between devices: 9.6 us -> 16.1 us
  blocking collectives: 50.5 us -> 47.7 us
  Pallas kernels: 10.8 us -> 8.9 us
  local copies, waits for them, and re-layouts: 2.87 us -> 1.18 us
    all_to_all x1, waiting for transfers between devices: 5.38 us -> 11 us  [shards(): lax.all_to_all(call(total_kernel, shape((16, QUARTER, 128)))(quarters), '...]
    all_to_all x1, starting transfers between devices: 14.9 us -> 20.1 us  [shards(): lax.all_to_all(call(total_kernel, shape((16, QUARTER, 128)))(quarters), '...]
    all_to_all x1, blocking collectives: 9.51 us -> 6.7 us  [shards(): lax.all_to_all(sums, 'ctx', 0, 0, tiled=True, axis_index_groups=in_x)]
    pallas_call x1, Pallas kernels: 5.37 us -> 2.58 us  [shards(): call_with_scalar(project_kernel, [shape((count, 384)), shape((count, 256)...]
    ppermute x3, starting transfers between devices: 15.2 us -> 17.1 us  [across(): return lax.ppermute(value, 'head', [(h, h ^ 1) for h in range(8)])]
    unnamed x12 -> x8, local copies, waits for them, and re-layouts: 1.86 us -> 0.02 us
    pallas_call x2 -> x4, Pallas kernels: 2.88 us -> 3.73 us  [the longest x1 1.68 us: shards(): call_with_scalar(own_kernel, shape((4, count, 256), F32), 2)]
  transfers between devices with their start and end apart: 5 -> 5, of which waited for: 4 -> 3; matrix products, arithmetic and copies ran while one was open for 0% -> 0% of each run, Pallas kernels for 8% -> 5%
where the time goes in v6:
time: 115 us; the launch traced here: 114 us
  blocking collectives  47.7 us (41%)
  starting transfers between devices  39.4 us (34%)
  waiting for transfers between devices  16.1 us (14%)
  Pallas kernels  8.9 us (8%)
  local copies, waits for them, and re-layouts  1.18 us (1%)
    all_to_all x1, starting transfers between devices, shards(): lax.all_to_all(call(total_kernel, shape((16, QUARTER, 128)))(quarters), '...  20.1 us
    all_to_all x1, blocking collectives, shards(): lax.all_to_all(summed, 'head', 0, 0, tiled=True, axis_index_groups=along_y)  17.4 us
    ppermute x3, starting transfers between devices, across(): return lax.ppermute(value, 'head', [(h, h ^ 1) for h in range(8)])  17.1 us
    all_to_all x1, blocking collectives, shards(): lax.all_to_all(jnp.broadcast_to(tokens[None], (4,) + tokens.shape), 'head...  15.5 us
    all_to_all x1, waiting for transfers between devices, shards(): lax.all_to_all(call(total_kernel, shape((16, QUARTER, 128)))(quarters), '...  11 us
    all_to_all x1, blocking collectives, shards(): lax.all_to_all(states, 'ctx', 0, 0, tiled=True, axis_index_groups=in_x)  8.16 us
    all_to_all x1, blocking collectives, shards(): lax.all_to_all(sums, 'ctx', 0, 0, tiled=True, axis_index_groups=in_x)  6.7 us
    ppermute x1, waiting for transfers between devices, shards(): prev = lax.ppermute(rim, 'ctx', [(b, b + 1) for b in range(63)])  3.77 us
  transfers between devices with their start and end apart: 5, of which 3 were waited for; matrix products, arithmetic and copies ran while one was open for 0% of the time, Pallas kernels for 5%

profile of v6, /device:TPU:1, one launch (start us, length us, event | category | flops | bytes accessed | tf_op | source)
XLA Modules:
  0.0 114.4 jit_solution(13637970765231911547)
XLA Ops:
  0.0 0.0 copy-start.1
  0.0 0.0 copy-start
  0.0 0.0 copy-start.2
  0.0 0.0 copy-start.3
  0.0 1.2 %broadcast_in_dim.2 = bf16[4,512,256]{2,1,0:T(8,128)(2,1)S(1)} broadcast(bf16[512,256]{1,0:T(8,128)(2,1)} %param.6), dimensions={1,2} | broadcast | bytes 1310720 | tf_op jit(solution)/shard_map/broadcast_in_dim | solution.py:213
  1.2 15.5 %all_to_all.25.x_ref = bf16[4,512,256]{2,1,0:T(8,128)(2,1)S(1)} all-to-all(bf16[4,512,256]{2,1,0:T(8,128)(2,1)S(1)} %broadcast_in_dim.2), channel_id=1, replica_groups={{0,2,4,6},{1,3,5,7},{8,10,12,14},{9,11,13,15},{16,18,20,22},{17,19,21,2..., dimensions={0} | all-to-all | bytes 2097152 | tf_op jit(solution)/shard_map/all_to_all | solution.py:212
  16.7 7.3 %collective-permute-start = (bf16[4,512,256]{2,1,0:T(8,128)(2,1)S(1)}, bf16[4,512,256]{2,1,0:T(8,128)(2,1)}, u32[]{:S(2)}, u32[]{:S(2)}) collective-permute-start(bf16[4,512,256]{2,1,0:T(8,128)(2,1)S(1)} %all_to_all.25.x_ref), channel_id=1, source_target_pairs={{0,1},{1,0},{2,3},{3,2},{4,5},{5,4},{6,7},{7,6},{8,9},{9,8},{10,11... | collective-permute-start | bytes 3145736 | tf_op jit(solution)/shard_map/ppermute | solution.py:207
  24.0 0.0 copy-done.1
  24.0 0.0 copy-done
  24.0 0.0 copy-done.2
  24.0 0.0 copy-done.3
  24.0 1.0 shard_map.64.held_ref
  25.0 1.4 %collective-permute-done.x_ref = bf16[4,512,256]{2,1,0:T(8,128)(2,1)} collective-permute-done((bf16[4,512,256]{2,1,0:T(8,128)(2,1)S(1)}, bf16[4,512,256]{2,1,0:T(8,128)(2,1)}, u32[]{:S(2)}, u32[]{:S(2)}) %collective-permute-start) | collective-permute-done | bytes 1048608 | tf_op jit(solution)/shard_map/ppermute | solution.py:207
  26.4 2.6 %shard_map.65 = (bf16[512,384]{1,0:T(8,128)(2,1)S(1)}, bf16[512,256]{1,0:T(8,128)(2,1)S(1)}, bf16[4,40,128]{2,1,0:T(8,128)(2,1)S(1)}) custom-call(s32[1]{0:T(128)} %bitcast.core_ref, bf16[4,512,256]{2,1,0:T(8,128)(2,1)} %collective-permute-done.x_ref, f32[1,2048]{1,0:T(1,128)S(1)} %bitcast.8, bf16[32,2048]{1,0:T(8,128)(2,1)S(1)} %bitcast.6, ...), custom_call_target="tpu_custom_call" | custom-call | tf_op jit(solution)/shard_map/pallas_call | solution.py:218
  29.0 8.2 %all_to_all.26.got_ref.after_ref = bf16[4,40,128]{2,1,0:T(8,128)(2,1)S(1)} all-to-all(bf16[4,40,128]{2,1,0:T(8,128)(2,1)S(1)} %get-tuple-element.17), channel_id=1, replica_groups={{0,8,16,24},{32,40,48,56},{64,72,80,88},{96,104,112,120},{128,136,144,1..., dimensions={0} | all-to-all | bytes 81920 | tf_op jit(solution)/shard_map/all_to_all | solution.py:223
  37.1 2.2 %collective-permute-start.1 = (bf16[512,256]{1,0:T(8,128)(2,1)S(1)}, bf16[512,256]{1,0:T(8,128)(2,1)S(1)}, u32[]{:S(2)}, u32[]{:S(2)}) collective-permute-start(bf16[512,256]{1,0:T(8,128)(2,1)S(1)} %get-tuple-element.19.own_ref), channel_id=1, source_target_pairs={{0,8},{8,16},{16,24},{24,32},{32,40},{40,48},{48,56},{56,64},{64,7... | collective-permute-start | bytes 786440 | tf_op jit(solution)/shard_map/ppermute | solution.py:228
  39.3 3.8 %collective-permute-done.1.prev_ref = bf16[512,256]{1,0:T(8,128)(2,1)S(1)} collective-permute-done((bf16[512,256]{1,0:T(8,128)(2,1)S(1)}, bf16[512,256]{1,0:T(8,128)(2,1)S(1)}, u32[]{:S(2)}, u32[]{:S(2)}) %collective-permute-start.1) | collective-permute-done | bytes 262176 | tf_op jit(solution)/shard_map/ppermute | solution.py:228
  43.1 4.6 %collective-permute-start.3 = (bf16[256,2048]{1,0:T(8,128)(2,1)}, bf16[256,2048]{1,0:T(8,128)(2,1)S(1)}, u32[]{:S(2)}, u32[]{:S(2)}) collective-permute-start(bf16[256,2048]{1,0:T(8,128)(2,1)} %w_ref.1), channel_id=1, source_target_pairs={{0,1},{1,0},{2,3},{3,2},{4,5},{5,4},{6,7},{7,6},{8,9},{9,8},{10,11... | collective-permute-start | bytes 3145736 | tf_op jit(solution)/shard_map/ppermute | solution.py:207
  47.7 0.7 shard_map.66
  48.4 20.1 %all-to-all-start.2 = ((bf16[16,40,128]{2,1,0:T(8,128)(2,1)}), bf16[16,40,128]{2,1,0:T(8,128)(2,1)S(1)}, u32[]{:S(2)}, u32[]{:S(2)}) async-start(bf16[16,40,128]{2,1,0:T(8,128)(2,1)} %shard_map.66), calls=%async_computation.2 | async-start | bytes 327680 | tf_op jit(solution)/shard_map/all_to_all | solution.py:225
  68.6 0.6 shard_map.68.num_ref
  69.2 1.3 %shard_map.69.win_ref = bf16[512,128]{1,0:T(8,128)(2,1)S(1)} custom-call(s32[1]{0:T(128)} %bitcast.4.first_ref, bf16[512,384]{1,0:T(8,128)(2,1)S(1)} %get-tuple-element.15.pack_ref, bf16[512,256]{1,0:T(8,128)(2,1)S(1)} %get-tuple-element.19.own_ref, bf16[512,256]{1,0:T(8,128)(2,1)S(1)} %collective-permute-done.1.prev_ref), custom_call_target="tpu_custom_call" | custom-call | tf_op jit(solution)/shard_map/pallas_call | solution.py:232
  70.5 11.0 %all-to-all-done.2.totals_ref = bf16[16,40,128]{2,1,0:T(8,128)(2,1)S(1)} async-done(((bf16[16,40,128]{2,1,0:T(8,128)(2,1)}), bf16[16,40,128]{2,1,0:T(8,128)(2,1)S(1)}, u32[]{:S(2)}, u32[]{:S(2)}) %all-to-all-start.2) | async-done | bytes 163872 | tf_op jit(solution)/shard_map/all_to_all | solution.py:225
  81.5 6.7 %all_to_all.27.prefix_ref = bf16[4,40,128]{2,1,0:T(8,128)(2,1)S(1)} all-to-all(bf16[4,40,128]{2,1,0:T(8,128)(2,1)S(1)} %shard_map.67), channel_id=1, replica_groups={{0,8,16,24},{32,40,48,56},{64,72,80,88},{96,104,112,120},{128,136,144,1..., dimensions={0} | all-to-all | bytes 81920 | tf_op jit(solution)/shard_map/all_to_all | solution.py:237
  88.2 0.6 shard_map.70.mix_ref
  88.8 5.2 %collective-permute-start.2 = (bf16[512,256]{1,0:T(8,128)(2,1)S(1)}, bf16[512,256]{1,0:T(8,128)(2,1)S(1)}, u32[]{:S(2)}, u32[]{:S(2)}) collective-permute-start(bf16[512,256]{1,0:T(8,128)(2,1)S(1)} %shard_map.70.mix_ref), channel_id=1, source_target_pairs={{0,1},{1,0},{2,3},{3,2},{4,5},{5,4},{6,7},{7,6},{8,9},{9,8},{10,11... | collective-permute-start | bytes 786440 | tf_op jit(solution)/shard_map/ppermute | solution.py:207
  93.9 1.7 %shard_map.71.own_ref = f32[4,512,256]{2,1,0:T(8,128)S(1)} custom-call(s32[1]{0:T(128)} %bitcast.core_ref, bf16[512,256]{1,0:T(8,128)(2,1)S(1)} %shard_map.70.mix_ref, bf16[256,2048]{1,0:T(8,128)(2,1)} %w_ref.1), custom_call_target="tpu_custom_call" | custom-call | tf_op jit(solution)/shard_map/pallas_call | solution.py:239
  95.6 0.0 collective-permute-done.2.mix_ref
  95.6 0.0 collective-permute-done.3.w_ref
  95.6 0.5 shard_map.72
  96.1 17.4 %all_to_all.28 = bf16[4,512,256]{2,1,0:T(8,128)(2,1)S(1)} all-to-all(bf16[4,512,256]{2,1,0:T(8,128)(2,1)S(1)} %shard_map.72), channel_id=1, replica_groups={{0,2,4,6},{1,3,5,7},{8,10,12,14},{9,11,13,15},{16,18,20,22},{17,19,21,2..., dimensions={0} | all-to-all | bytes 2097152 | tf_op jit(solution)/shard_map/all_to_all | solution.py:241
  113.5 0.9 reduce_sum.12
  (1 shorter events, 0.0 us)
Async XLA Ops:
  0.0 24.0 %copy-start.1 = (bf16[2048,256]{1,0:T(8,128)(2,1)S(1)}, bf16[2048,256]{1,0:T(8,128)(2,1)}, u32[]{:S(2)}) copy-start(bf16[2048,256]{1,0:T(8,128)(2,1)} %ww_ref.3) | copy-start | bytes 3145732
  0.0 24.0 %copy-start = (bf16[2048,256]{1,0:T(8,128)(2,1)S(1)}, bf16[2048,256]{1,0:T(8,128)(2,1)}, u32[]{:S(2)}) copy-start(bf16[2048,256]{1,0:T(8,128)(2,1)} %wv_ref.3) | copy-start | bytes 3145732
  0.0 24.0 %copy-start.2 = (bf16[2048,32]{0,1:T(8,128)(2,1)S(1)}, bf16[2048,32]{0,1:T(8,128)(2,1)}, u32[]{:S(2)}) copy-start(bf16[2048,32]{0,1:T(8,128)(2,1)} %param.8) | copy-start | bytes 393220
  0.0 24.0 %copy-start.3 = (f32[2048]{0:T(1024)S(1)}, f32[2048]{0:T(1024)}, u32[]{:S(2)}) copy-start(f32[2048]{0:T(1024)} %param.7) | copy-start | bytes 24580
  16.7 9.7 %collective-permute-start = (bf16[4,512,256]{2,1,0:T(8,128)(2,1)S(1)}, bf16[4,512,256]{2,1,0:T(8,128)(2,1)}, u32[]{:S(2)}, u32[]{:S(2)}) collective-permute-start(bf16[4,512,256]{2,1,0:T(8,128)(2,1)S(1)} %all_to_all.25.x_ref), channel_id=1, source_target_pairs={{0,1},{1,0},{2,3},{3,2},{4,5},{5,4},{6,7},{7,6},{8,9},{9,8},{10,11... | collective-permute-start | bytes 3145736 | tf_op jit(solution)/shard_map/ppermute | solution.py:207
  37.1 6.0 %collective-permute-start.1 = (bf16[512,256]{1,0:T(8,128)(2,1)S(1)}, bf16[512,256]{1,0:T(8,128)(2,1)S(1)}, u32[]{:S(2)}, u32[]{:S(2)}) collective-permute-start(bf16[512,256]{1,0:T(8,128)(2,1)S(1)} %get-tuple-element.19.own_ref), channel_id=1, source_target_pairs={{0,8},{8,16},{16,24},{24,32},{32,40},{40,48},{48,56},{56,64},{64,7... | collective-permute-start | bytes 786440 | tf_op jit(solution)/shard_map/ppermute | solution.py:228
  43.1 52.6 %collective-permute-start.3 = (bf16[256,2048]{1,0:T(8,128)(2,1)}, bf16[256,2048]{1,0:T(8,128)(2,1)S(1)}, u32[]{:S(2)}, u32[]{:S(2)}) collective-permute-start(bf16[256,2048]{1,0:T(8,128)(2,1)} %w_ref.1), channel_id=1, source_target_pairs={{0,1},{1,0},{2,3},{3,2},{4,5},{5,4},{6,7},{7,6},{8,9},{9,8},{10,11... | collective-permute-start | bytes 3145736 | tf_op jit(solution)/shard_map/ppermute | solution.py:207
  48.4 33.0 %all-to-all-start.2 = ((bf16[16,40,128]{2,1,0:T(8,128)(2,1)}), bf16[16,40,128]{2,1,0:T(8,128)(2,1)S(1)}, u32[]{:S(2)}, u32[]{:S(2)}) async-start(bf16[16,40,128]{2,1,0:T(8,128)(2,1)} %shard_map.66), calls=%async_computation.2 | async-start | bytes 327680 | tf_op jit(solution)/shard_map/all_to_all | solution.py:225
  88.8 6.9 %collective-permute-start.2 = (bf16[512,256]{1,0:T(8,128)(2,1)S(1)}, bf16[512,256]{1,0:T(8,128)(2,1)S(1)}, u32[]{:S(2)}, u32[]{:S(2)}) collective-permute-start(bf16[512,256]{1,0:T(8,128)(2,1)S(1)} %shard_map.70.mix_ref), channel_id=1, source_target_pairs={{0,1},{1,0},{2,3},{3,2},{4,5},{5,4},{6,7},{7,6},{8,9},{9,8},{10,11... | collective-permute-start | bytes 786440 | tf_op jit(solution)/shard_map/ppermute | solution.py:207

commit v7 on v6

--- a/solution.py
+++ b/solution.py
@@ -212,7 +212,9 @@
     spread = lax.all_to_all(
         jnp.broadcast_to(tokens[None], (4,) + tokens.shape), "head", 0, 0, tiled=True, axis_index_groups=along_y
     )
+    spread, w_later = lax.optimization_barrier((spread, w_out))
     other = across(spread)
+    w_other = across(w_later)
     weights = (gain.reshape(1, -1), w_feat.T, w_value, w_window)
     held = call_with_scalar(begin_kernel, shape((count, 640), F32), 5)(core, spread, *weights)
     pack, rim, states = call_with_scalar(
@@ -227,8 +229,6 @@
     )
     prev = lax.ppermute(rim, "ctx", [(b, b + 1) for b in range(63)])
     numerator = call(inner_kernel, shape((count, 128), F32))(pack, quarters)
-    w_later, prev = lax.optimization_barrier((w_out, prev))
-    w_other = across(w_later)
     win_out = call_with_scalar(attend_kernel, shape((count, 128)), 3)(ctx.astype(jnp.int32).reshape(1), pack, rim, prev)
     sums = call_with_scalar(prefix_kernel, shape((4, QUARTER, 128)), 2)(
         (ctx // 4).astype(jnp.int32).reshape(1), quarters, totals

time: 115 us -> 104 us (0.904)
  waiting for transfers between devices: 16.1 us -> 8.03 us
  starting transfers between devices: 39.4 us -> 32.4 us
  blocking collectives: 47.7 us -> 50.5 us
  Pallas kernels: 8.9 us -> 10.1 us
    all_to_all x1, waiting for transfers between devices: 11 us -> 5.37 us  [shards(): lax.all_to_all(call(total_kernel, shape((16, QUARTER, 128)))(quarters), '...]
    all_to_all x1, starting transfers between devices: 20.1 us -> 14.9 us  [shards(): lax.all_to_all(call(total_kernel, shape((16, QUARTER, 128)))(quarters), '...]
    all_to_all x1, blocking collectives: 6.7 us -> 9.53 us  [shards(): lax.all_to_all(sums, 'ctx', 0, 0, tiled=True, axis_index_groups=in_x)]
    ppermute x3, starting transfers between devices: 17.1 us -> 15.3 us  [across(): return lax.ppermute(value, 'head', [(h, h ^ 1) for h in range(8)])]
    ppermute x3, waiting for transfers between devices: 1.36 us -> 0.01 us  [across(): return lax.ppermute(value, 'head', [(h, h ^ 1) for h in range(8)])]
    pallas_call x1, Pallas kernels: 0.46 us -> 1.68 us  [shards(): call_with_scalar(output_kernel, shape((4, count, 256)), 3)]
  transfers between devices with their start and end apart: 5 -> 5, of which waited for: 3 -> 2; matrix products, arithmetic and copies ran while one was open for 0% -> 0% of each run, Pallas kernels for 5% -> 8%
where the time goes in v7:
time: 104 us; the launch traced here: 103 us
  blocking collectives  50.5 us (49%)
  starting transfers between devices  32.4 us (31%)
  Pallas kernels  10.1 us (10%)
  waiting for transfers between devices  8.03 us (8%)
  local copies, waits for them, and re-layouts  1.18 us (1%)
    all_to_all x1, blocking collectives, shards(): lax.all_to_all(summed, 'head', 0, 0, tiled=True, axis_index_groups=along_y)  17.4 us
    all_to_all x1, blocking collectives, shards(): lax.all_to_all(jnp.broadcast_to(tokens[None], (4,) + tokens.shape), 'head...  15.5 us
    ppermute x3, starting transfers between devices, across(): return lax.ppermute(value, 'head', [(h, h ^ 1) for h in range(8)])  15.3 us
    all_to_all x1, starting transfers between devices, shards(): lax.all_to_all(call(total_kernel, shape((16, QUARTER, 128)))(quarters), '...  14.9 us
    all_to_all x1, blocking collectives, shards(): lax.all_to_all(sums, 'ctx', 0, 0, tiled=True, axis_index_groups=in_x)  9.53 us
    all_to_all x1, blocking collectives, shards(): lax.all_to_all(states, 'ctx', 0, 0, tiled=True, axis_index_groups=in_x)  8.15 us
    all_to_all x1, waiting for transfers between devices, shards(): lax.all_to_all(call(total_kernel, shape((16, QUARTER, 128)))(quarters), '...  5.37 us
    ppermute x1, waiting for transfers between devices, shards(): prev = lax.ppermute(rim, 'ctx', [(b, b + 1) for b in range(63)])  2.65 us
  transfers between devices with their start and end apart: 5, of which 2 were waited for; matrix products, arithmetic and copies ran while one was open for 0% of the time, Pallas kernels for 8%

profile of v7, /device:TPU:1, one launch (start us, length us, event | category | flops | bytes accessed | tf_op | source)
XLA Modules:
  0.0 103.4 jit_solution(10471120816753583156)
XLA Ops:
  0.0 0.0 copy-start.3
  0.0 0.0 copy-start.2
  0.0 0.0 copy-start.1
  0.0 0.0 copy-start
  0.0 1.2 %broadcast_in_dim.2 = bf16[4,512,256]{2,1,0:T(8,128)(2,1)S(1)} broadcast(bf16[512,256]{1,0:T(8,128)(2,1)} %param.6), dimensions={1,2} | broadcast | bytes 1310720 | tf_op jit(solution)/shard_map/broadcast_in_dim | solution.py:213
  1.2 15.5 %all_to_all.25.x_ref = bf16[4,512,256]{2,1,0:T(8,128)(2,1)S(1)} all-to-all(bf16[4,512,256]{2,1,0:T(8,128)(2,1)S(1)} %broadcast_in_dim.2), channel_id=1, replica_groups={{0,2,4,6},{1,3,5,7},{8,10,12,14},{9,11,13,15},{16,18,20,22},{17,19,21,2..., dimensions={0} | all-to-all | bytes 2097152 | tf_op jit(solution)/shard_map/all_to_all | solution.py:212
  16.7 7.3 %collective-permute-start = (bf16[4,512,256]{2,1,0:T(8,128)(2,1)S(1)}, bf16[4,512,256]{2,1,0:T(8,128)(2,1)}, u32[]{:S(2)}, u32[]{:S(2)}) collective-permute-start(bf16[4,512,256]{2,1,0:T(8,128)(2,1)S(1)} %all_to_all.25.x_ref), channel_id=1, source_target_pairs={{0,1},{1,0},{2,3},{3,2},{4,5},{5,4},{6,7},{7,6},{8,9},{9,8},{10,11... | collective-permute-start | bytes 3145736 | tf_op jit(solution)/shard_map/ppermute | solution.py:207
  24.0 1.9 %collective-permute-start.3 = (bf16[256,2048]{1,0:T(8,128)(2,1)}, bf16[256,2048]{1,0:T(8,128)(2,1)}, u32[]{:S(2)}, u32[]{:S(2)}) collective-permute-start(bf16[256,2048]{1,0:T(8,128)(2,1)} %w_ref.1), channel_id=1, source_target_pairs={{0,1},{1,0},{2,3},{3,2},{4,5},{5,4},{6,7},{7,6},{8,9},{9,8},{10,11... | collective-permute-start | bytes 3145736 | tf_op jit(solution)/shard_map/ppermute | solution.py:207
  25.9 0.0 copy-done.3
  25.9 0.0 copy-done.2
  25.9 0.0 copy-done.1
  25.9 0.0 copy-done
  25.9 1.0 shard_map.64.held_ref
  26.9 0.0 collective-permute-done.x_ref
  26.9 2.6 %shard_map.65 = (bf16[512,384]{1,0:T(8,128)(2,1)S(1)}, bf16[512,256]{1,0:T(8,128)(2,1)S(1)}, bf16[4,40,128]{2,1,0:T(8,128)(2,1)S(1)}) custom-call(s32[1]{0:T(128)} %bitcast.core_ref, bf16[4,512,256]{2,1,0:T(8,128)(2,1)} %collective-permute-done.x_ref, f32[1,2048]{1,0:T(1,128)S(1)} %bitcast.8, bf16[32,2048]{1,0:T(8,128)(2,1)S(1)} %bitcast.6, ...), custom_call_target="tpu_custom_call" | custom-call | tf_op jit(solution)/shard_map/pallas_call | solution.py:220
  29.5 8.2 %all_to_all.26.got_ref.after_ref = bf16[4,40,128]{2,1,0:T(8,128)(2,1)S(1)} all-to-all(bf16[4,40,128]{2,1,0:T(8,128)(2,1)S(1)} %get-tuple-element.18), channel_id=1, replica_groups={{0,8,16,24},{32,40,48,56},{64,72,80,88},{96,104,112,120},{128,136,144,1..., dimensions={0} | all-to-all | bytes 81920 | tf_op jit(solution)/shard_map/all_to_all | solution.py:225
  37.7 0.7 shard_map.66
  38.4 14.9 %all-to-all-start.2 = ((bf16[16,40,128]{2,1,0:T(8,128)(2,1)}), bf16[16,40,128]{2,1,0:T(8,128)(2,1)S(1)}, u32[]{:S(2)}, u32[]{:S(2)}) async-start(bf16[16,40,128]{2,1,0:T(8,128)(2,1)} %shard_map.66), calls=%async_computation.2 | async-start | bytes 327680 | tf_op jit(solution)/shard_map/all_to_all | solution.py:227
  53.3 2.2 %collective-permute-start.1 = (bf16[512,256]{1,0:T(8,128)(2,1)S(1)}, bf16[512,256]{1,0:T(8,128)(2,1)S(1)}, u32[]{:S(2)}, u32[]{:S(2)}) collective-permute-start(bf16[512,256]{1,0:T(8,128)(2,1)S(1)} %get-tuple-element.20.own_ref), channel_id=1, source_target_pairs={{0,8},{8,16},{16,24},{24,32},{32,40},{40,48},{48,56},{56,64},{64,7... | collective-permute-start | bytes 786440 | tf_op jit(solution)/shard_map/ppermute | solution.py:230
  55.5 0.6 shard_map.68.num_ref
  56.2 2.6 %collective-permute-done.1.prev_ref = bf16[512,256]{1,0:T(8,128)(2,1)S(1)} collective-permute-done((bf16[512,256]{1,0:T(8,128)(2,1)S(1)}, bf16[512,256]{1,0:T(8,128)(2,1)S(1)}, u32[]{:S(2)}, u32[]{:S(2)}) %collective-permute-start.1) | collective-permute-done | bytes 262176 | tf_op jit(solution)/shard_map/ppermute | solution.py:230
  58.8 1.3 %shard_map.69.win_ref = bf16[512,128]{1,0:T(8,128)(2,1)S(1)} custom-call(s32[1]{0:T(128)} %bitcast.4.first_ref, bf16[512,384]{1,0:T(8,128)(2,1)S(1)} %get-tuple-element.16.pack_ref, bf16[512,256]{1,0:T(8,128)(2,1)S(1)} %get-tuple-element.20.own_ref, bf16[512,256]{1,0:T(8,128)(2,1)S(1)} %collective-permute-done.1.prev_ref), custom_call_target="tpu_custom_call" | custom-call | tf_op jit(solution)/shard_map/pallas_call | solution.py:232
  60.1 5.4 %all-to-all-done.2.totals_ref = bf16[16,40,128]{2,1,0:T(8,128)(2,1)S(1)} async-done(((bf16[16,40,128]{2,1,0:T(8,128)(2,1)}), bf16[16,40,128]{2,1,0:T(8,128)(2,1)S(1)}, u32[]{:S(2)}, u32[]{:S(2)}) %all-to-all-start.2) | async-done | bytes 163872 | tf_op jit(solution)/shard_map/all_to_all | solution.py:227
  65.5 9.5 %all_to_all.27.prefix_ref = bf16[4,40,128]{2,1,0:T(8,128)(2,1)S(1)} all-to-all(bf16[4,40,128]{2,1,0:T(8,128)(2,1)S(1)} %shard_map.67), channel_id=1, replica_groups={{0,8,16,24},{32,40,48,56},{64,72,80,88},{96,104,112,120},{128,136,144,1..., dimensions={0} | all-to-all | bytes 81920 | tf_op jit(solution)/shard_map/all_to_all | solution.py:237
  75.0 0.6 shard_map.70.mix_ref
  75.6 6.1 %collective-permute-start.2 = (bf16[512,256]{1,0:T(8,128)(2,1)S(1)}, bf16[512,256]{1,0:T(8,128)(2,1)S(1)}, u32[]{:S(2)}, u32[]{:S(2)}) collective-permute-start(bf16[512,256]{1,0:T(8,128)(2,1)S(1)} %shard_map.70.mix_ref), channel_id=1, source_target_pairs={{0,1},{1,0},{2,3},{3,2},{4,5},{5,4},{6,7},{7,6},{8,9},{9,8},{10,11... | collective-permute-start | bytes 786440 | tf_op jit(solution)/shard_map/ppermute | solution.py:207
  81.7 1.7 %shard_map.71.own_ref = f32[4,512,256]{2,1,0:T(8,128)S(1)} custom-call(s32[1]{0:T(128)} %bitcast.core_ref, bf16[512,256]{1,0:T(8,128)(2,1)S(1)} %shard_map.70.mix_ref, bf16[256,2048]{1,0:T(8,128)(2,1)} %w_ref.1), custom_call_target="tpu_custom_call" | custom-call | tf_op jit(solution)/shard_map/pallas_call | solution.py:239
  83.4 0.0 collective-permute-done.3.w_ref
  83.4 0.0 collective-permute-done.2.mix_ref
  83.4 1.7 %shard_map.72 = bf16[4,512,256]{2,1,0:T(8,128)(2,1)S(1)} custom-call(s32[1]{0:T(128)} %bitcast.core_ref, bf16[512,256]{1,0:T(8,128)(2,1)S(1)} %collective-permute-done.2.mix_ref, bf16[256,2048]{1,0:T(8,128)(2,1)} %collective-permute-done.3.w_ref, f32[4,512,256]{2,1,0:T(8,128)S(1)} %shard_map.71.own_ref), custom_call_target="tpu_custom_call" | custom-call | tf_op jit(solution)/shard_map/pallas_call | solution.py:240
  85.1 17.4 %all_to_all.28 = bf16[4,512,256]{2,1,0:T(8,128)(2,1)S(1)} all-to-all(bf16[4,512,256]{2,1,0:T(8,128)(2,1)S(1)} %shard_map.72), channel_id=1, replica_groups={{0,2,4,6},{1,3,5,7},{8,10,12,14},{9,11,13,15},{16,18,20,22},{17,19,21,2..., dimensions={0} | all-to-all | bytes 2097152 | tf_op jit(solution)/shard_map/all_to_all | solution.py:241
  102.5 0.9 reduce_sum.12
  (1 shorter events, 0.0 us)
Async XLA Ops:
  0.0 25.9 %copy-start.3 = (f32[2048]{0:T(1024)S(1)}, f32[2048]{0:T(1024)}, u32[]{:S(2)}) copy-start(f32[2048]{0:T(1024)} %param.7) | copy-start | bytes 24580
  0.0 25.9 %copy-start.2 = (bf16[2048,32]{0,1:T(8,128)(2,1)S(1)}, bf16[2048,32]{0,1:T(8,128)(2,1)}, u32[]{:S(2)}) copy-start(bf16[2048,32]{0,1:T(8,128)(2,1)} %param.8) | copy-start | bytes 393220
  0.0 25.9 %copy-start.1 = (bf16[2048,256]{1,0:T(8,128)(2,1)S(1)}, bf16[2048,256]{1,0:T(8,128)(2,1)}, u32[]{:S(2)}) copy-start(bf16[2048,256]{1,0:T(8,128)(2,1)} %ww_ref.3) | copy-start | bytes 3145732
  0.0 25.9 %copy-start = (bf16[2048,256]{1,0:T(8,128)(2,1)S(1)}, bf16[2048,256]{1,0:T(8,128)(2,1)}, u32[]{:S(2)}) copy-start(bf16[2048,256]{1,0:T(8,128)(2,1)} %wv_ref.3) | copy-start | bytes 3145732
  16.7 10.3 %collective-permute-start = (bf16[4,512,256]{2,1,0:T(8,128)(2,1)S(1)}, bf16[4,512,256]{2,1,0:T(8,128)(2,1)}, u32[]{:S(2)}, u32[]{:S(2)}) collective-permute-start(bf16[4,512,256]{2,1,0:T(8,128)(2,1)S(1)} %all_to_all.25.x_ref), channel_id=1, source_target_pairs={{0,1},{1,0},{2,3},{3,2},{4,5},{5,4},{6,7},{7,6},{8,9},{9,8},{10,11... | collective-permute-start | bytes 3145736 | tf_op jit(solution)/shard_map/ppermute | solution.py:207
  24.0 59.4 %collective-permute-start.3 = (bf16[256,2048]{1,0:T(8,128)(2,1)}, bf16[256,2048]{1,0:T(8,128)(2,1)}, u32[]{:S(2)}, u32[]{:S(2)}) collective-permute-start(bf16[256,2048]{1,0:T(8,128)(2,1)} %w_ref.1), channel_id=1, source_target_pairs={{0,1},{1,0},{2,3},{3,2},{4,5},{5,4},{6,7},{7,6},{8,9},{9,8},{10,11... | collective-permute-start | bytes 3145736 | tf_op jit(solution)/shard_map/ppermute | solution.py:207
  38.4 27.1 %all-to-all-start.2 = ((bf16[16,40,128]{2,1,0:T(8,128)(2,1)}), bf16[16,40,128]{2,1,0:T(8,128)(2,1)S(1)}, u32[]{:S(2)}, u32[]{:S(2)}) async-start(bf16[16,40,128]{2,1,0:T(8,128)(2,1)} %shard_map.66), calls=%async_computation.2 | async-start | bytes 327680 | tf_op jit(solution)/shard_map/all_to_all | solution.py:227
  53.3 5.5 %collective-permute-start.1 = (bf16[512,256]{1,0:T(8,128)(2,1)S(1)}, bf16[512,256]{1,0:T(8,128)(2,1)S(1)}, u32[]{:S(2)}, u32[]{:S(2)}) collective-permute-start(bf16[512,256]{1,0:T(8,128)(2,1)S(1)} %get-tuple-element.20.own_ref), channel_id=1, source_target_pairs={{0,8},{8,16},{16,24},{24,32},{32,40},{40,48},{48,56},{56,64},{64,7... | collective-permute-start | bytes 786440 | tf_op jit(solution)/shard_map/ppermute | solution.py:230
  75.6 7.8 %collective-permute-start.2 = (bf16[512,256]{1,0:T(8,128)(2,1)S(1)}, bf16[512,256]{1,0:T(8,128)(2,1)S(1)}, u32[]{:S(2)}, u32[]{:S(2)}) collective-permute-start(bf16[512,256]{1,0:T(8,128)(2,1)S(1)} %shard_map.70.mix_ref), channel_id=1, source_target_pairs={{0,1},{1,0},{2,3},{3,2},{4,5},{5,4},{6,7},{7,6},{8,9},{9,8},{10,11... | collective-permute-start | bytes 786440 | tf_op jit(solution)/shard_map/ppermute | solution.py:207

commit v8 on v7

--- a/solution.py
+++ b/solution.py
@@ -166,16 +166,21 @@
     mix_ref[:, 128:] = win_ref[...]
 
 
+def pick_kernel(core_ref, w_ref, after_ref, out_ref):
+    for y in range(4):
+        at = pl.multiple_of((2 * y + 1 - core_ref[0]) * 256, 256)
+        out_ref[y, :, :] = w_ref[:, pl.ds(at, 256)]
+
+
 def own_kernel(core_ref, mix_ref, w_ref, sum_ref):
     for y in range(4):
         at = pl.multiple_of((2 * y + core_ref[0]) * 256, 256)
         sum_ref[y, :, :] = dot(mix_ref[...], w_ref[:, pl.ds(at, 256)])
 
 
-def output_kernel(core_ref, mix_ref, w_ref, own_ref, sum_ref):
-    for y in range(4):
-        at = pl.multiple_of((2 * y + core_ref[0]) * 256, 256)
-        sum_ref[y, :, :] = (own_ref[y, :, :] + dot(mix_ref[...], w_ref[:, pl.ds(at, 256)])).astype(BF)
+def output_kernel(mix_ref, w_ref, own_ref, sum_ref):
+    for y in range(4):
+        sum_ref[y, :, :] = (own_ref[y, :, :] + dot(mix_ref[...], w_ref[y, :, :])).astype(BF)
 
 
 def total_kernel(got_ref, out_ref):
@@ -212,9 +217,7 @@
     spread = lax.all_to_all(
         jnp.broadcast_to(tokens[None], (4,) + tokens.shape), "head", 0, 0, tiled=True, axis_index_groups=along_y
     )
-    spread, w_later = lax.optimization_barrier((spread, w_out))
     other = across(spread)
-    w_other = across(w_later)
     weights = (gain.reshape(1, -1), w_feat.T, w_value, w_window)
     held = call_with_scalar(begin_kernel, shape((count, 640), F32), 5)(core, spread, *weights)
     pack, rim, states = call_with_scalar(
@@ -229,6 +232,7 @@
     )
     prev = lax.ppermute(rim, "ctx", [(b, b + 1) for b in range(63)])
     numerator = call(inner_kernel, shape((count, 128), F32))(pack, quarters)
+    w_other = across(call_with_scalar(pick_kernel, shape((4, 256, 256)), 2)(core, w_out, quarters))
     win_out = call_with_scalar(attend_kernel, shape((count, 128)), 3)(ctx.astype(jnp.int32).reshape(1), pack, rim, prev)
     sums = call_with_scalar(prefix_kernel, shape((4, QUARTER, 128)), 2)(
         (ctx // 4).astype(jnp.int32).reshape(1), quarters, totals
@@ -237,7 +241,7 @@
     prefix = lax.all_to_all(sums, "ctx", 0, 0, tiled=True, axis_index_groups=in_x)
     mix = call(linear_kernel, shape((count, 256)))(pack, numerator, prefix, win_out)
     own = call_with_scalar(own_kernel, shape((4, count, 256), F32), 2)(core, mix, w_out)
-    summed = call_with_scalar(output_kernel, shape((4, count, 256)), 3)(core, across(mix), w_other, own)
+    summed = call(output_kernel, shape((4, count, 256)))(across(mix), w_other, own)
     parts = lax.all_to_all(summed, "head", 0, 0, tiled=True, axis_index_groups=along_y)
     return jnp.sum(parts.astype(F32), axis=0).astype(BF)
 

time: 104 us -> 103 us (level)
  waiting for transfers between devices: 8.03 us -> 4.04 us
  starting transfers between devices: 32.4 us -> 34.3 us
  Pallas kernels: 10.1 us -> 8.79 us
    all_to_all x1, waiting for transfers between devices: 5.37 us -> 2.03 us  [shards(): lax.all_to_all(call(total_kernel, shape((16, QUARTER, 128)))(quarters), '...]
    ppermute x1, waiting for transfers between devices: 2.65 us -> 0.01 us  [shards(): prev = lax.ppermute(rim, 'ctx', [(b, b + 1) for b in range(63)])]
    ppermute x3, waiting for transfers between devices: 0.01 us -> 2.01 us  [across(): return lax.ppermute(value, 'head', [(h, h ^ 1) for h in range(8)])]
    ppermute x3, starting transfers between devices: 15.3 us -> 16.5 us  [across(): return lax.ppermute(value, 'head', [(h, h ^ 1) for h in range(8)])]
    pallas_call x1, Pallas kernels: 1.68 us -> 0.45 us  [shards(): call_with_scalar(own_kernel, shape((4, count, 256), F32), 2)]
    pallas_call x1 -> x2, Pallas kernels: 1.68 us -> 0.51 us  [the longest x1 0.44 us: shards(): call(output_kernel, shape((4, count, 256)))(across(mix), w_other, own)]
  transfers between devices with their start and end apart: 5 -> 5, of which waited for: 2 -> 3; matrix products, arithmetic and copies ran while one was open for 0% -> 0% of each run, Pallas kernels for 8% -> 5%
where the time goes in v8:
time: 103 us; the launch traced here: 102 us
  blocking collectives  51.3 us (50%)
  starting transfers between devices  34.3 us (33%)
  Pallas kernels  8.79 us (9%)
  waiting for transfers between devices  4.04 us (4%)
  local copies, waits for them, and re-layouts  1.9 us (2%)
    all_to_all x1, blocking collectives, shards(): lax.all_to_all(summed, 'head', 0, 0, tiled=True, axis_index_groups=along_y)  17.3 us
    ppermute x3, starting transfers between devices, across(): return lax.ppermute(value, 'head', [(h, h ^ 1) for h in range(8)])  16.5 us
    all_to_all x1, blocking collectives, shards(): lax.all_to_all(jnp.broadcast_to(tokens[None], (4,) + tokens.shape), 'head...  15.5 us
    all_to_all x1, starting transfers between devices, shards(): lax.all_to_all(call(total_kernel, shape((16, QUARTER, 128)))(quarters), '...  14.9 us
    all_to_all x1, blocking collectives, shards(): lax.all_to_all(sums, 'ctx', 0, 0, tiled=True, axis_index_groups=in_x)  10.3 us
    all_to_all x1, blocking collectives, shards(): lax.all_to_all(states, 'ctx', 0, 0, tiled=True, axis_index_groups=in_x)  8.28 us
    ppermute x1, starting transfers between devices, shards(): prev = lax.ppermute(rim, 'ctx', [(b, b + 1) for b in range(63)])  2.9 us
    pallas_call x1, Pallas kernels, shards(): call_with_scalar(project_kernel, [shape((count, 384)), shape((count, 256)...  2.68 us
  transfers between devices with their start and end apart: 5, of which 3 were waited for; matrix products, arithmetic and copies ran while one was open for 0% of the time, Pallas kernels for 5%

profile of v8, /device:TPU:1, one launch (start us, length us, event | category | flops | bytes accessed | tf_op | source)
XLA Modules:
  0.0 101.5 jit_solution(9077866345138320083)
XLA Ops:
  0.0 0.0 copy-start.1
  0.0 0.0 copy-start
  0.0 0.0 copy-start.3
  0.0 0.0 copy-start.7
  0.0 1.2 %broadcast_in_dim.2 = bf16[4,512,256]{2,1,0:T(8,128)(2,1)S(1)} broadcast(bf16[512,256]{1,0:T(8,128)(2,1)} %param.6), dimensions={1,2} | broadcast | bytes 1310720 | tf_op jit(solution)/shard_map/broadcast_in_dim | solution.py:218
  1.2 15.5 %all_to_all.25.x_ref = bf16[4,512,256]{2,1,0:T(8,128)(2,1)S(1)} all-to-all(bf16[4,512,256]{2,1,0:T(8,128)(2,1)S(1)} %broadcast_in_dim.2), channel_id=1, replica_groups={{0,2,4,6},{1,3,5,7},{8,10,12,14},{9,11,13,15},{16,18,20,22},{17,19,21,2..., dimensions={0} | all-to-all | bytes 2097152 | tf_op jit(solution)/shard_map/all_to_all | solution.py:217
  16.7 7.3 %collective-permute-start = (bf16[4,512,256]{2,1,0:T(8,128)(2,1)S(1)}, bf16[4,512,256]{2,1,0:T(8,128)(2,1)}, u32[]{:S(2)}, u32[]{:S(2)}) collective-permute-start(bf16[4,512,256]{2,1,0:T(8,128)(2,1)S(1)} %all_to_all.25.x_ref), channel_id=1, source_target_pairs={{0,1},{1,0},{2,3},{3,2},{4,5},{5,4},{6,7},{7,6},{8,9},{9,8},{10,11... | collective-permute-start | bytes 3145736 | tf_op jit(solution)/shard_map/ppermute | solution.py:212
  24.0 0.0 copy-done.1
  24.0 0.0 copy-done
  24.0 0.0 copy-done.3
  24.0 0.0 copy-done.7
  24.0 0.0 copy-start.4
  24.0 1.0 shard_map.64.held_ref
  25.0 1.3 %collective-permute-done.x_ref = bf16[4,512,256]{2,1,0:T(8,128)(2,1)} collective-permute-done((bf16[4,512,256]{2,1,0:T(8,128)(2,1)S(1)}, bf16[4,512,256]{2,1,0:T(8,128)(2,1)}, u32[]{:S(2)}, u32[]{:S(2)}) %collective-permute-start) | collective-permute-done | bytes 1048608 | tf_op jit(solution)/shard_map/ppermute | solution.py:212
  26.4 0.0 copy-done.4
  26.4 0.0 copy-start.2
  26.4 2.7 %shard_map.65 = (bf16[512,384]{1,0:T(8,128)(2,1)S(1)}, bf16[512,256]{1,0:T(8,128)(2,1)S(1)}, bf16[4,40,128]{2,1,0:T(8,128)(2,1)S(1)}) custom-call(s32[1]{0:T(128)} %bitcast.core_ref, bf16[4,512,256]{2,1,0:T(8,128)(2,1)} %collective-permute-done.x_ref, f32[1,2048]{1,0:T(1,128)S(1)} %bitcast.8, bf16[32,2048]{1,0:T(8,128)(2,1)S(1)} %bitcast.6, ...), custom_call_target="tpu_custom_call" | custom-call | tf_op jit(solution)/shard_map/pallas_call | solution.py:223
  29.0 0.0 copy-start.5
  29.1 0.7 copy-done.5
  29.8 0.0 copy-start.6
  29.8 8.3 %all_to_all.26.got_ref.after_ref = bf16[4,40,128]{2,1,0:T(8,128)(2,1)S(1)} all-to-all(bf16[4,40,128]{2,1,0:T(8,128)(2,1)S(1)} %get-tuple-element.15), channel_id=1, replica_groups={{0,8,16,24},{32,40,48,56},{64,72,80,88},{96,104,112,120},{128,136,144,1..., dimensions={0} | all-to-all | bytes 81920 | tf_op jit(solution)/shard_map/all_to_all | solution.py:228
  38.0 0.7 shard_map.66
  38.7 14.9 %all-to-all-start.2 = ((bf16[16,40,128]{2,1,0:T(8,128)(2,1)}), bf16[16,40,128]{2,1,0:T(8,128)(2,1)S(1)}, u32[]{:S(2)}, u32[]{:S(2)}) async-start(bf16[16,40,128]{2,1,0:T(8,128)(2,1)} %shard_map.66), calls=%async_computation.2 | async-start | bytes 327680 | tf_op jit(solution)/shard_map/all_to_all | solution.py:230
  53.6 2.9 %collective-permute-start.1 = (bf16[512,256]{1,0:T(8,128)(2,1)}, bf16[512,256]{1,0:T(8,128)(2,1)}, u32[]{:S(2)}, u32[]{:S(2)}) collective-permute-start(bf16[512,256]{1,0:T(8,128)(2,1)} %copy-done.5), channel_id=1, source_target_pairs={{0,8},{8,16},{16,24},{24,32},{32,40},{40,48},{48,56},{56,64},{64,7... | collective-permute-start | bytes 786440 | tf_op jit(solution)/shard_map/ppermute | solution.py:233
  56.5 0.0 copy-done.2
  56.5 0.1 shard_map.71
  56.6 4.3 %collective-permute-start.3 = (bf16[4,256,256]{2,1,0:T(8,128)(2,1)S(1)}, bf16[4,256,256]{2,1,0:T(8,128)(2,1)S(1)}, u32[]{:S(2)}, u32[]{:S(2)}) collective-permute-start(bf16[4,256,256]{2,1,0:T(8,128)(2,1)S(1)} %shard_map.71), channel_id=1, source_target_pairs={{0,1},{1,0},{2,3},{3,2},{4,5},{5,4},{6,7},{7,6},{8,9},{9,8},{10,11... | collective-permute-start | bytes 1572872 | tf_op jit(solution)/shard_map/ppermute | solution.py:212
  60.9 0.6 shard_map.68.num_ref
  61.5 0.0 collective-permute-done.1.prev_ref
  61.5 0.0 copy-done.6
  61.6 2.2 %shard_map.69.win_ref = bf16[512,128]{1,0:T(8,128)(2,1)S(1)} custom-call(s32[1]{0:T(128)} %bitcast.4.first_ref, bf16[512,384]{1,0:T(8,128)(2,1)S(1)} %get-tuple-element.13.pack_ref, bf16[512,256]{1,0:T(8,128)(2,1)S(1)} %copy-done.6, bf16[512,256]{1,0:T(8,128)(2,1)} %collective-permute-done.1.prev_ref), custom_call_target="tpu_custom_call" | custom-call | tf_op jit(solution)/shard_map/pallas_call | solution.py:236
  63.8 2.0 %all-to-all-done.2.totals_ref = bf16[16,40,128]{2,1,0:T(8,128)(2,1)S(1)} async-done(((bf16[16,40,128]{2,1,0:T(8,128)(2,1)}), bf16[16,40,128]{2,1,0:T(8,128)(2,1)S(1)}, u32[]{:S(2)}, u32[]{:S(2)}) %all-to-all-start.2) | async-done | bytes 163872 | tf_op jit(solution)/shard_map/all_to_all | solution.py:230
  65.9 10.3 %all_to_all.27.prefix_ref = bf16[4,40,128]{2,1,0:T(8,128)(2,1)S(1)} all-to-all(bf16[4,40,128]{2,1,0:T(8,128)(2,1)S(1)} %shard_map.67), channel_id=1, replica_groups={{0,8,16,24},{32,40,48,56},{64,72,80,88},{96,104,112,120},{128,136,144,1..., dimensions={0} | all-to-all | bytes 81920 | tf_op jit(solution)/shard_map/all_to_all | solution.py:241
  76.2 0.6 shard_map.70.mix_ref
  76.8 5.0 %collective-permute-start.2 = (bf16[512,256]{1,0:T(8,128)(2,1)S(1)}, bf16[512,256]{1,0:T(8,128)(2,1)S(1)}, u32[]{:S(2)}, u32[]{:S(2)}) collective-permute-start(bf16[512,256]{1,0:T(8,128)(2,1)S(1)} %shard_map.70.mix_ref), channel_id=1, source_target_pairs={{0,1},{1,0},{2,3},{3,2},{4,5},{5,4},{6,7},{7,6},{8,9},{9,8},{10,11... | collective-permute-start | bytes 786440 | tf_op jit(solution)/shard_map/ppermute | solution.py:212
  81.7 0.5 shard_map.72.own_ref
  82.2 0.0 collective-permute-done.3.w_ref
  82.2 0.7 collective-permute-done.2.mix_ref
  82.9 0.4 shard_map.73
  83.3 17.3 %all_to_all.28 = bf16[4,512,256]{2,1,0:T(8,128)(2,1)S(1)} all-to-all(bf16[4,512,256]{2,1,0:T(8,128)(2,1)S(1)} %shard_map.73), channel_id=1, replica_groups={{0,2,4,6},{1,3,5,7},{8,10,12,14},{9,11,13,15},{16,18,20,22},{17,19,21,2..., dimensions={0} | all-to-all | bytes 2097152 | tf_op jit(solution)/shard_map/all_to_all | solution.py:245
  100.6 0.9 reduce_sum.12
  (1 shorter events, 0.0 us)
Async XLA Ops:
  0.0 24.0 %copy-start.1 = (bf16[2048,256]{1,0:T(8,128)(2,1)S(1)}, bf16[2048,256]{1,0:T(8,128)(2,1)}, u32[]{:S(2)}) copy-start(bf16[2048,256]{1,0:T(8,128)(2,1)} %ww_ref.3) | copy-start | bytes 3145732
  0.0 24.0 %copy-start = (bf16[2048,256]{1,0:T(8,128)(2,1)S(1)}, bf16[2048,256]{1,0:T(8,128)(2,1)}, u32[]{:S(2)}) copy-start(bf16[2048,256]{1,0:T(8,128)(2,1)} %wv_ref.3) | copy-start | bytes 3145732
  0.0 24.0 %copy-start.3 = (bf16[2048,32]{0,1:T(8,128)(2,1)S(1)}, bf16[2048,32]{0,1:T(8,128)(2,1)}, u32[]{:S(2)}) copy-start(bf16[2048,32]{0,1:T(8,128)(2,1)} %param.8) | copy-start | bytes 393220
  0.0 24.0 %copy-start.7 = (f32[2048]{0:T(1024)S(1)}, f32[2048]{0:T(1024)}, u32[]{:S(2)}) copy-start(f32[2048]{0:T(1024)} %param.7) | copy-start | bytes 24580
  16.7 9.7 %collective-permute-start = (bf16[4,512,256]{2,1,0:T(8,128)(2,1)S(1)}, bf16[4,512,256]{2,1,0:T(8,128)(2,1)}, u32[]{:S(2)}, u32[]{:S(2)}) collective-permute-start(bf16[4,512,256]{2,1,0:T(8,128)(2,1)S(1)} %all_to_all.25.x_ref), channel_id=1, source_target_pairs={{0,1},{1,0},{2,3},{3,2},{4,5},{5,4},{6,7},{7,6},{8,9},{9,8},{10,11... | collective-permute-start | bytes 3145736 | tf_op jit(solution)/shard_map/ppermute | solution.py:212
  24.0 2.3 %copy-start.4 = (bf16[2048,32]{0,1:T(8,128)(2,1)S(1)}, bf16[2048,32]{0,1:T(8,128)(2,1)}, u32[]{:S(2)}) copy-start(bf16[2048,32]{0,1:T(8,128)(2,1)} %param.8) | copy-start | bytes 393220
  26.4 30.2 %copy-start.2 = (bf16[256,2048]{1,0:T(8,128)(2,1)S(1)}, bf16[256,2048]{1,0:T(8,128)(2,1)}, u32[]{:S(2)}) copy-start(bf16[256,2048]{1,0:T(8,128)(2,1)} %w_ref.3) | copy-start | bytes 3145732
  29.0 0.7 copy-start.5
  29.8 31.8 %copy-start.6 = (bf16[512,256]{1,0:T(8,128)(2,1)S(1)}, bf16[512,256]{1,0:T(8,128)(2,1)}, u32[]{:S(2)}) copy-start(bf16[512,256]{1,0:T(8,128)(2,1)} %copy-done.5) | copy-start | bytes 786436
  38.7 27.1 %all-to-all-start.2 = ((bf16[16,40,128]{2,1,0:T(8,128)(2,1)}), bf16[16,40,128]{2,1,0:T(8,128)(2,1)S(1)}, u32[]{:S(2)}, u32[]{:S(2)}) async-start(bf16[16,40,128]{2,1,0:T(8,128)(2,1)} %shard_map.66), calls=%async_computation.2 | async-start | bytes 327680 | tf_op jit(solution)/shard_map/all_to_all | solution.py:230
  53.6 7.9 %collective-permute-start.1 = (bf16[512,256]{1,0:T(8,128)(2,1)}, bf16[512,256]{1,0:T(8,128)(2,1)}, u32[]{:S(2)}, u32[]{:S(2)}) collective-permute-start(bf16[512,256]{1,0:T(8,128)(2,1)} %copy-done.5), channel_id=1, source_target_pairs={{0,8},{8,16},{16,24},{24,32},{32,40},{40,48},{48,56},{56,64},{64,7... | collective-permute-start | bytes 786440 | tf_op jit(solution)/shard_map/ppermute | solution.py:233
  56.6 25.6 %collective-permute-start.3 = (bf16[4,256,256]{2,1,0:T(8,128)(2,1)S(1)}, bf16[4,256,256]{2,1,0:T(8,128)(2,1)S(1)}, u32[]{:S(2)}, u32[]{:S(2)}) collective-permute-start(bf16[4,256,256]{2,1,0:T(8,128)(2,1)S(1)} %shard_map.71), channel_id=1, source_target_pairs={{0,1},{1,0},{2,3},{3,2},{4,5},{5,4},{6,7},{7,6},{8,9},{9,8},{10,11... | collective-permute-start | bytes 1572872 | tf_op jit(solution)/shard_map/ppermute | solution.py:212
  76.8 6.1 %collective-permute-start.2 = (bf16[512,256]{1,0:T(8,128)(2,1)S(1)}, bf16[512,256]{1,0:T(8,128)(2,1)S(1)}, u32[]{:S(2)}, u32[]{:S(2)}) collective-permute-start(bf16[512,256]{1,0:T(8,128)(2,1)S(1)} %shard_map.70.mix_ref), channel_id=1, source_target_pairs={{0,1},{1,0},{2,3},{3,2},{4,5},{5,4},{6,7},{7,6},{8,9},{9,8},{10,11... | collective-permute-start | bytes 786440 | tf_op jit(solution)/shard_map/ppermute | solution.py:212

commit v9 on v8

--- a/solution.py
+++ b/solution.py
@@ -237,7 +237,7 @@
     sums = call_with_scalar(prefix_kernel, shape((4, QUARTER, 128)), 2)(
         (ctx // 4).astype(jnp.int32).reshape(1), quarters, totals
     )
-    sums, numerator, win_out = lax.optimization_barrier((sums, numerator, win_out))
+    sums, numerator = lax.optimization_barrier((sums, numerator))
     prefix = lax.all_to_all(sums, "ctx", 0, 0, tiled=True, axis_index_groups=in_x)
     mix = call(linear_kernel, shape((count, 256)))(pack, numerator, prefix, win_out)
     own = call_with_scalar(own_kernel, shape((4, count, 256), F32), 2)(core, mix, w_out)

time: 103 us -> 103 us (level)
  blocking collectives: 51.3 us -> 41 us
  waiting for transfers between devices: 4.04 us -> 9.98 us
  starting transfers between devices: 34.3 us -> 39.8 us
    all_to_all x1 -> x0, blocking collectives: 10.3 us -> none  [shards(): lax.all_to_all(sums, 'ctx', 0, 0, tiled=True, axis_index_groups=in_x)]
    all_to_all x0 -> x1, starting transfers between devices: none -> 3.27 us  [shards(): lax.all_to_all(sums, 'ctx', 0, 0, tiled=True, axis_index_groups=in_x)]
    all_to_all x0 -> x1, waiting for transfers between devices: none -> 3.01 us  [shards(): lax.all_to_all(sums, 'ctx', 0, 0, tiled=True, axis_index_groups=in_x)]
    ppermute x3, starting transfers between devices: 16.5 us -> 19.5 us  [across(): return lax.ppermute(value, 'head', [(h, h ^ 1) for h in range(8)])]
    all_to_all x1, waiting for transfers between devices: 2.03 us -> 4.96 us  [shards(): lax.all_to_all(call(total_kernel, shape((16, QUARTER, 128)))(quarters), '...]
  transfers between devices with their start and end apart: 5 -> 6, of which waited for: 3 -> 4; matrix products, arithmetic and copies ran while one was open for 0% -> 0% of each run, Pallas kernels for 5% -> 5%
where the time goes in v9:
time: 103 us; the launch traced here: 102 us
  blocking collectives  41 us (40%)
  starting transfers between devices  39.8 us (39%)
  waiting for transfers between devices  9.98 us (10%)
  Pallas kernels  8.44 us (8%)
  local copies, waits for them, and re-layouts  1.9 us (2%)
    ppermute x3, starting transfers between devices, across(): return lax.ppermute(value, 'head', [(h, h ^ 1) for h in range(8)])  19.5 us
    all_to_all x1, blocking collectives, shards(): lax.all_to_all(summed, 'head', 0, 0, tiled=True, axis_index_groups=along_y)  17.3 us
    all_to_all x1, blocking collectives, shards(): lax.all_to_all(jnp.broadcast_to(tokens[None], (4,) + tokens.shape), 'head...  15.5 us
    all_to_all x1, starting transfers between devices, shards(): lax.all_to_all(call(total_kernel, shape((16, QUARTER, 128)))(quarters), '...  14.9 us
    all_to_all x1, blocking collectives, shards(): lax.all_to_all(states, 'ctx', 0, 0, tiled=True, axis_index_groups=in_x)  8.28 us
    all_to_all x1, waiting for transfers between devices, shards(): lax.all_to_all(call(total_kernel, shape((16, QUARTER, 128)))(quarters), '...  4.96 us
    all_to_all x1, starting transfers between devices, shards(): lax.all_to_all(sums, 'ctx', 0, 0, tiled=True, axis_index_groups=in_x)  3.27 us
    all_to_all x1, waiting for transfers between devices, shards(): lax.all_to_all(sums, 'ctx', 0, 0, tiled=True, axis_index_groups=in_x)  3.01 us
  transfers between devices with their start and end apart: 6, of which 4 were waited for; matrix products, arithmetic and copies ran while one was open for 0% of the time, Pallas kernels for 5%

profile of v9, /device:TPU:1, one launch (start us, length us, event | category | flops | bytes accessed | tf_op | source)
XLA Modules:
  0.0 102.3 jit_solution(18396281197475060666)
XLA Ops:
  0.0 0.0 copy-start.1
  0.0 0.0 copy-start
  0.0 0.0 copy-start.3
  0.0 0.0 copy-start.7
  0.0 1.2 %broadcast_in_dim.2 = bf16[4,512,256]{2,1,0:T(8,128)(2,1)S(1)} broadcast(bf16[512,256]{1,0:T(8,128)(2,1)} %param.6), dimensions={1,2} | broadcast | bytes 1310720 | tf_op jit(solution)/shard_map/broadcast_in_dim | solution.py:218
  1.2 15.5 %all_to_all.25.x_ref = bf16[4,512,256]{2,1,0:T(8,128)(2,1)S(1)} all-to-all(bf16[4,512,256]{2,1,0:T(8,128)(2,1)S(1)} %broadcast_in_dim.2), channel_id=1, replica_groups={{0,2,4,6},{1,3,5,7},{8,10,12,14},{9,11,13,15},{16,18,20,22},{17,19,21,2..., dimensions={0} | all-to-all | bytes 2097152 | tf_op jit(solution)/shard_map/all_to_all | solution.py:217
  16.7 7.3 %collective-permute-start = (bf16[4,512,256]{2,1,0:T(8,128)(2,1)S(1)}, bf16[4,512,256]{2,1,0:T(8,128)(2,1)}, u32[]{:S(2)}, u32[]{:S(2)}) collective-permute-start(bf16[4,512,256]{2,1,0:T(8,128)(2,1)S(1)} %all_to_all.25.x_ref), channel_id=1, source_target_pairs={{0,1},{1,0},{2,3},{3,2},{4,5},{5,4},{6,7},{7,6},{8,9},{9,8},{10,11... | collective-permute-start | bytes 3145736 | tf_op jit(solution)/shard_map/ppermute | solution.py:212
  24.0 0.0 copy-done.1
  24.0 0.0 copy-done
  24.0 0.0 copy-done.3
  24.0 0.0 copy-done.7
  24.0 0.0 copy-start.4
  24.0 1.0 shard_map.64.held_ref
  25.0 1.3 %collective-permute-done.x_ref = bf16[4,512,256]{2,1,0:T(8,128)(2,1)} collective-permute-done((bf16[4,512,256]{2,1,0:T(8,128)(2,1)S(1)}, bf16[4,512,256]{2,1,0:T(8,128)(2,1)}, u32[]{:S(2)}, u32[]{:S(2)}) %collective-permute-start) | collective-permute-done | bytes 1048608 | tf_op jit(solution)/shard_map/ppermute | solution.py:212
  26.4 0.0 copy-done.4
  26.4 0.0 copy-start.2
  26.4 2.7 %shard_map.65 = (bf16[512,384]{1,0:T(8,128)(2,1)S(1)}, bf16[512,256]{1,0:T(8,128)(2,1)S(1)}, bf16[4,40,128]{2,1,0:T(8,128)(2,1)S(1)}) custom-call(s32[1]{0:T(128)} %bitcast.core_ref, bf16[4,512,256]{2,1,0:T(8,128)(2,1)} %collective-permute-done.x_ref, f32[1,2048]{1,0:T(1,128)S(1)} %bitcast.8, bf16[32,2048]{1,0:T(8,128)(2,1)S(1)} %bitcast.6, ...), custom_call_target="tpu_custom_call" | custom-call | tf_op jit(solution)/shard_map/pallas_call | solution.py:223
  29.0 0.0 copy-start.5
  29.1 0.7 copy-done.5
  29.8 0.0 copy-start.6
  29.8 8.3 %all_to_all.26.got_ref.after_ref = bf16[4,40,128]{2,1,0:T(8,128)(2,1)S(1)} all-to-all(bf16[4,40,128]{2,1,0:T(8,128)(2,1)S(1)} %get-tuple-element.14), channel_id=1, replica_groups={{0,8,16,24},{32,40,48,56},{64,72,80,88},{96,104,112,120},{128,136,144,1..., dimensions={0} | all-to-all | bytes 81920 | tf_op jit(solution)/shard_map/all_to_all | solution.py:228
  38.0 0.7 shard_map.66
  38.7 14.9 %all-to-all-start.2 = ((bf16[16,40,128]{2,1,0:T(8,128)(2,1)}), bf16[16,40,128]{2,1,0:T(8,128)(2,1)S(1)}, u32[]{:S(2)}, u32[]{:S(2)}) async-start(bf16[16,40,128]{2,1,0:T(8,128)(2,1)} %shard_map.66), calls=%async_computation.2 | async-start | bytes 327680 | tf_op jit(solution)/shard_map/all_to_all | solution.py:230
  53.6 2.2 %collective-permute-start.1 = (bf16[512,256]{1,0:T(8,128)(2,1)}, bf16[512,256]{1,0:T(8,128)(2,1)S(1)}, u32[]{:S(2)}, u32[]{:S(2)}) collective-permute-start(bf16[512,256]{1,0:T(8,128)(2,1)} %copy-done.5), channel_id=1, source_target_pairs={{0,8},{8,16},{16,24},{24,32},{32,40},{40,48},{48,56},{56,64},{64,7... | collective-permute-start | bytes 786440 | tf_op jit(solution)/shard_map/ppermute | solution.py:233
  55.8 0.0 copy-done.2
  55.9 0.1 shard_map.71
  55.9 4.3 %collective-permute-start.3 = (bf16[4,256,256]{2,1,0:T(8,128)(2,1)S(1)}, bf16[4,256,256]{2,1,0:T(8,128)(2,1)S(1)}, u32[]{:S(2)}, u32[]{:S(2)}) collective-permute-start(bf16[4,256,256]{2,1,0:T(8,128)(2,1)S(1)} %shard_map.71), channel_id=1, source_target_pairs={{0,1},{1,0},{2,3},{3,2},{4,5},{5,4},{6,7},{7,6},{8,9},{9,8},{10,11... | collective-permute-start | bytes 1572872 | tf_op jit(solution)/shard_map/ppermute | solution.py:212
  60.2 0.6 shard_map.68.num_ref
  60.8 5.0 %all-to-all-done.2.totals_ref = bf16[16,40,128]{2,1,0:T(8,128)(2,1)S(1)} async-done(((bf16[16,40,128]{2,1,0:T(8,128)(2,1)}), bf16[16,40,128]{2,1,0:T(8,128)(2,1)S(1)}, u32[]{:S(2)}, u32[]{:S(2)}) %all-to-all-start.2) | async-done | bytes 163872 | tf_op jit(solution)/shard_map/all_to_all | solution.py:230
  65.8 0.7 shard_map.67
  66.5 3.3 %all-to-all-start.3 = ((bf16[4,40,128]{2,1,0:T(8,128)(2,1)}), bf16[4,40,128]{2,1,0:T(8,128)(2,1)S(1)}, u32[]{:S(2)}, u32[]{:S(2)}) async-start(bf16[4,40,128]{2,1,0:T(8,128)(2,1)} %shard_map.67), calls=%async_computation.3 | async-start | bytes 81920 | tf_op jit(solution)/shard_map/all_to_all | solution.py:241
  69.7 0.0 collective-permute-done.1.prev_ref
  69.8 0.0 copy-done.6
  69.8 1.3 %shard_map.69.win_ref = bf16[512,128]{1,0:T(8,128)(2,1)S(1)} custom-call(s32[1]{0:T(128)} %bitcast.4.first_ref, bf16[512,384]{1,0:T(8,128)(2,1)S(1)} %get-tuple-element.12.pack_ref, bf16[512,256]{1,0:T(8,128)(2,1)S(1)} %copy-done.6, bf16[512,256]{1,0:T(8,128)(2,1)S(1)} %collective-permute-done.1.prev_ref), custom_call_target="tpu_custom_call" | custom-call | tf_op jit(solution)/shard_map/pallas_call | solution.py:236
  71.0 3.0 %all-to-all-done.3.prefix_ref = bf16[4,40,128]{2,1,0:T(8,128)(2,1)S(1)} async-done(((bf16[4,40,128]{2,1,0:T(8,128)(2,1)}), bf16[4,40,128]{2,1,0:T(8,128)(2,1)S(1)}, u32[]{:S(2)}, u32[]{:S(2)}) %all-to-all-start.3) | async-done | bytes 40992 | tf_op jit(solution)/shard_map/all_to_all | solution.py:241
  74.1 0.6 shard_map.70.mix_ref
  74.6 7.9 %collective-permute-start.2 = (bf16[512,256]{1,0:T(8,128)(2,1)S(1)}, bf16[512,256]{1,0:T(8,128)(2,1)S(1)}, u32[]{:S(2)}, u32[]{:S(2)}) collective-permute-start(bf16[512,256]{1,0:T(8,128)(2,1)S(1)} %shard_map.70.mix_ref), channel_id=1, source_target_pairs={{0,1},{1,0},{2,3},{3,2},{4,5},{5,4},{6,7},{7,6},{8,9},{9,8},{10,11... | collective-permute-start | bytes 786440 | tf_op jit(solution)/shard_map/ppermute | solution.py:212
  82.5 0.5 shard_map.72.own_ref
  83.0 0.0 collective-permute-done.3.w_ref
  83.0 0.7 collective-permute-done.2.mix_ref
  83.7 0.4 shard_map.73
  84.1 17.3 %all_to_all.27 = bf16[4,512,256]{2,1,0:T(8,128)(2,1)S(1)} all-to-all(bf16[4,512,256]{2,1,0:T(8,128)(2,1)S(1)} %shard_map.73), channel_id=1, replica_groups={{0,2,4,6},{1,3,5,7},{8,10,12,14},{9,11,13,15},{16,18,20,22},{17,19,21,2..., dimensions={0} | all-to-all | bytes 2097152 | tf_op jit(solution)/shard_map/all_to_all | solution.py:245
  101.4 0.9 reduce_sum.12
Async XLA Ops:
  0.0 24.0 %copy-start.1 = (bf16[2048,256]{1,0:T(8,128)(2,1)S(1)}, bf16[2048,256]{1,0:T(8,128)(2,1)}, u32[]{:S(2)}) copy-start(bf16[2048,256]{1,0:T(8,128)(2,1)} %ww_ref.3) | copy-start | bytes 3145732
  0.0 24.0 %copy-start = (bf16[2048,256]{1,0:T(8,128)(2,1)S(1)}, bf16[2048,256]{1,0:T(8,128)(2,1)}, u32[]{:S(2)}) copy-start(bf16[2048,256]{1,0:T(8,128)(2,1)} %wv_ref.3) | copy-start | bytes 3145732
  0.0 24.0 %copy-start.3 = (bf16[2048,32]{0,1:T(8,128)(2,1)S(1)}, bf16[2048,32]{0,1:T(8,128)(2,1)}, u32[]{:S(2)}) copy-start(bf16[2048,32]{0,1:T(8,128)(2,1)} %param.8) | copy-start | bytes 393220
  0.0 24.0 %copy-start.7 = (f32[2048]{0:T(1024)S(1)}, f32[2048]{0:T(1024)}, u32[]{:S(2)}) copy-start(f32[2048]{0:T(1024)} %param.7) | copy-start | bytes 24580
  16.7 9.7 %collective-permute-start = (bf16[4,512,256]{2,1,0:T(8,128)(2,1)S(1)}, bf16[4,512,256]{2,1,0:T(8,128)(2,1)}, u32[]{:S(2)}, u32[]{:S(2)}) collective-permute-start(bf16[4,512,256]{2,1,0:T(8,128)(2,1)S(1)} %all_to_all.25.x_ref), channel_id=1, source_target_pairs={{0,1},{1,0},{2,3},{3,2},{4,5},{5,4},{6,7},{7,6},{8,9},{9,8},{10,11... | collective-permute-start | bytes 3145736 | tf_op jit(solution)/shard_map/ppermute | solution.py:212
  24.0 2.3 %copy-start.4 = (bf16[2048,32]{0,1:T(8,128)(2,1)S(1)}, bf16[2048,32]{0,1:T(8,128)(2,1)}, u32[]{:S(2)}) copy-start(bf16[2048,32]{0,1:T(8,128)(2,1)} %param.8) | copy-start | bytes 393220
  26.4 29.5 %copy-start.2 = (bf16[256,2048]{1,0:T(8,128)(2,1)S(1)}, bf16[256,2048]{1,0:T(8,128)(2,1)}, u32[]{:S(2)}) copy-start(bf16[256,2048]{1,0:T(8,128)(2,1)} %w_ref.3) | copy-start | bytes 3145732
  29.0 0.7 copy-start.5
  29.8 40.0 %copy-start.6 = (bf16[512,256]{1,0:T(8,128)(2,1)S(1)}, bf16[512,256]{1,0:T(8,128)(2,1)}, u32[]{:S(2)}) copy-start(bf16[512,256]{1,0:T(8,128)(2,1)} %copy-done.5) | copy-start | bytes 786436
  38.7 27.1 %all-to-all-start.2 = ((bf16[16,40,128]{2,1,0:T(8,128)(2,1)}), bf16[16,40,128]{2,1,0:T(8,128)(2,1)S(1)}, u32[]{:S(2)}, u32[]{:S(2)}) async-start(bf16[16,40,128]{2,1,0:T(8,128)(2,1)} %shard_map.66), calls=%async_computation.2 | async-start | bytes 327680 | tf_op jit(solution)/shard_map/all_to_all | solution.py:230
  53.6 16.1 %collective-permute-start.1 = (bf16[512,256]{1,0:T(8,128)(2,1)}, bf16[512,256]{1,0:T(8,128)(2,1)S(1)}, u32[]{:S(2)}, u32[]{:S(2)}) collective-permute-start(bf16[512,256]{1,0:T(8,128)(2,1)} %copy-done.5), channel_id=1, source_target_pairs={{0,8},{8,16},{16,24},{24,32},{32,40},{40,48},{48,56},{56,64},{64,7... | collective-permute-start | bytes 786440 | tf_op jit(solution)/shard_map/ppermute | solution.py:233
  55.9 27.1 %collective-permute-start.3 = (bf16[4,256,256]{2,1,0:T(8,128)(2,1)S(1)}, bf16[4,256,256]{2,1,0:T(8,128)(2,1)S(1)}, u32[]{:S(2)}, u32[]{:S(2)}) collective-permute-start(bf16[4,256,256]{2,1,0:T(8,128)(2,1)S(1)} %shard_map.71), channel_id=1, source_target_pairs={{0,1},{1,0},{2,3},{3,2},{4,5},{5,4},{6,7},{7,6},{8,9},{9,8},{10,11... | collective-permute-start | bytes 1572872 | tf_op jit(solution)/shard_map/ppermute | solution.py:212
  66.5 7.6 %all-to-all-start.3 = ((bf16[4,40,128]{2,1,0:T(8,128)(2,1)}), bf16[4,40,128]{2,1,0:T(8,128)(2,1)S(1)}, u32[]{:S(2)}, u32[]{:S(2)}) async-start(bf16[4,40,128]{2,1,0:T(8,128)(2,1)} %shard_map.67), calls=%async_computation.3 | async-start | bytes 81920 | tf_op jit(solution)/shard_map/all_to_all | solution.py:241
  74.6 9.0 %collective-permute-start.2 = (bf16[512,256]{1,0:T(8,128)(2,1)S(1)}, bf16[512,256]{1,0:T(8,128)(2,1)S(1)}, u32[]{:S(2)}, u32[]{:S(2)}) collective-permute-start(bf16[512,256]{1,0:T(8,128)(2,1)S(1)} %shard_map.70.mix_ref), channel_id=1, source_target_pairs={{0,1},{1,0},{2,3},{3,2},{4,5},{5,4},{6,7},{7,6},{8,9},{9,8},{10,11... | collective-permute-start | bytes 786440 | tf_op jit(solution)/shard_map/ppermute | solution.py:212

commit v10 on v9

--- a/solution.py
+++ b/solution.py
@@ -226,13 +226,14 @@
     in_x = [[4 * z + x for x in range(4)] for z in range(16)]
     in_z = [[4 * z + x for z in range(16)] for x in range(4)]
     quarters = lax.all_to_all(states, "ctx", 0, 0, tiled=True, axis_index_groups=in_x)
-    rim, quarters = lax.optimization_barrier((rim, quarters))
     totals = lax.all_to_all(
         call(total_kernel, shape((16, QUARTER, 128)))(quarters), "ctx", 0, 0, tiled=True, axis_index_groups=in_z
     )
+    picked = call_with_scalar(pick_kernel, shape((4, 256, 256)), 2)(core, w_out, quarters)
+    w_other = across(picked)
+    numerator = call(inner_kernel, shape((count, 128), F32))(pack, picked)
+    rim, numerator = lax.optimization_barrier((rim, numerator))
     prev = lax.ppermute(rim, "ctx", [(b, b + 1) for b in range(63)])
-    numerator = call(inner_kernel, shape((count, 128), F32))(pack, quarters)
-    w_other = across(call_with_scalar(pick_kernel, shape((4, 256, 256)), 2)(core, w_out, quarters))
     win_out = call_with_scalar(attend_kernel, shape((count, 128)), 3)(ctx.astype(jnp.int32).reshape(1), pack, rim, prev)
     sums = call_with_scalar(prefix_kernel, shape((4, QUARTER, 128)), 2)(
         (ctx // 4).astype(jnp.int32).reshape(1), quarters, totals

time: 103 us -> 103 us (level)
  no operation moved by 1% of the time
where the time goes in v10:
time: 103 us; the launch traced here: 102 us
  blocking collectives  41 us (40%)
  starting transfers between devices  39.6 us (38%)
  waiting for transfers between devices  9.97 us (10%)
  Pallas kernels  8.46 us (8%)
  local copies, waits for them, and re-layouts  1.9 us (2%)
    ppermute x3, starting transfers between devices, across(): return lax.ppermute(value, 'head', [(h, h ^ 1) for h in range(8)])  19.2 us
    all_to_all x1, blocking collectives, shards(): lax.all_to_all(summed, 'head', 0, 0, tiled=True, axis_index_groups=along_y)  17.3 us
    all_to_all x1, blocking collectives, shards(): lax.all_to_all(jnp.broadcast_to(tokens[None], (4,) + tokens.shape), 'head...  15.5 us
    all_to_all x1, starting transfers between devices, shards(): lax.all_to_all(call(total_kernel, shape((16, QUARTER, 128)))(quarters), '...  14.9 us
    all_to_all x1, blocking collectives, shards(): lax.all_to_all(states, 'ctx', 0, 0, tiled=True, axis_index_groups=in_x)  8.28 us
    all_to_all x1, waiting for transfers between devices, shards(): lax.all_to_all(call(total_kernel, shape((16, QUARTER, 128)))(quarters), '...  4.95 us
    all_to_all x1, starting transfers between devices, shards(): lax.all_to_all(sums, 'ctx', 0, 0, tiled=True, axis_index_groups=in_x)  3.27 us
    all_to_all x1, waiting for transfers between devices, shards(): lax.all_to_all(sums, 'ctx', 0, 0, tiled=True, axis_index_groups=in_x)  3 us
  transfers between devices with their start and end apart: 6, of which 4 were waited for; matrix products, arithmetic and copies ran while one was open for 0% of the time, Pallas kernels for 5%

profile of v10, /device:TPU:1, one launch (start us, length us, event | category | flops | bytes accessed | tf_op | source)
XLA Modules:
  0.0 102.0 jit_solution(10141541136665762022)
XLA Ops:
  0.0 0.0 copy-start.1
  0.0 0.0 copy-start
  0.0 0.0 copy-start.3
  0.0 0.0 copy-start.7
  0.0 1.2 %broadcast_in_dim.2 = bf16[4,512,256]{2,1,0:T(8,128)(2,1)S(1)} broadcast(bf16[512,256]{1,0:T(8,128)(2,1)} %param.6), dimensions={1,2} | broadcast | bytes 1310720 | tf_op jit(solution)/shard_map/broadcast_in_dim | solution.py:218
  1.2 15.5 %all_to_all.25.x_ref = bf16[4,512,256]{2,1,0:T(8,128)(2,1)S(1)} all-to-all(bf16[4,512,256]{2,1,0:T(8,128)(2,1)S(1)} %broadcast_in_dim.2), channel_id=1, replica_groups={{0,2,4,6},{1,3,5,7},{8,10,12,14},{9,11,13,15},{16,18,20,22},{17,19,21,2..., dimensions={0} | all-to-all | bytes 2097152 | tf_op jit(solution)/shard_map/all_to_all | solution.py:217
  16.7 7.3 %collective-permute-start = (bf16[4,512,256]{2,1,0:T(8,128)(2,1)S(1)}, bf16[4,512,256]{2,1,0:T(8,128)(2,1)}, u32[]{:S(2)}, u32[]{:S(2)}) collective-permute-start(bf16[4,512,256]{2,1,0:T(8,128)(2,1)S(1)} %all_to_all.25.x_ref), channel_id=1, source_target_pairs={{0,1},{1,0},{2,3},{3,2},{4,5},{5,4},{6,7},{7,6},{8,9},{9,8},{10,11... | collective-permute-start | bytes 3145736 | tf_op jit(solution)/shard_map/ppermute | solution.py:212
  24.0 0.0 copy-done.1
  24.0 0.0 copy-done
  24.0 0.0 copy-done.3
  24.0 0.0 copy-done.7
  24.0 0.0 copy-start.4
  24.0 1.0 shard_map.64.held_ref
  25.0 1.3 %collective-permute-done.x_ref = bf16[4,512,256]{2,1,0:T(8,128)(2,1)} collective-permute-done((bf16[4,512,256]{2,1,0:T(8,128)(2,1)S(1)}, bf16[4,512,256]{2,1,0:T(8,128)(2,1)}, u32[]{:S(2)}, u32[]{:S(2)}) %collective-permute-start) | collective-permute-done | bytes 1048608 | tf_op jit(solution)/shard_map/ppermute | solution.py:212
  26.4 0.0 copy-done.4
  26.4 0.0 copy-start.2
  26.4 2.7 %shard_map.65 = (bf16[512,384]{1,0:T(8,128)(2,1)S(1)}, bf16[512,256]{1,0:T(8,128)(2,1)S(1)}, bf16[4,40,128]{2,1,0:T(8,128)(2,1)S(1)}) custom-call(s32[1]{0:T(128)} %bitcast.core_ref, bf16[4,512,256]{2,1,0:T(8,128)(2,1)} %collective-permute-done.x_ref, f32[1,2048]{1,0:T(1,128)S(1)} %bitcast.8, bf16[32,2048]{1,0:T(8,128)(2,1)S(1)} %bitcast.6, ...), custom_call_target="tpu_custom_call" | custom-call | tf_op jit(solution)/shard_map/pallas_call | solution.py:223
  29.0 0.0 copy-start.5
  29.1 0.7 copy-done.5
  29.8 0.0 copy-start.6
  29.8 8.3 %all_to_all.26.got_ref.after_ref = bf16[4,40,128]{2,1,0:T(8,128)(2,1)S(1)} all-to-all(bf16[4,40,128]{2,1,0:T(8,128)(2,1)S(1)} %get-tuple-element.13), channel_id=1, replica_groups={{0,8,16,24},{32,40,48,56},{64,72,80,88},{96,104,112,120},{128,136,144,1..., dimensions={0} | all-to-all | bytes 81920 | tf_op jit(solution)/shard_map/all_to_all | solution.py:228
  38.0 0.7 shard_map.66
  38.7 14.9 %all-to-all-start.2 = ((bf16[16,40,128]{2,1,0:T(8,128)(2,1)}), bf16[16,40,128]{2,1,0:T(8,128)(2,1)S(1)}, u32[]{:S(2)}, u32[]{:S(2)}) async-start(bf16[16,40,128]{2,1,0:T(8,128)(2,1)} %shard_map.66), calls=%async_computation.2 | async-start | bytes 327680 | tf_op jit(solution)/shard_map/all_to_all | solution.py:229
  53.6 0.0 copy-done.2
  53.6 0.1 shard_map.68.after_ref
  53.7 0.6 shard_map.69.num_ref
  54.3 0.0 copy-done.6
  54.4 2.2 %collective-permute-start.1 = (bf16[512,256]{1,0:T(8,128)(2,1)S(1)}, bf16[512,256]{1,0:T(8,128)(2,1)S(1)}, u32[]{:S(2)}, u32[]{:S(2)}) collective-permute-start(bf16[512,256]{1,0:T(8,128)(2,1)S(1)} %copy-done.6), channel_id=1, source_target_pairs={{0,8},{8,16},{16,24},{24,32},{32,40},{40,48},{48,56},{56,64},{64,7... | collective-permute-start | bytes 786440 | tf_op jit(solution)/shard_map/ppermute | solution.py:236
  56.6 4.3 %collective-permute-start.3 = (bf16[4,256,256]{2,1,0:T(8,128)(2,1)S(1)}, bf16[4,256,256]{2,1,0:T(8,128)(2,1)S(1)}, u32[]{:S(2)}, u32[]{:S(2)}) collective-permute-start(bf16[4,256,256]{2,1,0:T(8,128)(2,1)S(1)} %shard_map.68.after_ref), channel_id=1, source_target_pairs={{0,1},{1,0},{2,3},{3,2},{4,5},{5,4},{6,7},{7,6},{8,9},{9,8},{10,11... | collective-permute-start | bytes 1572872 | tf_op jit(solution)/shard_map/ppermute | solution.py:212
  60.9 5.0 %all-to-all-done.2.totals_ref = bf16[16,40,128]{2,1,0:T(8,128)(2,1)S(1)} async-done(((bf16[16,40,128]{2,1,0:T(8,128)(2,1)}), bf16[16,40,128]{2,1,0:T(8,128)(2,1)S(1)}, u32[]{:S(2)}, u32[]{:S(2)}) %all-to-all-start.2) | async-done | bytes 163872 | tf_op jit(solution)/shard_map/all_to_all | solution.py:229
  65.8 0.7 shard_map.67
  66.5 3.3 %all-to-all-start.3 = ((bf16[4,40,128]{2,1,0:T(8,128)(2,1)}), bf16[4,40,128]{2,1,0:T(8,128)(2,1)S(1)}, u32[]{:S(2)}, u32[]{:S(2)}) async-start(bf16[4,40,128]{2,1,0:T(8,128)(2,1)} %shard_map.67), calls=%async_computation.3 | async-start | bytes 81920 | tf_op jit(solution)/shard_map/all_to_all | solution.py:242
  69.8 0.0 collective-permute-done.1.prev_ref
  69.8 1.3 %shard_map.70.win_ref = bf16[512,128]{1,0:T(8,128)(2,1)S(1)} custom-call(s32[1]{0:T(128)} %bitcast.4.first_ref, bf16[512,384]{1,0:T(8,128)(2,1)S(1)} %get-tuple-element.12.pack_ref, bf16[512,256]{1,0:T(8,128)(2,1)S(1)} %copy-done.6, bf16[512,256]{1,0:T(8,128)(2,1)S(1)} %collective-permute-done.1.prev_ref), custom_call_target="tpu_custom_call" | custom-call | tf_op jit(solution)/shard_map/pallas_call | solution.py:237
  71.1 3.0 %all-to-all-done.3.prefix_ref = bf16[4,40,128]{2,1,0:T(8,128)(2,1)S(1)} async-done(((bf16[4,40,128]{2,1,0:T(8,128)(2,1)}), bf16[4,40,128]{2,1,0:T(8,128)(2,1)S(1)}, u32[]{:S(2)}, u32[]{:S(2)}) %all-to-all-start.3) | async-done | bytes 40992 | tf_op jit(solution)/shard_map/all_to_all | solution.py:242
  74.1 0.6 shard_map.71.mix_ref
  74.6 7.6 %collective-permute-start.2 = (bf16[512,256]{1,0:T(8,128)(2,1)S(1)}, bf16[512,256]{1,0:T(8,128)(2,1)S(1)}, u32[]{:S(2)}, u32[]{:S(2)}) collective-permute-start(bf16[512,256]{1,0:T(8,128)(2,1)S(1)} %shard_map.71.mix_ref), channel_id=1, source_target_pairs={{0,1},{1,0},{2,3},{3,2},{4,5},{5,4},{6,7},{7,6},{8,9},{9,8},{10,11... | collective-permute-start | bytes 786440 | tf_op jit(solution)/shard_map/ppermute | solution.py:212
  82.3 0.5 shard_map.72.own_ref
  82.7 0.0 collective-permute-done.3.w_ref
  82.7 0.7 collective-permute-done.2.mix_ref
  83.4 0.4 shard_map.73
  83.9 17.3 %all_to_all.27 = bf16[4,512,256]{2,1,0:T(8,128)(2,1)S(1)} all-to-all(bf16[4,512,256]{2,1,0:T(8,128)(2,1)S(1)} %shard_map.73), channel_id=1, replica_groups={{0,2,4,6},{1,3,5,7},{8,10,12,14},{9,11,13,15},{16,18,20,22},{17,19,21,2..., dimensions={0} | all-to-all | bytes 2097152 | tf_op jit(solution)/shard_map/all_to_all | solution.py:246
  101.1 0.9 reduce_sum.12
Async XLA Ops:
  0.0 24.0 %copy-start.1 = (bf16[2048,256]{1,0:T(8,128)(2,1)S(1)}, bf16[2048,256]{1,0:T(8,128)(2,1)}, u32[]{:S(2)}) copy-start(bf16[2048,256]{1,0:T(8,128)(2,1)} %ww_ref.3) | copy-start | bytes 3145732
  0.0 24.0 %copy-start = (bf16[2048,256]{1,0:T(8,128)(2,1)S(1)}, bf16[2048,256]{1,0:T(8,128)(2,1)}, u32[]{:S(2)}) copy-start(bf16[2048,256]{1,0:T(8,128)(2,1)} %wv_ref.3) | copy-start | bytes 3145732
  0.0 24.0 %copy-start.3 = (bf16[2048,32]{0,1:T(8,128)(2,1)S(1)}, bf16[2048,32]{0,1:T(8,128)(2,1)}, u32[]{:S(2)}) copy-start(bf16[2048,32]{0,1:T(8,128)(2,1)} %param.8) | copy-start | bytes 393220
  0.0 24.0 %copy-start.7 = (f32[2048]{0:T(1024)S(1)}, f32[2048]{0:T(1024)}, u32[]{:S(2)}) copy-start(f32[2048]{0:T(1024)} %param.7) | copy-start | bytes 24580
  16.7 9.7 %collective-permute-start = (bf16[4,512,256]{2,1,0:T(8,128)(2,1)S(1)}, bf16[4,512,256]{2,1,0:T(8,128)(2,1)}, u32[]{:S(2)}, u32[]{:S(2)}) collective-permute-start(bf16[4,512,256]{2,1,0:T(8,128)(2,1)S(1)} %all_to_all.25.x_ref), channel_id=1, source_target_pairs={{0,1},{1,0},{2,3},{3,2},{4,5},{5,4},{6,7},{7,6},{8,9},{9,8},{10,11... | collective-permute-start | bytes 3145736 | tf_op jit(solution)/shard_map/ppermute | solution.py:212
  24.0 2.3 %copy-start.4 = (bf16[2048,32]{0,1:T(8,128)(2,1)S(1)}, bf16[2048,32]{0,1:T(8,128)(2,1)}, u32[]{:S(2)}) copy-start(bf16[2048,32]{0,1:T(8,128)(2,1)} %param.8) | copy-start | bytes 393220
  26.4 27.3 %copy-start.2 = (bf16[256,2048]{1,0:T(8,128)(2,1)S(1)}, bf16[256,2048]{1,0:T(8,128)(2,1)}, u32[]{:S(2)}) copy-start(bf16[256,2048]{1,0:T(8,128)(2,1)} %w_ref.3) | copy-start | bytes 3145732
  29.0 0.7 copy-start.5
  29.8 24.6 %copy-start.6 = (bf16[512,256]{1,0:T(8,128)(2,1)S(1)}, bf16[512,256]{1,0:T(8,128)(2,1)}, u32[]{:S(2)}) copy-start(bf16[512,256]{1,0:T(8,128)(2,1)} %copy-done.5) | copy-start | bytes 786436
  38.7 27.1 %all-to-all-start.2 = ((bf16[16,40,128]{2,1,0:T(8,128)(2,1)}), bf16[16,40,128]{2,1,0:T(8,128)(2,1)S(1)}, u32[]{:S(2)}, u32[]{:S(2)}) async-start(bf16[16,40,128]{2,1,0:T(8,128)(2,1)} %shard_map.66), calls=%async_computation.2 | async-start | bytes 327680 | tf_op jit(solution)/shard_map/all_to_all | solution.py:229
  54.4 15.4 %collective-permute-start.1 = (bf16[512,256]{1,0:T(8,128)(2,1)S(1)}, bf16[512,256]{1,0:T(8,128)(2,1)S(1)}, u32[]{:S(2)}, u32[]{:S(2)}) collective-permute-start(bf16[512,256]{1,0:T(8,128)(2,1)S(1)} %copy-done.6), channel_id=1, source_target_pairs={{0,8},{8,16},{16,24},{24,32},{32,40},{40,48},{48,56},{56,64},{64,7... | collective-permute-start | bytes 786440 | tf_op jit(solution)/shard_map/ppermute | solution.py:236
  56.6 26.2 %collective-permute-start.3 = (bf16[4,256,256]{2,1,0:T(8,128)(2,1)S(1)}, bf16[4,256,256]{2,1,0:T(8,128)(2,1)S(1)}, u32[]{:S(2)}, u32[]{:S(2)}) collective-permute-start(bf16[4,256,256]{2,1,0:T(8,128)(2,1)S(1)} %shard_map.68.after_ref), channel_id=1, source_target_pairs={{0,1},{1,0},{2,3},{3,2},{4,5},{5,4},{6,7},{7,6},{8,9},{9,8},{10,11... | collective-permute-start | bytes 1572872 | tf_op jit(solution)/shard_map/ppermute | solution.py:212
  66.5 7.6 %all-to-all-start.3 = ((bf16[4,40,128]{2,1,0:T(8,128)(2,1)}), bf16[4,40,128]{2,1,0:T(8,128)(2,1)S(1)}, u32[]{:S(2)}, u32[]{:S(2)}) async-start(bf16[4,40,128]{2,1,0:T(8,128)(2,1)} %shard_map.67), calls=%async_computation.3 | async-start | bytes 81920 | tf_op jit(solution)/shard_map/all_to_all | solution.py:242
  74.6 8.8 %collective-permute-start.2 = (bf16[512,256]{1,0:T(8,128)(2,1)S(1)}, bf16[512,256]{1,0:T(8,128)(2,1)S(1)}, u32[]{:S(2)}, u32[]{:S(2)}) collective-permute-start(bf16[512,256]{1,0:T(8,128)(2,1)S(1)} %shard_map.71.mix_ref), channel_id=1, source_target_pairs={{0,1},{1,0},{2,3},{3,2},{4,5},{5,4},{6,7},{7,6},{8,9},{9,8},{10,11... | collective-permute-start | bytes 786440 | tf_op jit(solution)/shard_map/ppermute | solution.py:212

commit v11 on v9

--- a/solution.py
+++ b/solution.py
@@ -26,11 +26,11 @@
     )
 
 
-def call_with_scalar(kernel, outs, count):
+def call_with_scalar(kernel, outs, count, scalars=1):
     return pl.pallas_call(
         kernel,
         out_shape=outs,
-        in_specs=[pl.BlockSpec(memory_space=pltpu.SMEM)] + [pl.BlockSpec(memory_space=pltpu.VMEM)] * count,
+        in_specs=[pl.BlockSpec(memory_space=pltpu.SMEM)] * scalars + [pl.BlockSpec(memory_space=pltpu.VMEM)] * count,
         compiler_params=pltpu.CompilerParams(vmem_limit_bytes=VMEM),
     )
 
@@ -73,11 +73,11 @@
     return lax.dot_general(a, b, dims, preferred_element_type=F32)
 
 
-def gather_products(flip, core_ref, x_ref, gain_ref, wf_ref, wv_ref, ww_ref):
+def gather_products(flip, core_ref, y_ref, blocks, gain_ref, wf_ref, wv_ref, ww_ref):
     squares = feats = values = windowed = 0.0
-    for y in range(4):
-        at = pl.multiple_of((2 * y + (core_ref[0] + flip) % 2) * 256, 256)
-        x = x_ref[y, :, :].astype(F32)
+    for back, x_ref in enumerate(blocks):
+        at = pl.multiple_of((2 * ((y_ref[0] + 4 - back) % 4) + (core_ref[0] + flip) % 2) * 256, 256)
+        x = x_ref[...].astype(F32)
         squares = squares + x * x
         scaled = (x * gain_ref[0:1, pl.ds(at, 256)]).astype(BF)
         feats = feats + dot(scaled, wf_ref[:, pl.ds(at, 256)], NT)
@@ -86,17 +86,26 @@
     return jnp.sum(squares, axis=1, keepdims=True), feats, values, windowed
 
 
-def begin_kernel(core_ref, x_ref, gain_ref, wf_ref, wv_ref, ww_ref, held_ref):
-    squares, feats, values, windowed = gather_products(0, core_ref, x_ref, gain_ref, wf_ref, wv_ref, ww_ref)
+def hold_kernel(core_ref, y_ref, gain_ref, wf_ref, wv_ref, ww_ref, gain_out, wf_out, wv_out, ww_out):
+    gain_out[...] = gain_ref[...]
+    wf_out[...] = wf_ref[...]
+    wv_out[...] = wv_ref[...]
+    ww_out[...] = ww_ref[...]
+
+
+def begin_kernel(core_ref, y_ref, b0, b1, b2, b3, gain_ref, wf_ref, wv_ref, ww_ref, held_ref):
+    squares, feats, values, windowed = gather_products(0, core_ref, y_ref, (b0, b1, b2, b3), gain_ref, wf_ref, wv_ref, ww_ref)
     held_ref[:, :256] = values
     held_ref[:, 256:512] = windowed
     held_ref[:, 512:544] = feats
     held_ref[:, 544:] = jnp.broadcast_to(squares, (squares.shape[0], 96))
 
 
-def project_kernel(core_ref, x_ref, gain_ref, wf_ref, wv_ref, ww_ref, held_ref, pack_ref, rim_ref, state_ref):
-    count = x_ref.shape[1]
-    squares, feats, values, windowed = gather_products(1, core_ref, x_ref, gain_ref, wf_ref, wv_ref, ww_ref)
+def project_kernel(
+    core_ref, y_ref, b0, b1, b2, b3, gain_ref, wf_ref, wv_ref, ww_ref, held_ref, pack_ref, rim_ref, state_ref
+):
+    count = b0.shape[0]
+    squares, feats, values, windowed = gather_products(1, core_ref, y_ref, (b0, b1, b2, b3), gain_ref, wf_ref, wv_ref, ww_ref)
     scale = lax.rsqrt((squares + held_ref[:, 544:545]) * (1.0 / 2048.0) + EPS)
     values = ((values + held_ref[:, :256]) * scale).astype(BF)
     windowed = ((windowed + held_ref[:, 256:512]) * scale).astype(BF)
@@ -214,15 +223,23 @@
     def shape(dims, kind=BF):
         return jax.ShapeDtypeStruct(dims, kind)
 
-    spread = lax.all_to_all(
-        jnp.broadcast_to(tokens[None], (4,) + tokens.shape), "head", 0, 0, tiled=True, axis_index_groups=along_y
-    )
-    other = across(spread)
-    weights = (gain.reshape(1, -1), w_feat.T, w_value, w_window)
-    held = call_with_scalar(begin_kernel, shape((count, 640), F32), 5)(core, spread, *weights)
+    near = [tokens] + [
+        lax.ppermute(tokens, "head", [(h, (h + 2 * k) % 8) for h in range(8)]) for k in (1, 2, 3)
+    ]
+    far = [across(near[0]), across(near[1]), None, across(near[3])]
+    row = (head // 2).astype(jnp.int32).reshape(1)
+    weights = call_with_scalar(
+        hold_kernel,
+        [shape((1, 2048), F32), shape(w_feat.shape[::-1]), shape(w_value.shape), shape(w_window.shape)],
+        4,
+        2,
+    )(core, row, gain.reshape(1, -1), w_feat.T, w_value, w_window)
+    near[2], far[1], far[3], *weights = lax.optimization_barrier((near[2], far[1], far[3], *weights))
+    far[2] = across(near[2])
+    held = call_with_scalar(begin_kernel, shape((count, 640), F32), 8, 2)(core, row, *near, *weights)
     pack, rim, states = call_with_scalar(
-        project_kernel, [shape((count, 384)), shape((count, 256)), shape((4, QUARTER, 128))], 6
-    )(core, other, *weights, held)
+        project_kernel, [shape((count, 384)), shape((count, 256)), shape((4, QUARTER, 128))], 9, 2
+    )(core, row, *far, *weights, held)
     in_x = [[4 * z + x for x in range(4)] for z in range(16)]
     in_z = [[4 * z + x for z in range(16)] for x in range(4)]
     quarters = lax.all_to_all(states, "ctx", 0, 0, tiled=True, axis_index_groups=in_x)

time: 103 us -> 107 us (1.039)
  starting transfers between devices: 39.8 us -> 56.4 us
  blocking collectives: 41 us -> 28.8 us
  local copies, waits for them, and re-layouts: 1.9 us -> 4.05 us
  waiting for transfers between devices: 9.98 us -> 8.83 us
  Pallas kernels: 8.44 us -> 7.34 us
    all_to_all x1 -> x0, blocking collectives: 15.5 us -> none  [shards(): lax.all_to_all(jnp.broadcast_to(tokens[None], (4,) + tokens.shape), 'head...]
    ppermute x0 -> x3, starting transfers between devices: none -> 10.9 us  [shards(): lax.ppermute(tokens, 'head', [(h, (h + 2 * k) % 8) for h in range(8)])]
    ppermute x3 -> x6, starting transfers between devices: 19.5 us -> 29 us  [across(): return lax.ppermute(value, 'head', [(h, h ^ 1) for h in range(8)])]
    all_to_all x1, blocking collectives: 17.3 us -> 22.1 us  [shards(): lax.all_to_all(summed, 'head', 0, 0, tiled=True, axis_index_groups=along_y)]
    all_to_all x1, starting transfers between devices: 14.9 us -> 11 us  [shards(): lax.all_to_all(call(total_kernel, shape((16, QUARTER, 128)))(quarters), '...]
    unnamed x16 -> x12, local copies, waits for them, and re-layouts: 0.73 us -> 4.05 us
    all_to_all x1, blocking collectives: 8.28 us -> 6.7 us  [shards(): lax.all_to_all(states, 'ctx', 0, 0, tiled=True, axis_index_groups=in_x)]
    pallas_call x1, Pallas kernels: 2.67 us -> 1.38 us  [shards(): call_with_scalar(project_kernel, [shape((count, 384)), shape((count, 256)...]
  transfers between devices with their start and end apart: 6 -> 12, of which waited for: 4 -> 4; matrix products, arithmetic and copies ran while one was open for 0% -> 0% of each run, Pallas kernels for 5% -> 5%
where the time goes in v11:
time: 107 us
  starting transfers between devices  56.4 us (53%)
  blocking collectives  28.8 us (27%)
  waiting for transfers between devices  8.83 us (8%)
  Pallas kernels  7.34 us (7%)
  local copies, waits for them, and re-layouts  4.05 us (4%)
    ppermute x6, starting transfers between devices, across(): return lax.ppermute(value, 'head', [(h, h ^ 1) for h in range(8)])  29 us
    all_to_all x1, blocking collectives, shards(): lax.all_to_all(summed, 'head', 0, 0, tiled=True, axis_index_groups=along_y)  22.1 us
    all_to_all x1, starting transfers between devices, shards(): lax.all_to_all(call(total_kernel, shape((16, QUARTER, 128)))(quarters), '...  11 us
    ppermute x3, starting transfers between devices, shards(): lax.ppermute(tokens, 'head', [(h, (h + 2 * k) % 8) for h in range(8)])  10.9 us
    all_to_all x1, blocking collectives, shards(): lax.all_to_all(states, 'ctx', 0, 0, tiled=True, axis_index_groups=in_x)  6.7 us
    all_to_all x1, waiting for transfers between devices, shards(): lax.all_to_all(call(total_kernel, shape((16, QUARTER, 128)))(quarters), '...  4.95 us
    unnamed x12, local copies, waits for them, and re-layouts  4.05 us
    all_to_all x1, starting transfers between devices, shards(): lax.all_to_all(sums, 'ctx', 0, 0, tiled=True, axis_index_groups=in_x)  3.27 us
  transfers between devices with their start and end apart: 12, of which 4 were waited for; matrix products, arithmetic and copies ran while one was open for 0% of the time, Pallas kernels for 5%

profile of v11, /device:TPU:1, one launch (start us, length us, event | category | flops | bytes accessed | tf_op | source)
XLA Modules:
  0.0 106.6 jit_solution(6246905915521394972)
XLA Ops:
  0.0 4.0 %collective-permute-start.2 = (bf16[512,256]{1,0:T(8,128)(2,1)}, bf16[512,256]{1,0:T(8,128)(2,1)S(1)}, u32[]{:S(2)}, u32[]{:S(2)}) collective-permute-start(bf16[512,256]{1,0:T(8,128)(2,1)} %b0.1), channel_id=1, source_target_pairs={{0,2},{1,3},{2,4},{3,5},{4,6},{5,7},{6,0},{7,1},{8,10},{9,11},{10,... | collective-permute-start | bytes 786440 | tf_op jit(solution)/shard_map/ppermute | solution.py:227
  4.0 3.4 %collective-permute-start.4 = (bf16[512,256]{1,0:T(8,128)(2,1)}, bf16[512,256]{1,0:T(8,128)(2,1)S(1)}, u32[]{:S(2)}, u32[]{:S(2)}) collective-permute-start(bf16[512,256]{1,0:T(8,128)(2,1)} %b0.1), channel_id=1, source_target_pairs={{0,6},{1,7},{2,0},{3,1},{4,2},{5,3},{6,4},{7,5},{8,14},{9,15},{10,... | collective-permute-start | bytes 786440 | tf_op jit(solution)/shard_map/ppermute | solution.py:227
  7.4 3.5 %collective-permute-start.1 = (bf16[512,256]{1,0:T(8,128)(2,1)}, bf16[512,256]{1,0:T(8,128)(2,1)S(1)}, u32[]{:S(2)}, u32[]{:S(2)}) collective-permute-start(bf16[512,256]{1,0:T(8,128)(2,1)} %b0.1), channel_id=1, source_target_pairs={{0,4},{1,5},{2,6},{3,7},{4,0},{5,1},{6,2},{7,3},{8,12},{9,13},{10,... | collective-permute-start | bytes 786440 | tf_op jit(solution)/shard_map/ppermute | solution.py:227
  10.9 0.0 collective-permute-done.2.b1
  11.0 10.3 %collective-permute-start.3 = (bf16[512,256]{1,0:T(8,128)(2,1)S(1)}, bf16[512,256]{1,0:T(8,128)(2,1)S(1)}, u32[]{:S(2)}, u32[]{:S(2)}) collective-permute-start(bf16[512,256]{1,0:T(8,128)(2,1)S(1)} %collective-permute-done.2.b1), channel_id=1, source_target_pairs={{0,1},{1,0},{2,3},{3,2},{4,5},{5,4},{6,7},{7,6},{8,9},{9,8},{10,11... | collective-permute-start | bytes 786440 | tf_op jit(solution)/shard_map/ppermute | solution.py:221
  21.3 0.0 collective-permute-done.4.b3
  21.3 2.2 %collective-permute-start.5 = (bf16[512,256]{1,0:T(8,128)(2,1)S(1)}, bf16[512,256]{1,0:T(8,128)(2,1)S(1)}, u32[]{:S(2)}, u32[]{:S(2)}) collective-permute-start(bf16[512,256]{1,0:T(8,128)(2,1)S(1)} %collective-permute-done.4.b3), channel_id=1, source_target_pairs={{0,1},{1,0},{2,3},{3,2},{4,5},{5,4},{6,7},{7,6},{8,9},{9,8},{10,11... | collective-permute-start | bytes 786440 | tf_op jit(solution)/shard_map/ppermute | solution.py:221
  23.5 2.1 %collective-permute-start = (bf16[512,256]{1,0:T(8,128)(2,1)}, bf16[512,256]{1,0:T(8,128)(2,1)S(1)}, u32[]{:S(2)}, u32[]{:S(2)}) collective-permute-start(bf16[512,256]{1,0:T(8,128)(2,1)} %b0.1), channel_id=1, source_target_pairs={{0,1},{1,0},{2,3},{3,2},{4,5},{5,4},{6,7},{7,6},{8,9},{9,8},{10,11... | collective-permute-start | bytes 786440 | tf_op jit(solution)/shard_map/ppermute | solution.py:221
  25.6 0.0 copy-start.1
  25.7 1.2 %copy-done.1 = bf16[2048,256]{1,0:T(8,128)(2,1)S(1)} copy-done((bf16[2048,256]{1,0:T(8,128)(2,1)S(1)}, bf16[2048,256]{1,0:T(8,128)(2,1)}, u32[]{:S(2)}) %copy-start.1) | copy-done | bytes 1048600
  26.9 0.0 copy-start.2
  26.9 1.2 %copy-done.2 = bf16[2048,256]{1,0:T(8,128)(2,1)S(1)} copy-done((bf16[2048,256]{1,0:T(8,128)(2,1)S(1)}, bf16[2048,256]{1,0:T(8,128)(2,1)}, u32[]{:S(2)}) %copy-start.2) | copy-done | bytes 1048600
  28.1 0.0 copy-start.4
  28.1 0.9 copy-done.4
  29.0 0.7 copy-done.5
  29.7 0.1 shard_map.64
  29.8 0.0 collective-permute-done.1.b2
  29.9 0.0 collective-permute-done.3.b1
  29.9 0.0 collective-permute-done.5.b3
  29.9 2.2 %collective-permute-start.6 = (bf16[512,256]{1,0:T(8,128)(2,1)S(1)}, bf16[512,256]{1,0:T(8,128)(2,1)S(1)}, u32[]{:S(2)}, u32[]{:S(2)}) collective-permute-start(bf16[512,256]{1,0:T(8,128)(2,1)S(1)} %collective-permute-done.1.b2), channel_id=1, source_target_pairs={{0,1},{1,0},{2,3},{3,2},{4,5},{5,4},{6,7},{7,6},{8,9},{9,8},{10,11... | collective-permute-start | bytes 786440 | tf_op jit(solution)/shard_map/ppermute | solution.py:221
  32.1 0.0 copy-done.3
  32.1 1.0 shard_map.65.held_ref
  33.1 0.0 copy-start
  33.1 0.0 collective-permute-done.b0
  33.1 0.2 collective-permute-done.6.b2
  33.3 1.4 %shard_map.66 = (bf16[512,384]{1,0:T(8,128)(2,1)S(1)}, bf16[512,256]{1,0:T(8,128)(2,1)S(1)}, bf16[4,40,128]{2,1,0:T(8,128)(2,1)S(1)}) custom-call(s32[1]{0:T(128)} %bitcast.core_ref, s32[1]{0:T(128)} %bitcast.1.y_ref, bf16[512,256]{1,0:T(8,128)(2,1)S(1)} %collective-permute-done.b0, bf16[512,256]{1,0:T(8,128)(2,1)S(1)} %collective-permute-done.3.b1, ...), custom_call_target="tpu_custom_call" | custom-call | tf_op jit(solution)/shard_map/pallas_call | solution.py:240
  34.7 6.7 %all_to_all.20.got_ref.after_ref = bf16[4,40,128]{2,1,0:T(8,128)(2,1)S(1)} all-to-all(bf16[4,40,128]{2,1,0:T(8,128)(2,1)S(1)} %get-tuple-element.36), channel_id=1, replica_groups={{0,8,16,24},{32,40,48,56},{64,72,80,88},{96,104,112,120},{128,136,144,1..., dimensions={0} | all-to-all | bytes 81920 | tf_op jit(solution)/shard_map/all_to_all | solution.py:245
  41.4 0.7 shard_map.67
  42.1 11.0 %all-to-all-start.1 = ((bf16[16,40,128]{2,1,0:T(8,128)(2,1)}), bf16[16,40,128]{2,1,0:T(8,128)(2,1)S(1)}, u32[]{:S(2)}, u32[]{:S(2)}) async-start(bf16[16,40,128]{2,1,0:T(8,128)(2,1)} %shard_map.67), calls=%async_computation.1 | async-start | bytes 327680 | tf_op jit(solution)/shard_map/all_to_all | solution.py:247
  53.1 2.2 %collective-permute-start.7 = (bf16[512,256]{1,0:T(8,128)(2,1)S(1)}, bf16[512,256]{1,0:T(8,128)(2,1)S(1)}, u32[]{:S(2)}, u32[]{:S(2)}) collective-permute-start(bf16[512,256]{1,0:T(8,128)(2,1)S(1)} %get-tuple-element.40.own_ref), channel_id=1, source_target_pairs={{0,8},{8,16},{16,24},{24,32},{32,40},{40,48},{48,56},{56,64},{64,7... | collective-permute-start | bytes 786440 | tf_op jit(solution)/shard_map/ppermute | solution.py:250
  55.3 0.0 copy-done
  55.3 0.1 shard_map.72
  55.4 4.3 %collective-permute-start.9 = (bf16[4,256,256]{2,1,0:T(8,128)(2,1)S(1)}, bf16[4,256,256]{2,1,0:T(8,128)(2,1)S(1)}, u32[]{:S(2)}, u32[]{:S(2)}) collective-permute-start(bf16[4,256,256]{2,1,0:T(8,128)(2,1)S(1)} %shard_map.72), channel_id=1, source_target_pairs={{0,1},{1,0},{2,3},{3,2},{4,5},{5,4},{6,7},{7,6},{8,9},{9,8},{10,11... | collective-permute-start | bytes 1572872 | tf_op jit(solution)/shard_map/ppermute | solution.py:221
  59.7 0.6 shard_map.69.num_ref
  60.3 5.0 %all-to-all-done.1.totals_ref = bf16[16,40,128]{2,1,0:T(8,128)(2,1)S(1)} async-done(((bf16[16,40,128]{2,1,0:T(8,128)(2,1)}), bf16[16,40,128]{2,1,0:T(8,128)(2,1)S(1)}, u32[]{:S(2)}, u32[]{:S(2)}) %all-to-all-start.1) | async-done | bytes 163872 | tf_op jit(solution)/shard_map/all_to_all | solution.py:247
  65.3 0.7 shard_map.68
  66.0 3.3 %all-to-all-start.2 = ((bf16[4,40,128]{2,1,0:T(8,128)(2,1)}), bf16[4,40,128]{2,1,0:T(8,128)(2,1)S(1)}, u32[]{:S(2)}, u32[]{:S(2)}) async-start(bf16[4,40,128]{2,1,0:T(8,128)(2,1)} %shard_map.68), calls=%async_computation.2 | async-start | bytes 81920 | tf_op jit(solution)/shard_map/all_to_all | solution.py:258
  69.2 0.0 collective-permute-done.7.prev_ref
  69.2 1.3 %shard_map.70.win_ref = bf16[512,128]{1,0:T(8,128)(2,1)S(1)} custom-call(s32[1]{0:T(128)} %bitcast.5.first_ref, bf16[512,384]{1,0:T(8,128)(2,1)S(1)} %get-tuple-element.34.pack_ref, bf16[512,256]{1,0:T(8,128)(2,1)S(1)} %get-tuple-element.40.own_ref, bf16[512,256]{1,0:T(8,128)(2,1)S(1)} %collective-permute-done.7.prev_ref), custom_call_target="tpu_custom_call" | custom-call | tf_op jit(solution)/shard_map/pallas_call | solution.py:253
  70.5 3.0 %all-to-all-done.2.prefix_ref = bf16[4,40,128]{2,1,0:T(8,128)(2,1)S(1)} async-done(((bf16[4,40,128]{2,1,0:T(8,128)(2,1)}), bf16[4,40,128]{2,1,0:T(8,128)(2,1)S(1)}, u32[]{:S(2)}, u32[]{:S(2)}) %all-to-all-start.2) | async-done | bytes 40992 | tf_op jit(solution)/shard_map/all_to_all | solution.py:258
  73.5 0.6 shard_map.71.mix_ref
  74.1 7.9 %collective-permute-start.8 = (bf16[512,256]{1,0:T(8,128)(2,1)S(1)}, bf16[512,256]{1,0:T(8,128)(2,1)S(1)}, u32[]{:S(2)}, u32[]{:S(2)}) collective-permute-start(bf16[512,256]{1,0:T(8,128)(2,1)S(1)} %shard_map.71.mix_ref), channel_id=1, source_target_pairs={{0,1},{1,0},{2,3},{3,2},{4,5},{5,4},{6,7},{7,6},{8,9},{9,8},{10,11... | collective-permute-start | bytes 786440 | tf_op jit(solution)/shard_map/ppermute | solution.py:221
  82.0 0.5 shard_map.73.own_ref
  82.5 0.0 collective-permute-done.9.w_ref
  82.5 0.7 collective-permute-done.8.mix_ref
  83.1 0.4 shard_map.74
  83.6 22.1 %all_to_all.21 = bf16[4,512,256]{2,1,0:T(8,128)(2,1)S(1)} all-to-all(bf16[4,512,256]{2,1,0:T(8,128)(2,1)S(1)} %shard_map.74), channel_id=1, replica_groups={{0,2,4,6},{1,3,5,7},{8,10,12,14},{9,11,13,15},{16,18,20,22},{17,19,21,2..., dimensions={0} | all-to-all | bytes 2097152 | tf_op jit(solution)/shard_map/all_to_all | solution.py:262
  105.7 0.9 reduce_sum.12
  (2 shorter events, 0.0 us)
Async XLA Ops:
  0.0 10.9 %collective-permute-start.2 = (bf16[512,256]{1,0:T(8,128)(2,1)}, bf16[512,256]{1,0:T(8,128)(2,1)S(1)}, u32[]{:S(2)}, u32[]{:S(2)}) collective-permute-start(bf16[512,256]{1,0:T(8,128)(2,1)} %b0.1), channel_id=1, source_target_pairs={{0,2},{1,3},{2,4},{3,5},{4,6},{5,7},{6,0},{7,1},{8,10},{9,11},{10,... | collective-permute-start | bytes 786440 | tf_op jit(solution)/shard_map/ppermute | solution.py:227
  4.0 17.2 %collective-permute-start.4 = (bf16[512,256]{1,0:T(8,128)(2,1)}, bf16[512,256]{1,0:T(8,128)(2,1)S(1)}, u32[]{:S(2)}, u32[]{:S(2)}) collective-permute-start(bf16[512,256]{1,0:T(8,128)(2,1)} %b0.1), channel_id=1, source_target_pairs={{0,6},{1,7},{2,0},{3,1},{4,2},{5,3},{6,4},{7,5},{8,14},{9,15},{10,... | collective-permute-start | bytes 786440 | tf_op jit(solution)/shard_map/ppermute | solution.py:227
  7.4 22.5 %collective-permute-start.1 = (bf16[512,256]{1,0:T(8,128)(2,1)}, bf16[512,256]{1,0:T(8,128)(2,1)S(1)}, u32[]{:S(2)}, u32[]{:S(2)}) collective-permute-start(bf16[512,256]{1,0:T(8,128)(2,1)} %b0.1), channel_id=1, source_target_pairs={{0,4},{1,5},{2,6},{3,7},{4,0},{5,1},{6,2},{7,3},{8,12},{9,13},{10,... | collective-permute-start | bytes 786440 | tf_op jit(solution)/shard_map/ppermute | solution.py:227
  11.0 18.9 %collective-permute-start.3 = (bf16[512,256]{1,0:T(8,128)(2,1)S(1)}, bf16[512,256]{1,0:T(8,128)(2,1)S(1)}, u32[]{:S(2)}, u32[]{:S(2)}) collective-permute-start(bf16[512,256]{1,0:T(8,128)(2,1)S(1)} %collective-permute-done.2.b1), channel_id=1, source_target_pairs={{0,1},{1,0},{2,3},{3,2},{4,5},{5,4},{6,7},{7,6},{8,9},{9,8},{10,11... | collective-permute-start | bytes 786440 | tf_op jit(solution)/shard_map/ppermute | solution.py:221
  21.3 8.6 %collective-permute-start.5 = (bf16[512,256]{1,0:T(8,128)(2,1)S(1)}, bf16[512,256]{1,0:T(8,128)(2,1)S(1)}, u32[]{:S(2)}, u32[]{:S(2)}) collective-permute-start(bf16[512,256]{1,0:T(8,128)(2,1)S(1)} %collective-permute-done.4.b3), channel_id=1, source_target_pairs={{0,1},{1,0},{2,3},{3,2},{4,5},{5,4},{6,7},{7,6},{8,9},{9,8},{10,11... | collective-permute-start | bytes 786440 | tf_op jit(solution)/shard_map/ppermute | solution.py:221
  23.5 9.6 %collective-permute-start = (bf16[512,256]{1,0:T(8,128)(2,1)}, bf16[512,256]{1,0:T(8,128)(2,1)S(1)}, u32[]{:S(2)}, u32[]{:S(2)}) collective-permute-start(bf16[512,256]{1,0:T(8,128)(2,1)} %b0.1), channel_id=1, source_target_pairs={{0,1},{1,0},{2,3},{3,2},{4,5},{5,4},{6,7},{7,6},{8,9},{9,8},{10,11... | collective-permute-start | bytes 786440 | tf_op jit(solution)/shard_map/ppermute | solution.py:221
  25.6 1.2 %copy-start.1 = (bf16[2048,256]{1,0:T(8,128)(2,1)S(1)}, bf16[2048,256]{1,0:T(8,128)(2,1)}, u32[]{:S(2)}) copy-start(bf16[2048,256]{1,0:T(8,128)(2,1)} %wv_ref.1) | copy-start | bytes 3145732
  26.9 1.2 %copy-start.2 = (bf16[2048,256]{1,0:T(8,128)(2,1)S(1)}, bf16[2048,256]{1,0:T(8,128)(2,1)}, u32[]{:S(2)}) copy-start(bf16[2048,256]{1,0:T(8,128)(2,1)} %ww_ref.1) | copy-start | bytes 3145732
  28.1 0.9 copy-start.4
  29.0 0.7 copy-start.5
  29.7 2.4 %copy-start.3 = (bf16[512,256]{1,0:T(8,128)(2,1)S(1)}, bf16[512,256]{1,0:T(8,128)(2,1)}, u32[]{:S(2)}) copy-start(bf16[512,256]{1,0:T(8,128)(2,1)} %b0.1) | copy-start | bytes 786436
  29.9 3.4 %collective-permute-start.6 = (bf16[512,256]{1,0:T(8,128)(2,1)S(1)}, bf16[512,256]{1,0:T(8,128)(2,1)S(1)}, u32[]{:S(2)}, u32[]{:S(2)}) collective-permute-start(bf16[512,256]{1,0:T(8,128)(2,1)S(1)} %collective-permute-done.1.b2), channel_id=1, source_target_pairs={{0,1},{1,0},{2,3},{3,2},{4,5},{5,4},{6,7},{7,6},{8,9},{9,8},{10,11... | collective-permute-start | bytes 786440 | tf_op jit(solution)/shard_map/ppermute | solution.py:221
  33.1 22.2 %copy-start = (bf16[256,2048]{1,0:T(8,128)(2,1)S(1)}, bf16[256,2048]{1,0:T(8,128)(2,1)}, u32[]{:S(2)}) copy-start(bf16[256,2048]{1,0:T(8,128)(2,1)} %w_ref.3) | copy-start | bytes 3145732
  42.1 23.2 %all-to-all-start.1 = ((bf16[16,40,128]{2,1,0:T(8,128)(2,1)}), bf16[16,40,128]{2,1,0:T(8,128)(2,1)S(1)}, u32[]{:S(2)}, u32[]{:S(2)}) async-start(bf16[16,40,128]{2,1,0:T(8,128)(2,1)} %shard_map.67), calls=%async_computation.1 | async-start | bytes 327680 | tf_op jit(solution)/shard_map/all_to_all | solution.py:247
  53.1 16.1 %collective-permute-start.7 = (bf16[512,256]{1,0:T(8,128)(2,1)S(1)}, bf16[512,256]{1,0:T(8,128)(2,1)S(1)}, u32[]{:S(2)}, u32[]{:S(2)}) collective-permute-start(bf16[512,256]{1,0:T(8,128)(2,1)S(1)} %get-tuple-element.40.own_ref), channel_id=1, source_target_pairs={{0,8},{8,16},{16,24},{24,32},{32,40},{40,48},{48,56},{56,64},{64,7... | collective-permute-start | bytes 786440 | tf_op jit(solution)/shard_map/ppermute | solution.py:250
  55.4 27.0 %collective-permute-start.9 = (bf16[4,256,256]{2,1,0:T(8,128)(2,1)S(1)}, bf16[4,256,256]{2,1,0:T(8,128)(2,1)S(1)}, u32[]{:S(2)}, u32[]{:S(2)}) collective-permute-start(bf16[4,256,256]{2,1,0:T(8,128)(2,1)S(1)} %shard_map.72), channel_id=1, source_target_pairs={{0,1},{1,0},{2,3},{3,2},{4,5},{5,4},{6,7},{7,6},{8,9},{9,8},{10,11... | collective-permute-start | bytes 1572872 | tf_op jit(solution)/shard_map/ppermute | solution.py:221
  66.0 7.6 %all-to-all-start.2 = ((bf16[4,40,128]{2,1,0:T(8,128)(2,1)}), bf16[4,40,128]{2,1,0:T(8,128)(2,1)S(1)}, u32[]{:S(2)}, u32[]{:S(2)}) async-start(bf16[4,40,128]{2,1,0:T(8,128)(2,1)} %shard_map.68), calls=%async_computation.2 | async-start | bytes 81920 | tf_op jit(solution)/shard_map/all_to_all | solution.py:258
  74.1 9.0 %collective-permute-start.8 = (bf16[512,256]{1,0:T(8,128)(2,1)S(1)}, bf16[512,256]{1,0:T(8,128)(2,1)S(1)}, u32[]{:S(2)}, u32[]{:S(2)}) collective-permute-start(bf16[512,256]{1,0:T(8,128)(2,1)S(1)} %shard_map.71.mix_ref), channel_id=1, source_target_pairs={{0,1},{1,0},{2,3},{3,2},{4,5},{5,4},{6,7},{7,6},{8,9},{9,8},{10,11... | collective-permute-start | bytes 786440 | tf_op jit(solution)/shard_map/ppermute | solution.py:221

commit v12 on v9

--- a/solution.py
+++ b/solution.py
@@ -26,11 +26,11 @@
     )
 
 
-def call_with_scalar(kernel, outs, count):
+def call_with_scalar(kernel, outs, count, scalars=1):
     return pl.pallas_call(
         kernel,
         out_shape=outs,
-        in_specs=[pl.BlockSpec(memory_space=pltpu.SMEM)] + [pl.BlockSpec(memory_space=pltpu.VMEM)] * count,
+        in_specs=[pl.BlockSpec(memory_space=pltpu.SMEM)] * scalars + [pl.BlockSpec(memory_space=pltpu.VMEM)] * count,
         compiler_params=pltpu.CompilerParams(vmem_limit_bytes=VMEM),
     )
 
@@ -84,6 +84,11 @@
         values = values + dot(scaled, wv_ref[pl.ds(at, 256), :])
         windowed = windowed + dot(scaled, ww_ref[pl.ds(at, 256), :])
     return jnp.sum(squares, axis=1, keepdims=True), feats, values, windowed
+
+
+def copies_kernel(core_ref, ctx_ref, row_ref, x_ref, out_ref):
+    for y in range(4):
+        out_ref[y, :, :] = x_ref[...]
 
 
 def begin_kernel(core_ref, x_ref, gain_ref, wf_ref, wv_ref, ww_ref, held_ref):
@@ -214,9 +219,10 @@
     def shape(dims, kind=BF):
         return jax.ShapeDtypeStruct(dims, kind)
 
-    spread = lax.all_to_all(
-        jnp.broadcast_to(tokens[None], (4,) + tokens.shape), "head", 0, 0, tiled=True, axis_index_groups=along_y
-    )
+    block = ctx.astype(jnp.int32).reshape(1)
+    row = (ctx // 4).astype(jnp.int32).reshape(1)
+    copies = call_with_scalar(copies_kernel, shape((4,) + tokens.shape), 1, 3)(core, block, row, tokens)
+    spread = lax.all_to_all(copies, "head", 0, 0, tiled=True, axis_index_groups=along_y)
     other = across(spread)
     weights = (gain.reshape(1, -1), w_feat.T, w_value, w_window)
     held = call_with_scalar(begin_kernel, shape((count, 640), F32), 5)(core, spread, *weights)
@@ -233,9 +239,9 @@
     prev = lax.ppermute(rim, "ctx", [(b, b + 1) for b in range(63)])
     numerator = call(inner_kernel, shape((count, 128), F32))(pack, quarters)
     w_other = across(call_with_scalar(pick_kernel, shape((4, 256, 256)), 2)(core, w_out, quarters))
-    win_out = call_with_scalar(attend_kernel, shape((count, 128)), 3)(ctx.astype(jnp.int32).reshape(1), pack, rim, prev)
+    win_out = call_with_scalar(attend_kernel, shape((count, 128)), 3)(block, pack, rim, prev)
     sums = call_with_scalar(prefix_kernel, shape((4, QUARTER, 128)), 2)(
-        (ctx // 4).astype(jnp.int32).reshape(1), quarters, totals
+        row, quarters, totals
     )
     sums, numerator = lax.optimization_barrier((sums, numerator))
     prefix = lax.all_to_all(sums, "ctx", 0, 0, tiled=True, axis_index_groups=in_x)

time: 103 us -> 101 us (0.981)
  Pallas kernels: 8.44 us -> 7.21 us
    pallas_call x1, Pallas kernels: 2.67 us -> 1.36 us  [shards(): call_with_scalar(project_kernel, [shape((count, 384)), shape((count, 256)...]
    broadcast_in_dim x1 -> x0, local copies, waits for them, and re-layouts: 1.17 us -> none  [shards(): jnp.broadcast_to(tokens[None], (4,) + tokens.shape)]
    unnamed x16 -> x18, local copies, waits for them, and re-layouts: 0.73 us -> 1.82 us
where the time goes in v12:
time: 101 us
  blocking collectives  41 us (41%)
  starting transfers between devices  39.8 us (39%)
  waiting for transfers between devices  9.86 us (10%)
  Pallas kernels  7.21 us (7%)
  local copies, waits for them, and re-layouts  1.82 us (2%)
    ppermute x3, starting transfers between devices, across(): return lax.ppermute(value, 'head', [(h, h ^ 1) for h in range(8)])  19.4 us
    all_to_all x1, blocking collectives, shards(): lax.all_to_all(summed, 'head', 0, 0, tiled=True, axis_index_groups=along_y)  17.3 us
    all_to_all x1, blocking collectives, shards(): lax.all_to_all(copies, 'head', 0, 0, tiled=True, axis_index_groups=along_y)  15.5 us
    all_to_all x1, starting transfers between devices, shards(): lax.all_to_all(call(total_kernel, shape((16, QUARTER, 128)))(quarters), '...  14.9 us
    all_to_all x1, blocking collectives, shards(): lax.all_to_all(states, 'ctx', 0, 0, tiled=True, axis_index_groups=in_x)  8.27 us
    all_to_all x1, waiting for transfers between devices, shards(): lax.all_to_all(call(total_kernel, shape((16, QUARTER, 128)))(quarters), '...  4.98 us
    all_to_all x1, starting transfers between devices, shards(): lax.all_to_all(sums, 'ctx', 0, 0, tiled=True, axis_index_groups=in_x)  3.27 us
    all_to_all x1, waiting for transfers between devices, shards(): lax.all_to_all(sums, 'ctx', 0, 0, tiled=True, axis_index_groups=in_x)  2.99 us
  transfers between devices with their start and end apart: 6, of which 4 were waited for; matrix products, arithmetic and copies ran while one was open for 0% of the time, Pallas kernels for 5%

profile of v12, /device:TPU:1, one launch (start us, length us, event | category | flops | bytes accessed | tf_op | source)
XLA Modules:
  0.0 100.9 jit_solution(663030463886235510)
XLA Ops:
  0.0 0.0 copy-start.1
  0.0 0.0 copy-start
  0.0 0.0 copy-start.3
  0.0 0.0 copy-start.5
  0.0 1.1 %copy-done.5 = bf16[512,256]{1,0:T(8,128)(2,1)S(1)} copy-done((bf16[512,256]{1,0:T(8,128)(2,1)S(1)}, bf16[512,256]{1,0:T(8,128)(2,1)}, u32[]{:S(2)}) %copy-start.5) | copy-done | bytes 262168
  1.1 0.0 copy-start.8
  1.1 0.1 shard_map.64
  1.2 15.5 %all_to_all.25.x_ref = bf16[4,512,256]{2,1,0:T(8,128)(2,1)S(1)} all-to-all(bf16[4,512,256]{2,1,0:T(8,128)(2,1)S(1)} %shard_map.64), channel_id=1, replica_groups={{0,2,4,6},{1,3,5,7},{8,10,12,14},{9,11,13,15},{16,18,20,22},{17,19,21,2..., dimensions={0} | all-to-all | bytes 2097152 | tf_op jit(solution)/shard_map/all_to_all | solution.py:225
  16.7 7.3 %collective-permute-start = (bf16[4,512,256]{2,1,0:T(8,128)(2,1)S(1)}, bf16[4,512,256]{2,1,0:T(8,128)(2,1)S(1)}, u32[]{:S(2)}, u32[]{:S(2)}) collective-permute-start(bf16[4,512,256]{2,1,0:T(8,128)(2,1)S(1)} %all_to_all.25.x_ref), channel_id=1, source_target_pairs={{0,1},{1,0},{2,3},{3,2},{4,5},{5,4},{6,7},{7,6},{8,9},{9,8},{10,11... | collective-permute-start | bytes 3145736 | tf_op jit(solution)/shard_map/ppermute | solution.py:217
  24.0 0.0 copy-done.1
  24.0 0.0 copy-done
  24.0 0.0 copy-done.3
  24.0 0.0 copy-done.8
  24.0 0.0 copy-start.4
  24.0 1.0 shard_map.65.held_ref
  25.0 0.0 copy-start.2
  25.0 1.2 %collective-permute-done.x_ref = bf16[4,512,256]{2,1,0:T(8,128)(2,1)S(1)} collective-permute-done((bf16[4,512,256]{2,1,0:T(8,128)(2,1)S(1)}, bf16[4,512,256]{2,1,0:T(8,128)(2,1)S(1)}, u32[]{:S(2)}, u32[]{:S(2)}) %collective-permute-start) | collective-permute-done | bytes 1048608 | tf_op jit(solution)/shard_map/ppermute | solution.py:217
  26.2 0.0 copy-done.4
  26.2 1.4 %shard_map.66 = (bf16[512,384]{1,0:T(8,128)(2,1)S(1)}, bf16[512,256]{1,0:T(8,128)(2,1)S(1)}, bf16[4,40,128]{2,1,0:T(8,128)(2,1)S(1)}) custom-call(s32[1]{0:T(128)} %bitcast.core_ref, bf16[4,512,256]{2,1,0:T(8,128)(2,1)S(1)} %collective-permute-done.x_ref, f32[1,2048]{1,0:T(1,128)S(1)} %bitcast.8, bf16[32,2048]{1,0:T(8,128)(2,1)S(1)} %bitcast.6, ...), custom_call_target="tpu_custom_call" | custom-call | tf_op jit(solution)/shard_map/pallas_call | solution.py:229
  27.6 0.0 copy-start.6
  27.6 0.7 copy-done.6
  28.3 0.0 copy-start.7
  28.3 8.3 %all_to_all.26.got_ref.after_ref = bf16[4,40,128]{2,1,0:T(8,128)(2,1)S(1)} all-to-all(bf16[4,40,128]{2,1,0:T(8,128)(2,1)S(1)} %get-tuple-element.14), channel_id=1, replica_groups={{0,8,16,24},{32,40,48,56},{64,72,80,88},{96,104,112,120},{128,136,144,1..., dimensions={0} | all-to-all | bytes 81920 | tf_op jit(solution)/shard_map/all_to_all | solution.py:234
  36.6 0.7 shard_map.67
  37.3 14.9 %all-to-all-start.2 = ((bf16[16,40,128]{2,1,0:T(8,128)(2,1)}), bf16[16,40,128]{2,1,0:T(8,128)(2,1)S(1)}, u32[]{:S(2)}, u32[]{:S(2)}) async-start(bf16[16,40,128]{2,1,0:T(8,128)(2,1)} %shard_map.67), calls=%async_computation.2 | async-start | bytes 327680 | tf_op jit(solution)/shard_map/all_to_all | solution.py:236
  52.2 2.2 %collective-permute-start.1 = (bf16[512,256]{1,0:T(8,128)(2,1)}, bf16[512,256]{1,0:T(8,128)(2,1)S(1)}, u32[]{:S(2)}, u32[]{:S(2)}) collective-permute-start(bf16[512,256]{1,0:T(8,128)(2,1)} %copy-done.6), channel_id=1, source_target_pairs={{0,8},{8,16},{16,24},{24,32},{32,40},{40,48},{48,56},{56,64},{64,7... | collective-permute-start | bytes 786440 | tf_op jit(solution)/shard_map/ppermute | solution.py:239
  54.4 0.0 copy-done.2
  54.4 0.1 shard_map.72
  54.5 4.3 %collective-permute-start.3 = (bf16[4,256,256]{2,1,0:T(8,128)(2,1)S(1)}, bf16[4,256,256]{2,1,0:T(8,128)(2,1)S(1)}, u32[]{:S(2)}, u32[]{:S(2)}) collective-permute-start(bf16[4,256,256]{2,1,0:T(8,128)(2,1)S(1)} %shard_map.72), channel_id=1, source_target_pairs={{0,1},{1,0},{2,3},{3,2},{4,5},{5,4},{6,7},{7,6},{8,9},{9,8},{10,11... | collective-permute-start | bytes 1572872 | tf_op jit(solution)/shard_map/ppermute | solution.py:217
  58.8 0.6 shard_map.69.num_ref
  59.4 5.0 %all-to-all-done.2.totals_ref = bf16[16,40,128]{2,1,0:T(8,128)(2,1)S(1)} async-done(((bf16[16,40,128]{2,1,0:T(8,128)(2,1)}), bf16[16,40,128]{2,1,0:T(8,128)(2,1)S(1)}, u32[]{:S(2)}, u32[]{:S(2)}) %all-to-all-start.2) | async-done | bytes 163872 | tf_op jit(solution)/shard_map/all_to_all | solution.py:236
  64.4 0.7 shard_map.68
  65.0 3.3 %all-to-all-start.3 = ((bf16[4,40,128]{2,1,0:T(8,128)(2,1)}), bf16[4,40,128]{2,1,0:T(8,128)(2,1)S(1)}, u32[]{:S(2)}, u32[]{:S(2)}) async-start(bf16[4,40,128]{2,1,0:T(8,128)(2,1)} %shard_map.68), calls=%async_computation.3 | async-start | bytes 81920 | tf_op jit(solution)/shard_map/all_to_all | solution.py:247
  68.3 0.0 collective-permute-done.1.prev_ref
  68.3 0.0 copy-done.7
  68.3 1.3 %shard_map.70.win_ref = bf16[512,128]{1,0:T(8,128)(2,1)S(1)} custom-call(s32[1]{0:T(128)} %bitcast.1.ctx_ref.first_ref, bf16[512,384]{1,0:T(8,128)(2,1)S(1)} %get-tuple-element.12.pack_ref, bf16[512,256]{1,0:T(8,128)(2,1)S(1)} %copy-done.7, bf16[512,256]{1,0:T(8,128)(2,1)S(1)} %collective-permute-done.1.prev_ref), custom_call_target="tpu_custom_call" | custom-call | tf_op jit(solution)/shard_map/pallas_call | solution.py:242
  69.6 3.0 %all-to-all-done.3.prefix_ref = bf16[4,40,128]{2,1,0:T(8,128)(2,1)S(1)} async-done(((bf16[4,40,128]{2,1,0:T(8,128)(2,1)}), bf16[4,40,128]{2,1,0:T(8,128)(2,1)S(1)}, u32[]{:S(2)}, u32[]{:S(2)}) %all-to-all-start.3) | async-done | bytes 40992 | tf_op jit(solution)/shard_map/all_to_all | solution.py:247
  72.6 0.6 shard_map.71.mix_ref
  73.2 7.9 %collective-permute-start.2 = (bf16[512,256]{1,0:T(8,128)(2,1)S(1)}, bf16[512,256]{1,0:T(8,128)(2,1)S(1)}, u32[]{:S(2)}, u32[]{:S(2)}) collective-permute-start(bf16[512,256]{1,0:T(8,128)(2,1)S(1)} %shard_map.71.mix_ref), channel_id=1, source_target_pairs={{0,1},{1,0},{2,3},{3,2},{4,5},{5,4},{6,7},{7,6},{8,9},{9,8},{10,11... | collective-permute-start | bytes 786440 | tf_op jit(solution)/shard_map/ppermute | solution.py:217
  81.1 0.5 shard_map.73.own_ref
  81.6 0.0 collective-permute-done.3.w_ref
  81.6 0.7 collective-permute-done.2.mix_ref
  82.3 0.4 shard_map.74
  82.7 17.3 %all_to_all.27 = bf16[4,512,256]{2,1,0:T(8,128)(2,1)S(1)} all-to-all(bf16[4,512,256]{2,1,0:T(8,128)(2,1)S(1)} %shard_map.74), channel_id=1, replica_groups={{0,2,4,6},{1,3,5,7},{8,10,12,14},{9,11,13,15},{16,18,20,22},{17,19,21,2..., dimensions={0} | all-to-all | bytes 2097152 | tf_op jit(solution)/shard_map/all_to_all | solution.py:251
  100.0 0.9 reduce_sum.12
Async XLA Ops:
  0.0 24.0 %copy-start.1 = (bf16[2048,256]{1,0:T(8,128)(2,1)S(1)}, bf16[2048,256]{1,0:T(8,128)(2,1)}, u32[]{:S(2)}) copy-start(bf16[2048,256]{1,0:T(8,128)(2,1)} %ww_ref.3) | copy-start | bytes 3145732
  0.0 24.0 %copy-start = (bf16[2048,256]{1,0:T(8,128)(2,1)S(1)}, bf16[2048,256]{1,0:T(8,128)(2,1)}, u32[]{:S(2)}) copy-start(bf16[2048,256]{1,0:T(8,128)(2,1)} %wv_ref.3) | copy-start | bytes 3145732
  0.0 24.0 %copy-start.3 = (bf16[2048,32]{0,1:T(8,128)(2,1)S(1)}, bf16[2048,32]{0,1:T(8,128)(2,1)}, u32[]{:S(2)}) copy-start(bf16[2048,32]{0,1:T(8,128)(2,1)} %param.8) | copy-start | bytes 393220
  0.0 1.1 %copy-start.5 = (bf16[512,256]{1,0:T(8,128)(2,1)S(1)}, bf16[512,256]{1,0:T(8,128)(2,1)}, u32[]{:S(2)}) copy-start(bf16[512,256]{1,0:T(8,128)(2,1)} %x_ref.1) | copy-start | bytes 786436
  1.1 22.9 %copy-start.8 = (f32[2048]{0:T(1024)S(1)}, f32[2048]{0:T(1024)}, u32[]{:S(2)}) copy-start(f32[2048]{0:T(1024)} %param.7) | copy-start | bytes 24580
  16.7 9.6 %collective-permute-start = (bf16[4,512,256]{2,1,0:T(8,128)(2,1)S(1)}, bf16[4,512,256]{2,1,0:T(8,128)(2,1)S(1)}, u32[]{:S(2)}, u32[]{:S(2)}) collective-permute-start(bf16[4,512,256]{2,1,0:T(8,128)(2,1)S(1)} %all_to_all.25.x_ref), channel_id=1, source_target_pairs={{0,1},{1,0},{2,3},{3,2},{4,5},{5,4},{6,7},{7,6},{8,9},{9,8},{10,11... | collective-permute-start | bytes 3145736 | tf_op jit(solution)/shard_map/ppermute | solution.py:217
  24.0 2.2 %copy-start.4 = (bf16[2048,32]{0,1:T(8,128)(2,1)S(1)}, bf16[2048,32]{0,1:T(8,128)(2,1)}, u32[]{:S(2)}) copy-start(bf16[2048,32]{0,1:T(8,128)(2,1)} %param.8) | copy-start | bytes 393220
  25.0 29.4 %copy-start.2 = (bf16[256,2048]{1,0:T(8,128)(2,1)S(1)}, bf16[256,2048]{1,0:T(8,128)(2,1)}, u32[]{:S(2)}) copy-start(bf16[256,2048]{1,0:T(8,128)(2,1)} %w_ref.3) | copy-start | bytes 3145732
  27.6 0.7 copy-start.6
  28.3 40.0 %copy-start.7 = (bf16[512,256]{1,0:T(8,128)(2,1)S(1)}, bf16[512,256]{1,0:T(8,128)(2,1)}, u32[]{:S(2)}) copy-start(bf16[512,256]{1,0:T(8,128)(2,1)} %copy-done.6) | copy-start | bytes 786436
  37.3 27.1 %all-to-all-start.2 = ((bf16[16,40,128]{2,1,0:T(8,128)(2,1)}), bf16[16,40,128]{2,1,0:T(8,128)(2,1)S(1)}, u32[]{:S(2)}, u32[]{:S(2)}) async-start(bf16[16,40,128]{2,1,0:T(8,128)(2,1)} %shard_map.67), calls=%async_computation.2 | async-start | bytes 327680 | tf_op jit(solution)/shard_map/all_to_all | solution.py:236
  52.2 16.1 %collective-permute-start.1 = (bf16[512,256]{1,0:T(8,128)(2,1)}, bf16[512,256]{1,0:T(8,128)(2,1)S(1)}, u32[]{:S(2)}, u32[]{:S(2)}) collective-permute-start(bf16[512,256]{1,0:T(8,128)(2,1)} %copy-done.6), channel_id=1, source_target_pairs={{0,8},{8,16},{16,24},{24,32},{32,40},{40,48},{48,56},{56,64},{64,7... | collective-permute-start | bytes 786440 | tf_op jit(solution)/shard_map/ppermute | solution.py:239
  54.5 27.1 %collective-permute-start.3 = (bf16[4,256,256]{2,1,0:T(8,128)(2,1)S(1)}, bf16[4,256,256]{2,1,0:T(8,128)(2,1)S(1)}, u32[]{:S(2)}, u32[]{:S(2)}) collective-permute-start(bf16[4,256,256]{2,1,0:T(8,128)(2,1)S(1)} %shard_map.72), channel_id=1, source_target_pairs={{0,1},{1,0},{2,3},{3,2},{4,5},{5,4},{6,7},{7,6},{8,9},{9,8},{10,11... | collective-permute-start | bytes 1572872 | tf_op jit(solution)/shard_map/ppermute | solution.py:217
  65.0 7.6 %all-to-all-start.3 = ((bf16[4,40,128]{2,1,0:T(8,128)(2,1)}), bf16[4,40,128]{2,1,0:T(8,128)(2,1)S(1)}, u32[]{:S(2)}, u32[]{:S(2)}) async-start(bf16[4,40,128]{2,1,0:T(8,128)(2,1)} %shard_map.68), calls=%async_computation.3 | async-start | bytes 81920 | tf_op jit(solution)/shard_map/all_to_all | solution.py:247
  73.2 9.0 %collective-permute-start.2 = (bf16[512,256]{1,0:T(8,128)(2,1)S(1)}, bf16[512,256]{1,0:T(8,128)(2,1)S(1)}, u32[]{:S(2)}, u32[]{:S(2)}) collective-permute-start(bf16[512,256]{1,0:T(8,128)(2,1)S(1)} %shard_map.71.mix_ref), channel_id=1, source_target_pairs={{0,1},{1,0},{2,3},{3,2},{4,5},{5,4},{6,7},{7,6},{8,9},{9,8},{10,11... | collective-permute-start | bytes 786440 | tf_op jit(solution)/shard_map/ppermute | solution.py:217

commit v13 on v12

--- a/solution.py
+++ b/solution.py
@@ -112,7 +112,9 @@
     pack_ref[:, :128] = windowed[:, :128]
     pack_ref[:, 128:256] = vlin
     pack_ref[:, 256:288] = feats
-    pack_ref[:, 288:] = jnp.zeros((count, 96), BF)
+    pack_ref[:, 288:384] = jnp.zeros((count, 96), BF)
+    pack_ref[:, 384:512] = windowed[:, 128:]
+    pack_ref[:, 512:] = values[:, 128:]
     first, second = pick((ROWS, FEAT), 0)
     scale, add_first, add_second = weights_of((ROWS, 1), 0, False)
     k = feats[:, FEAT:]
@@ -137,14 +139,14 @@
         num_ref[t * tile : (t + 1) * tile, :] = dot(weight, pack_ref[: (t + 1) * tile, 128:256])
 
 
-def attend_kernel(first_ref, pack_ref, own_ref, prev_ref, win_ref):
+def attend_kernel(first_ref, pack_ref, prev_ref, win_ref):
     count = pack_ref.shape[0]
     tile = 256
     no_prev = first_ref[0] == 0
     for t in range(count // tile):
         q = pack_ref[t * tile : (t + 1) * tile, :128]
         old = prev_ref[t * tile :, :]
-        new = own_ref[: (t + 1) * tile, :]
+        new = pack_ref[: (t + 1) * tile, 384:]
         keys = jnp.concatenate([old[:, :128], new[:, :128]], axis=0)
         vals = jnp.concatenate([old[:, 128:], new[:, 128:]], axis=0)
         width = keys.shape[0]
@@ -227,7 +229,7 @@
     weights = (gain.reshape(1, -1), w_feat.T, w_value, w_window)
     held = call_with_scalar(begin_kernel, shape((count, 640), F32), 5)(core, spread, *weights)
     pack, rim, states = call_with_scalar(
-        project_kernel, [shape((count, 384)), shape((count, 256)), shape((4, QUARTER, 128))], 6
+        project_kernel, [shape((count, 640)), shape((count, 256)), shape((4, QUARTER, 128))], 6
     )(core, other, *weights, held)
     in_x = [[4 * z + x for x in range(4)] for z in range(16)]
     in_z = [[4 * z + x for z in range(16)] for x in range(4)]
@@ -239,7 +241,7 @@
     prev = lax.ppermute(rim, "ctx", [(b, b + 1) for b in range(63)])
     numerator = call(inner_kernel, shape((count, 128), F32))(pack, quarters)
     w_other = across(call_with_scalar(pick_kernel, shape((4, 256, 256)), 2)(core, w_out, quarters))
-    win_out = call_with_scalar(attend_kernel, shape((count, 128)), 3)(block, pack, rim, prev)
+    win_out = call_with_scalar(attend_kernel, shape((count, 128)), 2)(block, pack, prev)
     sums = call_with_scalar(prefix_kernel, shape((4, QUARTER, 128)), 2)(
         row, quarters, totals
     )

time: 101 us -> 101 us (level)
  waiting for transfers between devices: 9.86 us -> 8.52 us
    all_to_all x1, waiting for transfers between devices: 4.98 us -> 3.62 us  [shards(): lax.all_to_all(call(total_kernel, shape((16, QUARTER, 128)))(quarters), '...]
    unnamed x18 -> x14, local copies, waits for them, and re-layouts: 1.82 us -> 2.33 us
where the time goes in v13:
time: 101 us
  blocking collectives  40.9 us (40%)
  starting transfers between devices  40 us (40%)
  waiting for transfers between devices  8.52 us (8%)
  Pallas kernels  7.68 us (8%)
  local copies, waits for them, and re-layouts  2.33 us (2%)
    ppermute x3, starting transfers between devices, across(): return lax.ppermute(value, 'head', [(h, h ^ 1) for h in range(8)])  19.6 us
    all_to_all x1, blocking collectives, shards(): lax.all_to_all(summed, 'head', 0, 0, tiled=True, axis_index_groups=along_y)  17.3 us
    all_to_all x1, blocking collectives, shards(): lax.all_to_all(copies, 'head', 0, 0, tiled=True, axis_index_groups=along_y)  15.5 us
    all_to_all x1, starting transfers between devices, shards(): lax.all_to_all(call(total_kernel, shape((16, QUARTER, 128)))(quarters), '...  14.9 us
    all_to_all x1, blocking collectives, shards(): lax.all_to_all(states, 'ctx', 0, 0, tiled=True, axis_index_groups=in_x)  8.15 us
    all_to_all x1, waiting for transfers between devices, shards(): lax.all_to_all(call(total_kernel, shape((16, QUARTER, 128)))(quarters), '...  3.62 us
    all_to_all x1, starting transfers between devices, shards(): lax.all_to_all(sums, 'ctx', 0, 0, tiled=True, axis_index_groups=in_x)  3.27 us
    all_to_all x1, waiting for transfers between devices, shards(): lax.all_to_all(sums, 'ctx', 0, 0, tiled=True, axis_index_groups=in_x)  3 us
  transfers between devices with their start and end apart: 6, of which 4 were waited for; matrix products, arithmetic and copies ran while one was open for 0% of the time, Pallas kernels for 5%

profile of v13, /device:TPU:1, one launch (start us, length us, event | category | flops | bytes accessed | tf_op | source)
XLA Modules:
  0.0 100.5 jit_solution(4241509068203621280)
XLA Ops:
  0.0 0.0 copy-start.1
  0.0 0.0 copy-start
  0.0 0.0 copy-start.4
  0.0 0.0 copy-start.5
  0.0 1.1 %copy-done.5 = bf16[512,256]{1,0:T(8,128)(2,1)S(1)} copy-done((bf16[512,256]{1,0:T(8,128)(2,1)S(1)}, bf16[512,256]{1,0:T(8,128)(2,1)}, u32[]{:S(2)}) %copy-start.5) | copy-done | bytes 262168
  1.1 0.0 copy-start.6
  1.1 0.1 shard_map.64
  1.2 15.5 %all_to_all.25.x_ref = bf16[4,512,256]{2,1,0:T(8,128)(2,1)S(1)} all-to-all(bf16[4,512,256]{2,1,0:T(8,128)(2,1)S(1)} %shard_map.64), channel_id=1, replica_groups={{0,2,4,6},{1,3,5,7},{8,10,12,14},{9,11,13,15},{16,18,20,22},{17,19,21,2..., dimensions={0} | all-to-all | bytes 2097152 | tf_op jit(solution)/shard_map/all_to_all | solution.py:227
  16.7 7.3 %collective-permute-start = (bf16[4,512,256]{2,1,0:T(8,128)(2,1)S(1)}, bf16[4,512,256]{2,1,0:T(8,128)(2,1)S(1)}, u32[]{:S(2)}, u32[]{:S(2)}) collective-permute-start(bf16[4,512,256]{2,1,0:T(8,128)(2,1)S(1)} %all_to_all.25.x_ref), channel_id=1, source_target_pairs={{0,1},{1,0},{2,3},{3,2},{4,5},{5,4},{6,7},{7,6},{8,9},{9,8},{10,11... | collective-permute-start | bytes 3145736 | tf_op jit(solution)/shard_map/ppermute | solution.py:219
  24.0 0.0 copy-done.1
  24.0 0.0 copy-done
  24.0 0.0 copy-done.4
  24.0 0.0 copy-done.6
  24.0 1.0 shard_map.65.held_ref
  25.0 1.2 %collective-permute-done.x_ref = bf16[4,512,256]{2,1,0:T(8,128)(2,1)S(1)} collective-permute-done((bf16[4,512,256]{2,1,0:T(8,128)(2,1)S(1)}, bf16[4,512,256]{2,1,0:T(8,128)(2,1)S(1)}, u32[]{:S(2)}, u32[]{:S(2)}) %collective-permute-start) | collective-permute-done | bytes 1048608 | tf_op jit(solution)/shard_map/ppermute | solution.py:219
  26.2 1.8 %shard_map.66 = (bf16[512,640]{1,0:T(8,128)(2,1)S(1)}, bf16[512,256]{1,0:T(8,128)(2,1)}, bf16[4,40,128]{2,1,0:T(8,128)(2,1)S(1)}) custom-call(s32[1]{0:T(128)} %bitcast.core_ref, bf16[4,512,256]{2,1,0:T(8,128)(2,1)S(1)} %collective-permute-done.x_ref, f32[1,2048]{1,0:T(1,128)S(1)} %bitcast.8, bf16[32,2048]{1,0:T(8,128)(2,1)S(1)} %bitcast.6, ...), custom_call_target="tpu_custom_call" | custom-call | tf_op jit(solution)/shard_map/pallas_call | solution.py:231
  28.1 8.2 %all_to_all.26.got_ref.after_ref = bf16[4,40,128]{2,1,0:T(8,128)(2,1)S(1)} all-to-all(bf16[4,40,128]{2,1,0:T(8,128)(2,1)S(1)} %get-tuple-element.14), channel_id=1, replica_groups={{0,8,16,24},{32,40,48,56},{64,72,80,88},{96,104,112,120},{128,136,144,1..., dimensions={0} | all-to-all | bytes 81920 | tf_op jit(solution)/shard_map/all_to_all | solution.py:236
  36.2 0.7 shard_map.67
  36.9 14.9 %all-to-all-start.2 = ((bf16[16,40,128]{2,1,0:T(8,128)(2,1)}), bf16[16,40,128]{2,1,0:T(8,128)(2,1)S(1)}, u32[]{:S(2)}, u32[]{:S(2)}) async-start(bf16[16,40,128]{2,1,0:T(8,128)(2,1)} %shard_map.67), calls=%async_computation.2 | async-start | bytes 327680 | tf_op jit(solution)/shard_map/all_to_all | solution.py:238
  51.8 2.2 %collective-permute-start.1 = (bf16[512,256]{1,0:T(8,128)(2,1)}, bf16[512,256]{1,0:T(8,128)(2,1)S(1)}, u32[]{:S(2)}, u32[]{:S(2)}) collective-permute-start(bf16[512,256]{1,0:T(8,128)(2,1)} %get-tuple-element.18), channel_id=1, source_target_pairs={{0,8},{8,16},{16,24},{24,32},{32,40},{40,48},{48,56},{56,64},{64,7... | collective-permute-start | bytes 786440 | tf_op jit(solution)/shard_map/ppermute | solution.py:241
  54.0 0.0 copy-start.2
  54.0 1.2 %copy-done.2 = bf16[256,2048]{1,0:T(8,128)(2,1)S(1)} copy-done((bf16[256,2048]{1,0:T(8,128)(2,1)S(1)}, bf16[256,2048]{1,0:T(8,128)(2,1)}, u32[]{:S(2)}) %copy-start.2) | copy-done | bytes 1048600
  55.3 0.1 shard_map.72
  55.3 0.0 copy-start.3
  55.3 4.4 %collective-permute-start.3 = (bf16[4,256,256]{2,1,0:T(8,128)(2,1)S(1)}, bf16[4,256,256]{2,1,0:T(8,128)(2,1)S(1)}, u32[]{:S(2)}, u32[]{:S(2)}) collective-permute-start(bf16[4,256,256]{2,1,0:T(8,128)(2,1)S(1)} %shard_map.72), channel_id=1, source_target_pairs={{0,1},{1,0},{2,3},{3,2},{4,5},{5,4},{6,7},{7,6},{8,9},{9,8},{10,11... | collective-permute-start | bytes 1572872 | tf_op jit(solution)/shard_map/ppermute | solution.py:219
  59.8 0.6 shard_map.69.num_ref
  60.4 3.6 %all-to-all-done.2.totals_ref = bf16[16,40,128]{2,1,0:T(8,128)(2,1)S(1)} async-done(((bf16[16,40,128]{2,1,0:T(8,128)(2,1)}), bf16[16,40,128]{2,1,0:T(8,128)(2,1)S(1)}, u32[]{:S(2)}, u32[]{:S(2)}) %all-to-all-start.2) | async-done | bytes 163872 | tf_op jit(solution)/shard_map/all_to_all | solution.py:238
  64.0 0.7 shard_map.68
  64.7 3.3 %all-to-all-start.3 = ((bf16[4,40,128]{2,1,0:T(8,128)(2,1)}), bf16[4,40,128]{2,1,0:T(8,128)(2,1)S(1)}, u32[]{:S(2)}, u32[]{:S(2)}) async-start(bf16[4,40,128]{2,1,0:T(8,128)(2,1)} %shard_map.68), calls=%async_computation.3 | async-start | bytes 81920 | tf_op jit(solution)/shard_map/all_to_all | solution.py:249
  67.9 0.0 collective-permute-done.1.prev_ref
  67.9 1.3 %shard_map.70.win_ref = bf16[512,128]{1,0:T(8,128)(2,1)S(1)} custom-call(s32[1]{0:T(128)} %bitcast.1.ctx_ref.first_ref, bf16[512,640]{1,0:T(8,128)(2,1)S(1)} %get-tuple-element.12.pack_ref, bf16[512,256]{1,0:T(8,128)(2,1)S(1)} %collective-permute-done.1.prev_ref), custom_call_target="tpu_custom_call" | custom-call | tf_op jit(solution)/shard_map/pallas_call | solution.py:244
  69.2 3.0 %all-to-all-done.3.prefix_ref = bf16[4,40,128]{2,1,0:T(8,128)(2,1)S(1)} async-done(((bf16[4,40,128]{2,1,0:T(8,128)(2,1)}), bf16[4,40,128]{2,1,0:T(8,128)(2,1)S(1)}, u32[]{:S(2)}, u32[]{:S(2)}) %all-to-all-start.3) | async-done | bytes 40992 | tf_op jit(solution)/shard_map/all_to_all | solution.py:249
  72.2 0.6 shard_map.71.mix_ref
  72.8 7.9 %collective-permute-start.2 = (bf16[512,256]{1,0:T(8,128)(2,1)S(1)}, bf16[512,256]{1,0:T(8,128)(2,1)S(1)}, u32[]{:S(2)}, u32[]{:S(2)}) collective-permute-start(bf16[512,256]{1,0:T(8,128)(2,1)S(1)} %shard_map.71.mix_ref), channel_id=1, source_target_pairs={{0,1},{1,0},{2,3},{3,2},{4,5},{5,4},{6,7},{7,6},{8,9},{9,8},{10,11... | collective-permute-start | bytes 786440 | tf_op jit(solution)/shard_map/ppermute | solution.py:219
  80.7 0.0 copy-done.3
  80.7 0.4 shard_map.73.own_ref
  81.2 0.0 collective-permute-done.3.w_ref
  81.2 0.7 collective-permute-done.2.mix_ref
  81.9 0.4 shard_map.74
  82.3 17.3 %all_to_all.27 = bf16[4,512,256]{2,1,0:T(8,128)(2,1)S(1)} all-to-all(bf16[4,512,256]{2,1,0:T(8,128)(2,1)S(1)} %shard_map.74), channel_id=1, replica_groups={{0,2,4,6},{1,3,5,7},{8,10,12,14},{9,11,13,15},{16,18,20,22},{17,19,21,2..., dimensions={0} | all-to-all | bytes 2097152 | tf_op jit(solution)/shard_map/all_to_all | solution.py:253
  99.6 0.9 reduce_sum.12
Async XLA Ops:
  0.0 24.0 %copy-start.1 = (bf16[2048,256]{1,0:T(8,128)(2,1)S(1)}, bf16[2048,256]{1,0:T(8,128)(2,1)}, u32[]{:S(2)}) copy-start(bf16[2048,256]{1,0:T(8,128)(2,1)} %ww_ref.3) | copy-start | bytes 3145732
  0.0 24.0 %copy-start = (bf16[2048,256]{1,0:T(8,128)(2,1)S(1)}, bf16[2048,256]{1,0:T(8,128)(2,1)}, u32[]{:S(2)}) copy-start(bf16[2048,256]{1,0:T(8,128)(2,1)} %wv_ref.3) | copy-start | bytes 3145732
  0.0 24.0 %copy-start.4 = (bf16[2048,32]{0,1:T(8,128)(2,1)S(1)}, bf16[2048,32]{0,1:T(8,128)(2,1)}, u32[]{:S(2)}) copy-start(bf16[2048,32]{0,1:T(8,128)(2,1)} %param.8) | copy-start | bytes 393220
  0.0 1.1 %copy-start.5 = (bf16[512,256]{1,0:T(8,128)(2,1)S(1)}, bf16[512,256]{1,0:T(8,128)(2,1)}, u32[]{:S(2)}) copy-start(bf16[512,256]{1,0:T(8,128)(2,1)} %x_ref.1) | copy-start | bytes 786436
  1.1 22.9 %copy-start.6 = (f32[2048]{0:T(1024)S(1)}, f32[2048]{0:T(1024)}, u32[]{:S(2)}) copy-start(f32[2048]{0:T(1024)} %param.7) | copy-start | bytes 24580
  16.7 9.6 %collective-permute-start = (bf16[4,512,256]{2,1,0:T(8,128)(2,1)S(1)}, bf16[4,512,256]{2,1,0:T(8,128)(2,1)S(1)}, u32[]{:S(2)}, u32[]{:S(2)}) collective-permute-start(bf16[4,512,256]{2,1,0:T(8,128)(2,1)S(1)} %all_to_all.25.x_ref), channel_id=1, source_target_pairs={{0,1},{1,0},{2,3},{3,2},{4,5},{5,4},{6,7},{7,6},{8,9},{9,8},{10,11... | collective-permute-start | bytes 3145736 | tf_op jit(solution)/shard_map/ppermute | solution.py:219
  36.9 27.1 %all-to-all-start.2 = ((bf16[16,40,128]{2,1,0:T(8,128)(2,1)}), bf16[16,40,128]{2,1,0:T(8,128)(2,1)S(1)}, u32[]{:S(2)}, u32[]{:S(2)}) async-start(bf16[16,40,128]{2,1,0:T(8,128)(2,1)} %shard_map.67), calls=%async_computation.2 | async-start | bytes 327680 | tf_op jit(solution)/shard_map/all_to_all | solution.py:238
  51.8 16.1 %collective-permute-start.1 = (bf16[512,256]{1,0:T(8,128)(2,1)}, bf16[512,256]{1,0:T(8,128)(2,1)S(1)}, u32[]{:S(2)}, u32[]{:S(2)}) collective-permute-start(bf16[512,256]{1,0:T(8,128)(2,1)} %get-tuple-element.18), channel_id=1, source_target_pairs={{0,8},{8,16},{16,24},{24,32},{32,40},{40,48},{48,56},{56,64},{64,7... | collective-permute-start | bytes 786440 | tf_op jit(solution)/shard_map/ppermute | solution.py:241
  54.0 1.2 %copy-start.2 = (bf16[256,2048]{1,0:T(8,128)(2,1)S(1)}, bf16[256,2048]{1,0:T(8,128)(2,1)}, u32[]{:S(2)}) copy-start(bf16[256,2048]{1,0:T(8,128)(2,1)} %w_ref.3) | copy-start | bytes 3145732
  55.3 25.4 %copy-start.3 = (bf16[256,2048]{1,0:T(8,128)(2,1)S(1)}, bf16[256,2048]{1,0:T(8,128)(2,1)}, u32[]{:S(2)}) copy-start(bf16[256,2048]{1,0:T(8,128)(2,1)} %w_ref.3) | copy-start | bytes 3145732
  55.3 25.9 %collective-permute-start.3 = (bf16[4,256,256]{2,1,0:T(8,128)(2,1)S(1)}, bf16[4,256,256]{2,1,0:T(8,128)(2,1)S(1)}, u32[]{:S(2)}, u32[]{:S(2)}) collective-permute-start(bf16[4,256,256]{2,1,0:T(8,128)(2,1)S(1)} %shard_map.72), channel_id=1, source_target_pairs={{0,1},{1,0},{2,3},{3,2},{4,5},{5,4},{6,7},{7,6},{8,9},{9,8},{10,11... | collective-permute-start | bytes 1572872 | tf_op jit(solution)/shard_map/ppermute | solution.py:219
  64.7 7.6 %all-to-all-start.3 = ((bf16[4,40,128]{2,1,0:T(8,128)(2,1)}), bf16[4,40,128]{2,1,0:T(8,128)(2,1)S(1)}, u32[]{:S(2)}, u32[]{:S(2)}) async-start(bf16[4,40,128]{2,1,0:T(8,128)(2,1)} %shard_map.68), calls=%async_computation.3 | async-start | bytes 81920 | tf_op jit(solution)/shard_map/all_to_all | solution.py:249
  72.8 9.0 %collective-permute-start.2 = (bf16[512,256]{1,0:T(8,128)(2,1)S(1)}, bf16[512,256]{1,0:T(8,128)(2,1)S(1)}, u32[]{:S(2)}, u32[]{:S(2)}) collective-permute-start(bf16[512,256]{1,0:T(8,128)(2,1)S(1)} %shard_map.71.mix_ref), channel_id=1, source_target_pairs={{0,1},{1,0},{2,3},{3,2},{4,5},{5,4},{6,7},{7,6},{8,9},{9,8},{10,11... | collective-permute-start | bytes 786440 | tf_op jit(solution)/shard_map/ppermute | solution.py:219

commit v14 on v13

--- a/solution.py
+++ b/solution.py
@@ -10,8 +10,9 @@
 
 EPS = 1e-05
 FEAT = 16
-QUARTER = 40
-ROWS = 4 * QUARTER
+NEAR = 8
+SHARE = 24
+ROWS = NEAR * SHARE
 BF = jnp.bfloat16
 F32 = jnp.float32
 VMEM = 12 * 1024 * 1024
@@ -120,8 +121,8 @@
     k = feats[:, FEAT:]
     phi = (dot(first, k, NT) + add_first) * (dot(second, k, NT) + add_second) * scale
     state = dot(phi.astype(BF), vlin)
-    for i in range(4):
-        state_ref[i, :, :] = state[QUARTER * i : QUARTER * (i + 1), :].astype(BF)
+    for i in range(NEAR):
+        state_ref[i, :, :] = state[SHARE * i : SHARE * (i + 1), :].astype(BF)
 
 
 def inner_kernel(pack_ref, after_ref, num_ref):
@@ -166,7 +167,7 @@
     scale, add_first, add_second = weights_of((1, ROWS), 1, True)
     q = pack_ref[:, 256 : 256 + FEAT]
     phi = (dot(q, first) + add_first) * (dot(q, second) + add_second) * scale
-    prefix = jnp.concatenate([prefix_ref[i, :, :].astype(F32) for i in range(4)], axis=0).astype(BF)
+    prefix = jnp.concatenate([prefix_ref[i, :, :].astype(F32) for i in range(NEAR)], axis=0).astype(BF)
     numerator = num_ref[...] + dot(phi.astype(BF), prefix)
     mean = jnp.mean(numerator * numerator, axis=1, keepdims=True)
     mix_ref[:, :128] = (numerator * lax.rsqrt(mean + EPS)).astype(BF)
@@ -192,18 +193,18 @@
 
 def total_kernel(got_ref, out_ref):
     total = got_ref[0, :, :].astype(F32)
-    for i in range(1, 4):
+    for i in range(1, NEAR):
         total = total + got_ref[i, :, :].astype(F32)
     total = total.astype(BF)
-    for z in range(16):
+    for z in range(out_ref.shape[0]):
         out_ref[z, :, :] = total
 
 
 def prefix_kernel(place_ref, got_ref, totals_ref, out_ref):
-    state = jnp.zeros((QUARTER, 128), F32)
-    for z in range(15):
+    state = jnp.zeros((SHARE, 128), F32)
+    for z in range(totals_ref.shape[0] - 1):
         state = state + jnp.where(z < place_ref[0], totals_ref[z, :, :].astype(F32), 0.0)
-    for i in range(4):
+    for i in range(NEAR):
         out_ref[i, :, :] = state.astype(BF)
         state = state + got_ref[i, :, :].astype(F32)
 
@@ -222,27 +223,27 @@
         return jax.ShapeDtypeStruct(dims, kind)
 
     block = ctx.astype(jnp.int32).reshape(1)
-    row = (ctx // 4).astype(jnp.int32).reshape(1)
+    row = (ctx // NEAR).astype(jnp.int32).reshape(1)
     copies = call_with_scalar(copies_kernel, shape((4,) + tokens.shape), 1, 3)(core, block, row, tokens)
     spread = lax.all_to_all(copies, "head", 0, 0, tiled=True, axis_index_groups=along_y)
     other = across(spread)
     weights = (gain.reshape(1, -1), w_feat.T, w_value, w_window)
     held = call_with_scalar(begin_kernel, shape((count, 640), F32), 5)(core, spread, *weights)
     pack, rim, states = call_with_scalar(
-        project_kernel, [shape((count, 640)), shape((count, 256)), shape((4, QUARTER, 128))], 6
+        project_kernel, [shape((count, 640)), shape((count, 256)), shape((NEAR, SHARE, 128))], 6
     )(core, other, *weights, held)
-    in_x = [[4 * z + x for x in range(4)] for z in range(16)]
-    in_z = [[4 * z + x for z in range(16)] for x in range(4)]
+    in_x = [[NEAR * z + x for x in range(NEAR)] for z in range(8)]
+    in_z = [[NEAR * z + x for z in range(8)] for x in range(NEAR)]
     quarters = lax.all_to_all(states, "ctx", 0, 0, tiled=True, axis_index_groups=in_x)
     rim, quarters = lax.optimization_barrier((rim, quarters))
     totals = lax.all_to_all(
-        call(total_kernel, shape((16, QUARTER, 128)))(quarters), "ctx", 0, 0, tiled=True, axis_index_groups=in_z
+        call(total_kernel, shape((8, SHARE, 128)))(quarters), "ctx", 0, 0, tiled=True, axis_index_groups=in_z
     )
     prev = lax.ppermute(rim, "ctx", [(b, b + 1) for b in range(63)])
     numerator = call(inner_kernel, shape((count, 128), F32))(pack, quarters)
     w_other = across(call_with_scalar(pick_kernel, shape((4, 256, 256)), 2)(core, w_out, quarters))
     win_out = call_with_scalar(attend_kernel, shape((count, 128)), 2)(block, pack, prev)
-    sums = call_with_scalar(prefix_kernel, shape((4, QUARTER, 128)), 2)(
+    sums = call_with_scalar(prefix_kernel, shape((NEAR, SHARE, 128)), 2)(
         row, quarters, totals
     )
     sums, numerator = lax.optimization_barrier((sums, numerator))

time: 101 us -> 101 us (level)
  starting transfers between devices: 40 us -> 37.4 us
  blocking collectives: 40.9 us -> 43.1 us
    all_to_all x1, blocking collectives: 8.15 us -> 10.3 us  [shards(): lax.all_to_all(states, 'ctx', 0, 0, tiled=True, axis_index_groups=in_x)]
    ppermute x3, starting transfers between devices: 19.6 us -> 18 us  [across(): return lax.ppermute(value, 'head', [(h, h ^ 1) for h in range(8)])]
    unnamed x14 -> x16, local copies, waits for them, and re-layouts: 2.33 us -> 3.03 us
where the time goes in v14:
time: 101 us
  blocking collectives  43.1 us (43%)
  starting transfers between devices  37.4 us (37%)
  waiting for transfers between devices  9.14 us (9%)
  Pallas kernels  7.17 us (7%)
  local copies, waits for them, and re-layouts  3.03 us (3%)
    ppermute x3, starting transfers between devices, across(): return lax.ppermute(value, 'head', [(h, h ^ 1) for h in range(8)])  18 us
    all_to_all x1, blocking collectives, shards(): lax.all_to_all(summed, 'head', 0, 0, tiled=True, axis_index_groups=along_y)  17.3 us
    all_to_all x1, blocking collectives, shards(): lax.all_to_all(copies, 'head', 0, 0, tiled=True, axis_index_groups=along_y)  15.5 us
    all_to_all x1, starting transfers between devices, shards(): lax.all_to_all(call(total_kernel, shape((8, SHARE, 128)))(quarters), 'ctx...  13.9 us
    all_to_all x1, blocking collectives, shards(): lax.all_to_all(states, 'ctx', 0, 0, tiled=True, axis_index_groups=in_x)  10.3 us
    all_to_all x1, waiting for transfers between devices, shards(): lax.all_to_all(sums, 'ctx', 0, 0, tiled=True, axis_index_groups=in_x)  3.79 us
    all_to_all x1, waiting for transfers between devices, shards(): lax.all_to_all(call(total_kernel, shape((8, SHARE, 128)))(quarters), 'ctx...  3.45 us
    all_to_all x1, starting transfers between devices, shards(): lax.all_to_all(sums, 'ctx', 0, 0, tiled=True, axis_index_groups=in_x)  3.34 us
  transfers between devices with their start and end apart: 6, of which 4 were waited for; matrix products, arithmetic and copies ran while one was open for 0% of the time, Pallas kernels for 5%

profile of v14, /device:TPU:1, one launch (start us, length us, event | category | flops | bytes accessed | tf_op | source)
XLA Modules:
  0.0 100.9 jit_solution(12177254175654099980)
XLA Ops:
  0.0 0.0 copy-start.1
  0.0 0.0 copy-start
  0.0 0.0 copy-start.4
  0.0 0.0 copy-start.5
  0.0 1.1 %copy-done.5 = bf16[512,256]{1,0:T(8,128)(2,1)S(1)} copy-done((bf16[512,256]{1,0:T(8,128)(2,1)S(1)}, bf16[512,256]{1,0:T(8,128)(2,1)}, u32[]{:S(2)}) %copy-start.5) | copy-done | bytes 262168
  1.1 0.0 copy-start.6
  1.1 0.1 shard_map.64
  1.2 15.5 %all_to_all.25.x_ref = bf16[4,512,256]{2,1,0:T(8,128)(2,1)S(1)} all-to-all(bf16[4,512,256]{2,1,0:T(8,128)(2,1)S(1)} %shard_map.64), channel_id=1, replica_groups={{0,2,4,6},{1,3,5,7},{8,10,12,14},{9,11,13,15},{16,18,20,22},{17,19,21,2..., dimensions={0} | all-to-all | bytes 2097152 | tf_op jit(solution)/shard_map/all_to_all | solution.py:228
  16.7 7.3 %collective-permute-start = (bf16[4,512,256]{2,1,0:T(8,128)(2,1)S(1)}, bf16[4,512,256]{2,1,0:T(8,128)(2,1)S(1)}, u32[]{:S(2)}, u32[]{:S(2)}) collective-permute-start(bf16[4,512,256]{2,1,0:T(8,128)(2,1)S(1)} %all_to_all.25.x_ref), channel_id=1, source_target_pairs={{0,1},{1,0},{2,3},{3,2},{4,5},{5,4},{6,7},{7,6},{8,9},{9,8},{10,11... | collective-permute-start | bytes 3145736 | tf_op jit(solution)/shard_map/ppermute | solution.py:220
  24.0 0.0 copy-done.1
  24.0 0.0 copy-done
  24.0 0.0 copy-done.4
  24.0 0.0 copy-done.6
  24.0 1.0 shard_map.65.held_ref
  25.0 1.2 %collective-permute-done.x_ref = bf16[4,512,256]{2,1,0:T(8,128)(2,1)S(1)} collective-permute-done((bf16[4,512,256]{2,1,0:T(8,128)(2,1)S(1)}, bf16[4,512,256]{2,1,0:T(8,128)(2,1)S(1)}, u32[]{:S(2)}, u32[]{:S(2)}) %collective-permute-start) | collective-permute-done | bytes 1048608 | tf_op jit(solution)/shard_map/ppermute | solution.py:220
  26.2 1.4 %shard_map.66 = (bf16[512,640]{1,0:T(8,128)(2,1)S(1)}, bf16[512,256]{1,0:T(8,128)(2,1)S(1)}, bf16[8,24,128]{2,1,0:T(8,128)(2,1)S(1)}) custom-call(s32[1]{0:T(128)} %bitcast.core_ref, bf16[4,512,256]{2,1,0:T(8,128)(2,1)S(1)} %collective-permute-done.x_ref, f32[1,2048]{1,0:T(1,128)S(1)} %bitcast.8, bf16[32,2048]{1,0:T(8,128)(2,1)S(1)} %bitcast.6, ...), custom_call_target="tpu_custom_call" | custom-call | tf_op jit(solution)/shard_map/pallas_call | solution.py:232
  27.7 0.0 copy-start.7
  27.7 0.7 copy-done.7
  28.4 10.3 %all_to_all.26.got_ref.after_ref = bf16[8,24,128]{2,1,0:T(8,128)(2,1)S(1)} all-to-all(bf16[8,24,128]{2,1,0:T(8,128)(2,1)S(1)} %get-tuple-element.14), channel_id=1, replica_groups={{0,8,16,24,32,40,48,56},{64,72,80,88,96,104,112,120},{128,136,144,152,1..., dimensions={0} | all-to-all | bytes 98304 | tf_op jit(solution)/shard_map/all_to_all | solution.py:237
  38.7 0.6 shard_map.67
  39.3 13.9 %all-to-all-start.2 = ((bf16[8,24,128]{2,1,0:T(8,128)(2,1)}), bf16[8,24,128]{2,1,0:T(8,128)(2,1)S(1)}, u32[]{:S(2)}, u32[]{:S(2)}) async-start(bf16[8,24,128]{2,1,0:T(8,128)(2,1)} %shard_map.67), calls=%async_computation.2 | async-start | bytes 98304 | tf_op jit(solution)/shard_map/all_to_all | solution.py:239
  53.2 2.2 %collective-permute-start.1 = (bf16[512,256]{1,0:T(8,128)(2,1)}, bf16[512,256]{1,0:T(8,128)(2,1)S(1)}, u32[]{:S(2)}, u32[]{:S(2)}) collective-permute-start(bf16[512,256]{1,0:T(8,128)(2,1)} %copy-done.7), channel_id=1, source_target_pairs={{0,8},{8,16},{16,24},{24,32},{32,40},{40,48},{48,56},{56,64},{64,7... | collective-permute-start | bytes 786440 | tf_op jit(solution)/shard_map/ppermute | solution.py:242
  55.4 0.0 copy-start.2
  55.4 1.2 %copy-done.2 = bf16[256,2048]{1,0:T(8,128)(2,1)S(1)} copy-done((bf16[256,2048]{1,0:T(8,128)(2,1)S(1)}, bf16[256,2048]{1,0:T(8,128)(2,1)}, u32[]{:S(2)}) %copy-start.2) | copy-done | bytes 1048600
  56.7 0.1 shard_map.72
  56.7 0.0 copy-start.3
  56.7 4.4 %collective-permute-start.3 = (bf16[4,256,256]{2,1,0:T(8,128)(2,1)S(1)}, bf16[4,256,256]{2,1,0:T(8,128)(2,1)S(1)}, u32[]{:S(2)}, u32[]{:S(2)}) collective-permute-start(bf16[4,256,256]{2,1,0:T(8,128)(2,1)S(1)} %shard_map.72), channel_id=1, source_target_pairs={{0,1},{1,0},{2,3},{3,2},{4,5},{5,4},{6,7},{7,6},{8,9},{9,8},{10,11... | collective-permute-start | bytes 1572872 | tf_op jit(solution)/shard_map/ppermute | solution.py:220
  61.1 0.6 shard_map.69.num_ref
  61.8 3.5 %all-to-all-done.2.totals_ref = bf16[8,24,128]{2,1,0:T(8,128)(2,1)S(1)} async-done(((bf16[8,24,128]{2,1,0:T(8,128)(2,1)}), bf16[8,24,128]{2,1,0:T(8,128)(2,1)S(1)}, u32[]{:S(2)}, u32[]{:S(2)}) %all-to-all-start.2) | async-done | bytes 49184 | tf_op jit(solution)/shard_map/all_to_all | solution.py:239
  65.2 0.6 shard_map.68
  65.8 3.3 %all-to-all-start.3 = ((bf16[8,24,128]{2,1,0:T(8,128)(2,1)}), bf16[8,24,128]{2,1,0:T(8,128)(2,1)S(1)}, u32[]{:S(2)}, u32[]{:S(2)}) async-start(bf16[8,24,128]{2,1,0:T(8,128)(2,1)} %shard_map.68), calls=%async_computation.3 | async-start | bytes 98304 | tf_op jit(solution)/shard_map/all_to_all | solution.py:250
  69.2 0.0 collective-permute-done.1.prev_ref
  69.2 1.3 %shard_map.70.win_ref = bf16[512,128]{1,0:T(8,128)(2,1)S(1)} custom-call(s32[1]{0:T(128)} %bitcast.1.ctx_ref.first_ref, bf16[512,640]{1,0:T(8,128)(2,1)S(1)} %get-tuple-element.12.pack_ref, bf16[512,256]{1,0:T(8,128)(2,1)S(1)} %collective-permute-done.1.prev_ref), custom_call_target="tpu_custom_call" | custom-call | tf_op jit(solution)/shard_map/pallas_call | solution.py:245
  70.5 3.8 %all-to-all-done.3.prefix_ref = bf16[8,24,128]{2,1,0:T(8,128)(2,1)S(1)} async-done(((bf16[8,24,128]{2,1,0:T(8,128)(2,1)}), bf16[8,24,128]{2,1,0:T(8,128)(2,1)S(1)}, u32[]{:S(2)}, u32[]{:S(2)}) %all-to-all-start.3) | async-done | bytes 49184 | tf_op jit(solution)/shard_map/all_to_all | solution.py:250
  74.3 0.6 shard_map.71.mix_ref
  74.9 6.3 %collective-permute-start.2 = (bf16[512,256]{1,0:T(8,128)(2,1)S(1)}, bf16[512,256]{1,0:T(8,128)(2,1)S(1)}, u32[]{:S(2)}, u32[]{:S(2)}) collective-permute-start(bf16[512,256]{1,0:T(8,128)(2,1)S(1)} %shard_map.71.mix_ref), channel_id=1, source_target_pairs={{0,1},{1,0},{2,3},{3,2},{4,5},{5,4},{6,7},{7,6},{8,9},{9,8},{10,11... | collective-permute-start | bytes 786440 | tf_op jit(solution)/shard_map/ppermute | solution.py:220
  81.2 0.0 copy-done.3
  81.2 0.5 shard_map.73.own_ref
  81.6 0.0 collective-permute-done.3.w_ref
  81.6 0.7 collective-permute-done.2.mix_ref
  82.3 0.4 shard_map.74
  82.8 17.3 %all_to_all.27 = bf16[4,512,256]{2,1,0:T(8,128)(2,1)S(1)} all-to-all(bf16[4,512,256]{2,1,0:T(8,128)(2,1)S(1)} %shard_map.74), channel_id=1, replica_groups={{0,2,4,6},{1,3,5,7},{8,10,12,14},{9,11,13,15},{16,18,20,22},{17,19,21,2..., dimensions={0} | all-to-all | bytes 2097152 | tf_op jit(solution)/shard_map/all_to_all | solution.py:254
  100.0 0.9 reduce_sum.12
Async XLA Ops:
  0.0 24.0 %copy-start.1 = (bf16[2048,256]{1,0:T(8,128)(2,1)S(1)}, bf16[2048,256]{1,0:T(8,128)(2,1)}, u32[]{:S(2)}) copy-start(bf16[2048,256]{1,0:T(8,128)(2,1)} %ww_ref.3) | copy-start | bytes 3145732
  0.0 24.0 %copy-start = (bf16[2048,256]{1,0:T(8,128)(2,1)S(1)}, bf16[2048,256]{1,0:T(8,128)(2,1)}, u32[]{:S(2)}) copy-start(bf16[2048,256]{1,0:T(8,128)(2,1)} %wv_ref.3) | copy-start | bytes 3145732
  0.0 24.0 %copy-start.4 = (bf16[2048,32]{0,1:T(8,128)(2,1)S(1)}, bf16[2048,32]{0,1:T(8,128)(2,1)}, u32[]{:S(2)}) copy-start(bf16[2048,32]{0,1:T(8,128)(2,1)} %param.8) | copy-start | bytes 393220
  0.0 1.1 %copy-start.5 = (bf16[512,256]{1,0:T(8,128)(2,1)S(1)}, bf16[512,256]{1,0:T(8,128)(2,1)}, u32[]{:S(2)}) copy-start(bf16[512,256]{1,0:T(8,128)(2,1)} %x_ref.1) | copy-start | bytes 786436
  1.1 22.9 %copy-start.6 = (f32[2048]{0:T(1024)S(1)}, f32[2048]{0:T(1024)}, u32[]{:S(2)}) copy-start(f32[2048]{0:T(1024)} %param.7) | copy-start | bytes 24580
  16.7 9.6 %collective-permute-start = (bf16[4,512,256]{2,1,0:T(8,128)(2,1)S(1)}, bf16[4,512,256]{2,1,0:T(8,128)(2,1)S(1)}, u32[]{:S(2)}, u32[]{:S(2)}) collective-permute-start(bf16[4,512,256]{2,1,0:T(8,128)(2,1)S(1)} %all_to_all.25.x_ref), channel_id=1, source_target_pairs={{0,1},{1,0},{2,3},{3,2},{4,5},{5,4},{6,7},{7,6},{8,9},{9,8},{10,11... | collective-permute-start | bytes 3145736 | tf_op jit(solution)/shard_map/ppermute | solution.py:220
  27.7 0.7 copy-start.7
  39.3 25.9 %all-to-all-start.2 = ((bf16[8,24,128]{2,1,0:T(8,128)(2,1)}), bf16[8,24,128]{2,1,0:T(8,128)(2,1)S(1)}, u32[]{:S(2)}, u32[]{:S(2)}) async-start(bf16[8,24,128]{2,1,0:T(8,128)(2,1)} %shard_map.67), calls=%async_computation.2 | async-start | bytes 98304 | tf_op jit(solution)/shard_map/all_to_all | solution.py:239
  53.2 16.0 %collective-permute-start.1 = (bf16[512,256]{1,0:T(8,128)(2,1)}, bf16[512,256]{1,0:T(8,128)(2,1)S(1)}, u32[]{:S(2)}, u32[]{:S(2)}) collective-permute-start(bf16[512,256]{1,0:T(8,128)(2,1)} %copy-done.7), channel_id=1, source_target_pairs={{0,8},{8,16},{16,24},{24,32},{32,40},{40,48},{48,56},{56,64},{64,7... | collective-permute-start | bytes 786440 | tf_op jit(solution)/shard_map/ppermute | solution.py:242
  55.4 1.2 %copy-start.2 = (bf16[256,2048]{1,0:T(8,128)(2,1)S(1)}, bf16[256,2048]{1,0:T(8,128)(2,1)}, u32[]{:S(2)}) copy-start(bf16[256,2048]{1,0:T(8,128)(2,1)} %w_ref.3) | copy-start | bytes 3145732
  56.7 24.4 %copy-start.3 = (bf16[256,2048]{1,0:T(8,128)(2,1)S(1)}, bf16[256,2048]{1,0:T(8,128)(2,1)}, u32[]{:S(2)}) copy-start(bf16[256,2048]{1,0:T(8,128)(2,1)} %w_ref.3) | copy-start | bytes 3145732
  56.7 24.9 %collective-permute-start.3 = (bf16[4,256,256]{2,1,0:T(8,128)(2,1)S(1)}, bf16[4,256,256]{2,1,0:T(8,128)(2,1)S(1)}, u32[]{:S(2)}, u32[]{:S(2)}) collective-permute-start(bf16[4,256,256]{2,1,0:T(8,128)(2,1)S(1)} %shard_map.72), channel_id=1, source_target_pairs={{0,1},{1,0},{2,3},{3,2},{4,5},{5,4},{6,7},{7,6},{8,9},{9,8},{10,11... | collective-permute-start | bytes 1572872 | tf_op jit(solution)/shard_map/ppermute | solution.py:220
  65.8 8.4 %all-to-all-start.3 = ((bf16[8,24,128]{2,1,0:T(8,128)(2,1)}), bf16[8,24,128]{2,1,0:T(8,128)(2,1)S(1)}, u32[]{:S(2)}, u32[]{:S(2)}) async-start(bf16[8,24,128]{2,1,0:T(8,128)(2,1)} %shard_map.68), calls=%async_computation.3 | async-start | bytes 98304 | tf_op jit(solution)/shard_map/all_to_all | solution.py:250
  74.9 7.4 %collective-permute-start.2 = (bf16[512,256]{1,0:T(8,128)(2,1)S(1)}, bf16[512,256]{1,0:T(8,128)(2,1)S(1)}, u32[]{:S(2)}, u32[]{:S(2)}) collective-permute-start(bf16[512,256]{1,0:T(8,128)(2,1)S(1)} %shard_map.71.mix_ref), channel_id=1, source_target_pairs={{0,1},{1,0},{2,3},{3,2},{4,5},{5,4},{6,7},{7,6},{8,9},{9,8},{10,11... | collective-permute-start | bytes 786440 | tf_op jit(solution)/shard_map/ppermute | solution.py:220

commit v15 on v13

--- a/solution.py
+++ b/solution.py
@@ -99,7 +99,7 @@
     held_ref[:, 544:] = jnp.broadcast_to(squares, (squares.shape[0], 96))
 
 
-def project_kernel(core_ref, x_ref, gain_ref, wf_ref, wv_ref, ww_ref, held_ref, pack_ref, rim_ref, state_ref):
+def project_kernel(core_ref, x_ref, gain_ref, wf_ref, wv_ref, ww_ref, held_ref, pack_ref, rim_hbm, state_ref, rim_ref, sem):
     count = x_ref.shape[1]
     squares, feats, values, windowed = gather_products(1, core_ref, x_ref, gain_ref, wf_ref, wv_ref, ww_ref)
     scale = lax.rsqrt((squares + held_ref[:, 544:545]) * (1.0 / 2048.0) + EPS)
@@ -108,6 +108,8 @@
     feats = ((feats + held_ref[:, 512:544]) * scale).astype(BF)
     rim_ref[:, :128] = windowed[:, 128:]
     rim_ref[:, 128:] = values[:, 128:]
+    store = pltpu.make_async_copy(rim_ref, rim_hbm, sem)
+    store.start()
     vlin = values[:, :128]
     pack_ref[:, :128] = windowed[:, :128]
     pack_ref[:, 128:256] = vlin
@@ -122,6 +124,7 @@
     state = dot(phi.astype(BF), vlin)
     for i in range(4):
         state_ref[i, :, :] = state[QUARTER * i : QUARTER * (i + 1), :].astype(BF)
+    store.wait()
 
 
 def inner_kernel(pack_ref, after_ref, num_ref):
@@ -190,6 +193,13 @@
         sum_ref[y, :, :] = (own_ref[y, :, :] + dot(mix_ref[...], w_ref[y, :, :])).astype(BF)
 
 
+def sum_kernel(parts_ref, out_ref):
+    total = parts_ref[0, :, :].astype(F32)
+    for y in range(1, 4):
+        total = total + parts_ref[y, :, :].astype(F32)
+    out_ref[...] = total.astype(BF)
+
+
 def total_kernel(got_ref, out_ref):
     total = got_ref[0, :, :].astype(F32)
     for i in range(1, 4):
@@ -228,8 +238,14 @@
     other = across(spread)
     weights = (gain.reshape(1, -1), w_feat.T, w_value, w_window)
     held = call_with_scalar(begin_kernel, shape((count, 640), F32), 5)(core, spread, *weights)
-    pack, rim, states = call_with_scalar(
-        project_kernel, [shape((count, 640)), shape((count, 256)), shape((4, QUARTER, 128))], 6
+    vmem, hbm = pl.BlockSpec(memory_space=pltpu.VMEM), pl.BlockSpec(memory_space=pltpu.HBM)
+    pack, rim, states = pl.pallas_call(
+        project_kernel,
+        out_shape=[shape((count, 640)), shape((count, 256)), shape((4, QUARTER, 128))],
+        in_specs=[pl.BlockSpec(memory_space=pltpu.SMEM)] + [vmem] * 6,
+        out_specs=[vmem, hbm, vmem],
+        scratch_shapes=[pltpu.VMEM((count, 256), BF), pltpu.SemaphoreType.DMA],
+        compiler_params=pltpu.CompilerParams(vmem_limit_bytes=VMEM),
     )(core, other, *weights, held)
     in_x = [[4 * z + x for x in range(4)] for z in range(16)]
     in_z = [[4 * z + x for z in range(16)] for x in range(4)]
@@ -251,7 +267,7 @@
     own = call_with_scalar(own_kernel, shape((4, count, 256), F32), 2)(core, mix, w_out)
     summed = call(output_kernel, shape((4, count, 256)))(across(mix), w_other, own)
     parts = lax.all_to_all(summed, "head", 0, 0, tiled=True, axis_index_groups=along_y)
-    return jnp.sum(parts.astype(F32), axis=0).astype(BF)
+    return call(sum_kernel, shape((count, 256)))(parts)
 
 
 def solution(mesh):

time: 101 us -> 101 us (level)
    pallas_call x1 -> x2, Pallas kernels: 1.82 us -> 2.67 us  [the longest x1 1.83 us: shards(): pl.pallas_call(project_kernel, out_shape=[shape((count, 640)), shape((cou...]
where the time goes in v15:
time: 101 us; the launch traced here: 100 us
  blocking collectives  40.9 us (40%)
  starting transfers between devices  40 us (40%)
  Pallas kernels  8.54 us (8%)
  waiting for transfers between devices  8.5 us (8%)
  local copies, waits for them, and re-layouts  2.33 us (2%)
    ppermute x3, starting transfers between devices, across(): return lax.ppermute(value, 'head', [(h, h ^ 1) for h in range(8)])  19.6 us
    all_to_all x1, blocking collectives, shards(): lax.all_to_all(summed, 'head', 0, 0, tiled=True, axis_index_groups=along_y)  17.3 us
    all_to_all x1, blocking collectives, shards(): lax.all_to_all(copies, 'head', 0, 0, tiled=True, axis_index_groups=along_y)  15.5 us
    all_to_all x1, starting transfers between devices, shards(): lax.all_to_all(call(total_kernel, shape((16, QUARTER, 128)))(quarters), '...  14.9 us
    all_to_all x1, blocking collectives, shards(): lax.all_to_all(states, 'ctx', 0, 0, tiled=True, axis_index_groups=in_x)  8.16 us
    all_to_all x1, waiting for transfers between devices, shards(): lax.all_to_all(call(total_kernel, shape((16, QUARTER, 128)))(quarters), '...  3.61 us
    all_to_all x1, starting transfers between devices, shards(): lax.all_to_all(sums, 'ctx', 0, 0, tiled=True, axis_index_groups=in_x)  3.27 us
    all_to_all x1, waiting for transfers between devices, shards(): lax.all_to_all(sums, 'ctx', 0, 0, tiled=True, axis_index_groups=in_x)  3 us
  transfers between devices with their start and end apart: 6, of which 4 were waited for; matrix products, arithmetic and copies ran while one was open for 0% of the time, Pallas kernels for 5%

profile of v15, /device:TPU:1, one launch (start us, length us, event | category | flops | bytes accessed | tf_op | source)
XLA Modules:
  0.0 100.4 jit_solution(1748576807632992580)
XLA Ops:
  0.0 0.0 copy-start.1
  0.0 0.0 copy-start
  0.0 0.0 copy-start.4
  0.0 0.0 copy-start.5
  0.0 1.1 %copy-done.5 = bf16[512,256]{1,0:T(8,128)(2,1)S(1)} copy-done((bf16[512,256]{1,0:T(8,128)(2,1)S(1)}, bf16[512,256]{1,0:T(8,128)(2,1)}, u32[]{:S(2)}) %copy-start.5) | copy-done | bytes 262168
  1.1 0.0 copy-start.6
  1.1 0.1 shard_map.64
  1.2 15.5 %all_to_all.25.x_ref = bf16[4,512,256]{2,1,0:T(8,128)(2,1)S(1)} all-to-all(bf16[4,512,256]{2,1,0:T(8,128)(2,1)S(1)} %shard_map.64), channel_id=1, replica_groups={{0,2,4,6},{1,3,5,7},{8,10,12,14},{9,11,13,15},{16,18,20,22},{17,19,21,2..., dimensions={0} | all-to-all | bytes 2097152 | tf_op jit(solution)/shard_map/all_to_all | solution.py:237
  16.7 7.3 %collective-permute-start = (bf16[4,512,256]{2,1,0:T(8,128)(2,1)S(1)}, bf16[4,512,256]{2,1,0:T(8,128)(2,1)S(1)}, u32[]{:S(2)}, u32[]{:S(2)}) collective-permute-start(bf16[4,512,256]{2,1,0:T(8,128)(2,1)S(1)} %all_to_all.25.x_ref), channel_id=1, source_target_pairs={{0,1},{1,0},{2,3},{3,2},{4,5},{5,4},{6,7},{7,6},{8,9},{9,8},{10,11... | collective-permute-start | bytes 3145736 | tf_op jit(solution)/shard_map/ppermute | solution.py:229
  24.0 0.0 copy-done.1
  24.0 0.0 copy-done
  24.0 0.0 copy-done.4
  24.0 0.0 copy-done.6
  24.0 1.0 shard_map.65.held_ref
  25.0 1.2 %collective-permute-done.x_ref = bf16[4,512,256]{2,1,0:T(8,128)(2,1)S(1)} collective-permute-done((bf16[4,512,256]{2,1,0:T(8,128)(2,1)S(1)}, bf16[4,512,256]{2,1,0:T(8,128)(2,1)S(1)}, u32[]{:S(2)}, u32[]{:S(2)}) %collective-permute-start) | collective-permute-done | bytes 1048608 | tf_op jit(solution)/shard_map/ppermute | solution.py:229
  26.2 1.8 %shard_map.66 = (bf16[512,640]{1,0:T(8,128)(2,1)S(1)}, bf16[512,256]{1,0:T(8,128)(2,1)}, bf16[4,40,128]{2,1,0:T(8,128)(2,1)S(1)}) custom-call(s32[1]{0:T(128)} %bitcast.core_ref, bf16[4,512,256]{2,1,0:T(8,128)(2,1)S(1)} %collective-permute-done.x_ref, f32[1,2048]{1,0:T(1,128)S(1)} %bitcast.8, bf16[32,2048]{1,0:T(8,128)(2,1)S(1)} %bitcast.6, ...), custom_call_target="tpu_custom_call" | custom-call | tf_op jit(solution)/shard_map/pallas_call | solution.py:242
  28.1 8.2 %all_to_all.26.got_ref.after_ref = bf16[4,40,128]{2,1,0:T(8,128)(2,1)S(1)} all-to-all(bf16[4,40,128]{2,1,0:T(8,128)(2,1)S(1)} %get-tuple-element.14), channel_id=1, replica_groups={{0,8,16,24},{32,40,48,56},{64,72,80,88},{96,104,112,120},{128,136,144,1..., dimensions={0} | all-to-all | bytes 81920 | tf_op jit(solution)/shard_map/all_to_all | solution.py:252
  36.2 0.7 shard_map.67
  36.9 14.9 %all-to-all-start.2 = ((bf16[16,40,128]{2,1,0:T(8,128)(2,1)}), bf16[16,40,128]{2,1,0:T(8,128)(2,1)S(1)}, u32[]{:S(2)}, u32[]{:S(2)}) async-start(bf16[16,40,128]{2,1,0:T(8,128)(2,1)} %shard_map.67), calls=%async_computation.2 | async-start | bytes 327680 | tf_op jit(solution)/shard_map/all_to_all | solution.py:254
  51.8 2.2 %collective-permute-start.1 = (bf16[512,256]{1,0:T(8,128)(2,1)}, bf16[512,256]{1,0:T(8,128)(2,1)S(1)}, u32[]{:S(2)}, u32[]{:S(2)}) collective-permute-start(bf16[512,256]{1,0:T(8,128)(2,1)} %get-tuple-element.18), channel_id=1, source_target_pairs={{0,8},{8,16},{16,24},{24,32},{32,40},{40,48},{48,56},{56,64},{64,7... | collective-permute-start | bytes 786440 | tf_op jit(solution)/shard_map/ppermute | solution.py:257
  54.1 0.0 copy-start.2
  54.1 1.2 %copy-done.2 = bf16[256,2048]{1,0:T(8,128)(2,1)S(1)} copy-done((bf16[256,2048]{1,0:T(8,128)(2,1)S(1)}, bf16[256,2048]{1,0:T(8,128)(2,1)}, u32[]{:S(2)}) %copy-start.2) | copy-done | bytes 1048600
  55.3 0.1 shard_map.72
  55.4 0.0 copy-start.3
  55.4 4.4 %collective-permute-start.3 = (bf16[4,256,256]{2,1,0:T(8,128)(2,1)S(1)}, bf16[4,256,256]{2,1,0:T(8,128)(2,1)S(1)}, u32[]{:S(2)}, u32[]{:S(2)}) collective-permute-start(bf16[4,256,256]{2,1,0:T(8,128)(2,1)S(1)} %shard_map.72), channel_id=1, source_target_pairs={{0,1},{1,0},{2,3},{3,2},{4,5},{5,4},{6,7},{7,6},{8,9},{9,8},{10,11... | collective-permute-start | bytes 1572872 | tf_op jit(solution)/shard_map/ppermute | solution.py:229
  59.8 0.6 shard_map.69.num_ref
  60.4 3.6 %all-to-all-done.2.totals_ref = bf16[16,40,128]{2,1,0:T(8,128)(2,1)S(1)} async-done(((bf16[16,40,128]{2,1,0:T(8,128)(2,1)}), bf16[16,40,128]{2,1,0:T(8,128)(2,1)S(1)}, u32[]{:S(2)}, u32[]{:S(2)}) %all-to-all-start.2) | async-done | bytes 163872 | tf_op jit(solution)/shard_map/all_to_all | solution.py:254
  64.0 0.7 shard_map.68
  64.7 3.3 %all-to-all-start.3 = ((bf16[4,40,128]{2,1,0:T(8,128)(2,1)}), bf16[4,40,128]{2,1,0:T(8,128)(2,1)S(1)}, u32[]{:S(2)}, u32[]{:S(2)}) async-start(bf16[4,40,128]{2,1,0:T(8,128)(2,1)} %shard_map.68), calls=%async_computation.3 | async-start | bytes 81920 | tf_op jit(solution)/shard_map/all_to_all | solution.py:265
  68.0 0.0 collective-permute-done.1.prev_ref
  68.0 1.3 %shard_map.70.win_ref = bf16[512,128]{1,0:T(8,128)(2,1)S(1)} custom-call(s32[1]{0:T(128)} %bitcast.1.ctx_ref.first_ref, bf16[512,640]{1,0:T(8,128)(2,1)S(1)} %get-tuple-element.12.pack_ref, bf16[512,256]{1,0:T(8,128)(2,1)S(1)} %collective-permute-done.1.prev_ref), custom_call_target="tpu_custom_call" | custom-call | tf_op jit(solution)/shard_map/pallas_call | solution.py:260
  69.3 3.0 %all-to-all-done.3.prefix_ref = bf16[4,40,128]{2,1,0:T(8,128)(2,1)S(1)} async-done(((bf16[4,40,128]{2,1,0:T(8,128)(2,1)}), bf16[4,40,128]{2,1,0:T(8,128)(2,1)S(1)}, u32[]{:S(2)}, u32[]{:S(2)}) %all-to-all-start.3) | async-done | bytes 40992 | tf_op jit(solution)/shard_map/all_to_all | solution.py:265
  72.3 0.6 shard_map.71.mix_ref
  72.9 7.9 %collective-permute-start.2 = (bf16[512,256]{1,0:T(8,128)(2,1)S(1)}, bf16[512,256]{1,0:T(8,128)(2,1)S(1)}, u32[]{:S(2)}, u32[]{:S(2)}) collective-permute-start(bf16[512,256]{1,0:T(8,128)(2,1)S(1)} %shard_map.71.mix_ref), channel_id=1, source_target_pairs={{0,1},{1,0},{2,3},{3,2},{4,5},{5,4},{6,7},{7,6},{8,9},{9,8},{10,11... | collective-permute-start | bytes 786440 | tf_op jit(solution)/shard_map/ppermute | solution.py:229
  80.8 0.0 copy-done.3
  80.8 0.5 shard_map.73.own_ref
  81.2 0.0 collective-permute-done.3.w_ref
  81.2 0.7 collective-permute-done.2.mix_ref
  81.9 0.4 shard_map.74
  82.4 17.3 %all_to_all.27.parts_ref = bf16[4,512,256]{2,1,0:T(8,128)(2,1)S(1)} all-to-all(bf16[4,512,256]{2,1,0:T(8,128)(2,1)S(1)} %shard_map.74), channel_id=1, replica_groups={{0,2,4,6},{1,3,5,7},{8,10,12,14},{9,11,13,15},{16,18,20,22},{17,19,21,2..., dimensions={0} | all-to-all | bytes 2097152 | tf_op jit(solution)/shard_map/all_to_all | solution.py:269
  99.6 0.8 shard_map.75
Async XLA Ops:
  0.0 24.0 %copy-start.1 = (bf16[2048,256]{1,0:T(8,128)(2,1)S(1)}, bf16[2048,256]{1,0:T(8,128)(2,1)}, u32[]{:S(2)}) copy-start(bf16[2048,256]{1,0:T(8,128)(2,1)} %ww_ref.3) | copy-start | bytes 3145732
  0.0 24.0 %copy-start = (bf16[2048,256]{1,0:T(8,128)(2,1)S(1)}, bf16[2048,256]{1,0:T(8,128)(2,1)}, u32[]{:S(2)}) copy-start(bf16[2048,256]{1,0:T(8,128)(2,1)} %wv_ref.3) | copy-start | bytes 3145732
  0.0 24.0 %copy-start.4 = (bf16[2048,32]{0,1:T(8,128)(2,1)S(1)}, bf16[2048,32]{0,1:T(8,128)(2,1)}, u32[]{:S(2)}) copy-start(bf16[2048,32]{0,1:T(8,128)(2,1)} %param.8) | copy-start | bytes 393220
  0.0 1.1 %copy-start.5 = (bf16[512,256]{1,0:T(8,128)(2,1)S(1)}, bf16[512,256]{1,0:T(8,128)(2,1)}, u32[]{:S(2)}) copy-start(bf16[512,256]{1,0:T(8,128)(2,1)} %x_ref.1) | copy-start | bytes 786436
  1.1 22.9 %copy-start.6 = (f32[2048]{0:T(1024)S(1)}, f32[2048]{0:T(1024)}, u32[]{:S(2)}) copy-start(f32[2048]{0:T(1024)} %param.7) | copy-start | bytes 24580
  16.7 9.6 %collective-permute-start = (bf16[4,512,256]{2,1,0:T(8,128)(2,1)S(1)}, bf16[4,512,256]{2,1,0:T(8,128)(2,1)S(1)}, u32[]{:S(2)}, u32[]{:S(2)}) collective-permute-start(bf16[4,512,256]{2,1,0:T(8,128)(2,1)S(1)} %all_to_all.25.x_ref), channel_id=1, source_target_pairs={{0,1},{1,0},{2,3},{3,2},{4,5},{5,4},{6,7},{7,6},{8,9},{9,8},{10,11... | collective-permute-start | bytes 3145736 | tf_op jit(solution)/shard_map/ppermute | solution.py:229
  36.9 27.1 %all-to-all-start.2 = ((bf16[16,40,128]{2,1,0:T(8,128)(2,1)}), bf16[16,40,128]{2,1,0:T(8,128)(2,1)S(1)}, u32[]{:S(2)}, u32[]{:S(2)}) async-start(bf16[16,40,128]{2,1,0:T(8,128)(2,1)} %shard_map.67), calls=%async_computation.2 | async-start | bytes 327680 | tf_op jit(solution)/shard_map/all_to_all | solution.py:254
  51.8 16.1 %collective-permute-start.1 = (bf16[512,256]{1,0:T(8,128)(2,1)}, bf16[512,256]{1,0:T(8,128)(2,1)S(1)}, u32[]{:S(2)}, u32[]{:S(2)}) collective-permute-start(bf16[512,256]{1,0:T(8,128)(2,1)} %get-tuple-element.18), channel_id=1, source_target_pairs={{0,8},{8,16},{16,24},{24,32},{32,40},{40,48},{48,56},{56,64},{64,7... | collective-permute-start | bytes 786440 | tf_op jit(solution)/shard_map/ppermute | solution.py:257
  54.1 1.2 %copy-start.2 = (bf16[256,2048]{1,0:T(8,128)(2,1)S(1)}, bf16[256,2048]{1,0:T(8,128)(2,1)}, u32[]{:S(2)}) copy-start(bf16[256,2048]{1,0:T(8,128)(2,1)} %w_ref.3) | copy-start | bytes 3145732
  55.4 25.4 %copy-start.3 = (bf16[256,2048]{1,0:T(8,128)(2,1)S(1)}, bf16[256,2048]{1,0:T(8,128)(2,1)}, u32[]{:S(2)}) copy-start(bf16[256,2048]{1,0:T(8,128)(2,1)} %w_ref.3) | copy-start | bytes 3145732
  55.4 25.9 %collective-permute-start.3 = (bf16[4,256,256]{2,1,0:T(8,128)(2,1)S(1)}, bf16[4,256,256]{2,1,0:T(8,128)(2,1)S(1)}, u32[]{:S(2)}, u32[]{:S(2)}) collective-permute-start(bf16[4,256,256]{2,1,0:T(8,128)(2,1)S(1)} %shard_map.72), channel_id=1, source_target_pairs={{0,1},{1,0},{2,3},{3,2},{4,5},{5,4},{6,7},{7,6},{8,9},{9,8},{10,11... | collective-permute-start | bytes 1572872 | tf_op jit(solution)/shard_map/ppermute | solution.py:229
  64.7 7.6 %all-to-all-start.3 = ((bf16[4,40,128]{2,1,0:T(8,128)(2,1)}), bf16[4,40,128]{2,1,0:T(8,128)(2,1)S(1)}, u32[]{:S(2)}, u32[]{:S(2)}) async-start(bf16[4,40,128]{2,1,0:T(8,128)(2,1)} %shard_map.68), calls=%async_computation.3 | async-start | bytes 81920 | tf_op jit(solution)/shard_map/all_to_all | solution.py:265
  72.9 9.0 %collective-permute-start.2 = (bf16[512,256]{1,0:T(8,128)(2,1)S(1)}, bf16[512,256]{1,0:T(8,128)(2,1)S(1)}, u32[]{:S(2)}, u32[]{:S(2)}) collective-permute-start(bf16[512,256]{1,0:T(8,128)(2,1)S(1)} %shard_map.71.mix_ref), channel_id=1, source_target_pairs={{0,1},{1,0},{2,3},{3,2},{4,5},{5,4},{6,7},{7,6},{8,9},{9,8},{10,11... | collective-permute-start | bytes 786440 | tf_op jit(solution)/shard_map/ppermute | solution.py:229

commit v16 on v13

--- a/solution.py
+++ b/solution.py
@@ -161,7 +161,7 @@
         win_ref[t * tile : (t + 1) * tile, :] = dot(probs, vals).astype(BF)
 
 
-def linear_kernel(pack_ref, num_ref, prefix_ref, win_ref, mix_ref):
+def linear_kernel(pack_ref, num_ref, prefix_ref, after_ref, lin_ref):
     first, second = pick((FEAT, ROWS), 1)
     scale, add_first, add_second = weights_of((1, ROWS), 1, True)
     q = pack_ref[:, 256 : 256 + FEAT]
@@ -169,8 +169,7 @@
     prefix = jnp.concatenate([prefix_ref[i, :, :].astype(F32) for i in range(4)], axis=0).astype(BF)
     numerator = num_ref[...] + dot(phi.astype(BF), prefix)
     mean = jnp.mean(numerator * numerator, axis=1, keepdims=True)
-    mix_ref[:, :128] = (numerator * lax.rsqrt(mean + EPS)).astype(BF)
-    mix_ref[:, 128:] = win_ref[...]
+    lin_ref[...] = (numerator * lax.rsqrt(mean + EPS)).astype(BF)
 
 
 def pick_kernel(core_ref, w_ref, after_ref, out_ref):
@@ -179,15 +178,16 @@
         out_ref[y, :, :] = w_ref[:, pl.ds(at, 256)]
 
 
-def own_kernel(core_ref, mix_ref, w_ref, sum_ref):
-    for y in range(4):
-        at = pl.multiple_of((2 * y + core_ref[0]) * 256, 256)
-        sum_ref[y, :, :] = dot(mix_ref[...], w_ref[:, pl.ds(at, 256)])
-
-
-def output_kernel(mix_ref, w_ref, own_ref, sum_ref):
-    for y in range(4):
-        sum_ref[y, :, :] = (own_ref[y, :, :] + dot(mix_ref[...], w_ref[y, :, :])).astype(BF)
+def own_kernel(core_ref, lin_ref, win_ref, w_ref, win2_ref, w2_ref, sum_ref):
+    for y in range(4):
+        columns = pl.ds(pl.multiple_of((2 * y + core_ref[0]) * 256, 256), 256)
+        total = dot(lin_ref[...], w_ref[:128, columns]) + dot(win_ref[...], w_ref[128:, columns])
+        sum_ref[y, :, :] = total + dot(win2_ref[...], w2_ref[y, 128:, :])
+
+
+def output_kernel(lin_ref, w_ref, own_ref, sum_ref):
+    for y in range(4):
+        sum_ref[y, :, :] = (own_ref[y, :, :] + dot(lin_ref[...], w_ref[y, :128, :])).astype(BF)
 
 
 def total_kernel(got_ref, out_ref):
@@ -247,9 +247,10 @@
     )
     sums, numerator = lax.optimization_barrier((sums, numerator))
     prefix = lax.all_to_all(sums, "ctx", 0, 0, tiled=True, axis_index_groups=in_x)
-    mix = call(linear_kernel, shape((count, 256)))(pack, numerator, prefix, win_out)
-    own = call_with_scalar(own_kernel, shape((4, count, 256), F32), 2)(core, mix, w_out)
-    summed = call(output_kernel, shape((4, count, 256)))(across(mix), w_other, own)
+    win_other = across(win_out)
+    lin = call(linear_kernel, shape((count, 128)))(pack, numerator, prefix, win_other)
+    own = call_with_scalar(own_kernel, shape((4, count, 256), F32), 5)(core, lin, win_out, w_out, win_other, w_other)
+    summed = call(output_kernel, shape((4, count, 256)))(across(lin), w_other, own)
     parts = lax.all_to_all(summed, "head", 0, 0, tiled=True, axis_index_groups=along_y)
     return jnp.sum(parts.astype(F32), axis=0).astype(BF)
 

time: 101 us -> 104 us (1.030); the launches traced: 101 us -> 102 us
  starting transfers between devices: 40 us -> 43.4 us
  waiting for transfers between devices: 8.52 us -> 5.58 us
    all_to_all x1, starting transfers between devices: 3.27 us -> 8.29 us  [shards(): lax.all_to_all(sums, 'ctx', 0, 0, tiled=True, axis_index_groups=in_x)]
    all_to_all x1, waiting for transfers between devices: 3.62 us -> 0.01 us  [shards(): lax.all_to_all(call(total_kernel, shape((16, QUARTER, 128)))(quarters), '...]
    ppermute x3 -> x4, starting transfers between devices: 19.6 us -> 18 us  [across(): return lax.ppermute(value, 'head', [(h, h ^ 1) for h in range(8)])]
    all_to_all x1, waiting for transfers between devices: 3 us -> 4.34 us  [shards(): lax.all_to_all(sums, 'ctx', 0, 0, tiled=True, axis_index_groups=in_x)]
  transfers between devices with their start and end apart: 6 -> 7, of which waited for: 4 -> 2; matrix products, arithmetic and copies ran while one was open for 0% -> 0% of each run, Pallas kernels for 5% -> 5%
where the time goes in v16:
time: 104 us; the launch traced here: 102 us
  starting transfers between devices  43.4 us (42%)
  blocking collectives  41 us (39%)
  Pallas kernels  8.18 us (8%)
  waiting for transfers between devices  5.58 us (5%)
  local copies, waits for them, and re-layouts  2.33 us (2%)
    ppermute x4, starting transfers between devices, across(): return lax.ppermute(value, 'head', [(h, h ^ 1) for h in range(8)])  18 us
    all_to_all x1, blocking collectives, shards(): lax.all_to_all(summed, 'head', 0, 0, tiled=True, axis_index_groups=along_y)  17.3 us
    all_to_all x1, blocking collectives, shards(): lax.all_to_all(copies, 'head', 0, 0, tiled=True, axis_index_groups=along_y)  15.5 us
    all_to_all x1, starting transfers between devices, shards(): lax.all_to_all(call(total_kernel, shape((16, QUARTER, 128)))(quarters), '...  14.9 us
    all_to_all x1, starting transfers between devices, shards(): lax.all_to_all(sums, 'ctx', 0, 0, tiled=True, axis_index_groups=in_x)  8.29 us
    all_to_all x1, blocking collectives, shards(): lax.all_to_all(states, 'ctx', 0, 0, tiled=True, axis_index_groups=in_x)  8.15 us
    all_to_all x1, waiting for transfers between devices, shards(): lax.all_to_all(sums, 'ctx', 0, 0, tiled=True, axis_index_groups=in_x)  4.34 us
    unnamed x14, local copies, waits for them, and re-layouts  2.33 us
  transfers between devices with their start and end apart: 7, of which 2 were waited for; matrix products, arithmetic and copies ran while one was open for 0% of the time, Pallas kernels for 5%

profile of v16, /device:TPU:1, one launch (start us, length us, event | category | flops | bytes accessed | tf_op | source)
XLA Modules:
  0.0 101.6 jit_solution(14096491976233158286)
XLA Ops:
  0.0 0.0 copy-start.1
  0.0 0.0 copy-start
  0.0 0.0 copy-start.4
  0.0 0.0 copy-start.5
  0.0 1.1 %copy-done.5 = bf16[512,256]{1,0:T(8,128)(2,1)S(1)} copy-done((bf16[512,256]{1,0:T(8,128)(2,1)S(1)}, bf16[512,256]{1,0:T(8,128)(2,1)}, u32[]{:S(2)}) %copy-start.5) | copy-done | bytes 262168
  1.1 0.0 copy-start.6
  1.1 0.1 shard_map.64
  1.2 15.5 %all_to_all.25.x_ref = bf16[4,512,256]{2,1,0:T(8,128)(2,1)S(1)} all-to-all(bf16[4,512,256]{2,1,0:T(8,128)(2,1)S(1)} %shard_map.64), channel_id=1, replica_groups={{0,2,4,6},{1,3,5,7},{8,10,12,14},{9,11,13,15},{16,18,20,22},{17,19,21,2..., dimensions={0} | all-to-all | bytes 2097152 | tf_op jit(solution)/shard_map/all_to_all | solution.py:227
  16.7 7.3 %collective-permute-start = (bf16[4,512,256]{2,1,0:T(8,128)(2,1)S(1)}, bf16[4,512,256]{2,1,0:T(8,128)(2,1)S(1)}, u32[]{:S(2)}, u32[]{:S(2)}) collective-permute-start(bf16[4,512,256]{2,1,0:T(8,128)(2,1)S(1)} %all_to_all.25.x_ref), channel_id=1, source_target_pairs={{0,1},{1,0},{2,3},{3,2},{4,5},{5,4},{6,7},{7,6},{8,9},{9,8},{10,11... | collective-permute-start | bytes 3145736 | tf_op jit(solution)/shard_map/ppermute | solution.py:219
  24.0 0.0 copy-done.1
  24.0 0.0 copy-done
  24.0 0.0 copy-done.4
  24.0 0.0 copy-done.6
  24.0 1.0 shard_map.65.held_ref
  25.0 1.2 %collective-permute-done.x_ref = bf16[4,512,256]{2,1,0:T(8,128)(2,1)S(1)} collective-permute-done((bf16[4,512,256]{2,1,0:T(8,128)(2,1)S(1)}, bf16[4,512,256]{2,1,0:T(8,128)(2,1)S(1)}, u32[]{:S(2)}, u32[]{:S(2)}) %collective-permute-start) | collective-permute-done | bytes 1048608 | tf_op jit(solution)/shard_map/ppermute | solution.py:219
  26.2 1.8 %shard_map.66 = (bf16[512,640]{1,0:T(8,128)(2,1)S(1)}, bf16[512,256]{1,0:T(8,128)(2,1)}, bf16[4,40,128]{2,1,0:T(8,128)(2,1)S(1)}) custom-call(s32[1]{0:T(128)} %bitcast.core_ref, bf16[4,512,256]{2,1,0:T(8,128)(2,1)S(1)} %collective-permute-done.x_ref, f32[1,2048]{1,0:T(1,128)S(1)} %bitcast.8, bf16[32,2048]{1,0:T(8,128)(2,1)S(1)} %bitcast.6, ...), custom_call_target="tpu_custom_call" | custom-call | tf_op jit(solution)/shard_map/pallas_call | solution.py:231
  28.1 8.2 %all_to_all.26.got_ref.after_ref = bf16[4,40,128]{2,1,0:T(8,128)(2,1)S(1)} all-to-all(bf16[4,40,128]{2,1,0:T(8,128)(2,1)S(1)} %get-tuple-element.14), channel_id=1, replica_groups={{0,8,16,24},{32,40,48,56},{64,72,80,88},{96,104,112,120},{128,136,144,1..., dimensions={0} | all-to-all | bytes 81920 | tf_op jit(solution)/shard_map/all_to_all | solution.py:236
  36.2 0.7 shard_map.67
  36.9 14.9 %all-to-all-start.2 = ((bf16[16,40,128]{2,1,0:T(8,128)(2,1)}), bf16[16,40,128]{2,1,0:T(8,128)(2,1)S(1)}, u32[]{:S(2)}, u32[]{:S(2)}) async-start(bf16[16,40,128]{2,1,0:T(8,128)(2,1)} %shard_map.67), calls=%async_computation.2 | async-start | bytes 327680 | tf_op jit(solution)/shard_map/all_to_all | solution.py:238
  51.8 2.2 %collective-permute-start.1 = (bf16[512,256]{1,0:T(8,128)(2,1)}, bf16[512,256]{1,0:T(8,128)(2,1)S(1)}, u32[]{:S(2)}, u32[]{:S(2)}) collective-permute-start(bf16[512,256]{1,0:T(8,128)(2,1)} %get-tuple-element.18), channel_id=1, source_target_pairs={{0,8},{8,16},{16,24},{24,32},{32,40},{40,48},{48,56},{56,64},{64,7... | collective-permute-start | bytes 786440 | tf_op jit(solution)/shard_map/ppermute | solution.py:241
  54.0 0.0 copy-start.2
  54.0 1.2 %copy-done.2 = bf16[256,2048]{1,0:T(8,128)(2,1)S(1)} copy-done((bf16[256,2048]{1,0:T(8,128)(2,1)S(1)}, bf16[256,2048]{1,0:T(8,128)(2,1)}, u32[]{:S(2)}) %copy-start.2) | copy-done | bytes 1048600
  55.3 0.1 shard_map.72
  55.3 0.0 copy-start.3
  55.3 4.4 %collective-permute-start.4 = (bf16[4,256,256]{2,1,0:T(8,128)(2,1)S(1)}, bf16[4,256,256]{2,1,0:T(8,128)(2,1)S(1)}, u32[]{:S(2)}, u32[]{:S(2)}) collective-permute-start(bf16[4,256,256]{2,1,0:T(8,128)(2,1)S(1)} %shard_map.72), channel_id=1, source_target_pairs={{0,1},{1,0},{2,3},{3,2},{4,5},{5,4},{6,7},{7,6},{8,9},{9,8},{10,11... | collective-permute-start | bytes 1572872 | tf_op jit(solution)/shard_map/ppermute | solution.py:219
  59.8 0.0 collective-permute-done.1.prev_ref
  59.8 1.3 %shard_map.70.win_ref = bf16[512,128]{1,0:T(8,128)(2,1)S(1)} custom-call(s32[1]{0:T(128)} %bitcast.1.ctx_ref.first_ref, bf16[512,640]{1,0:T(8,128)(2,1)S(1)} %get-tuple-element.12.pack_ref, bf16[512,256]{1,0:T(8,128)(2,1)S(1)} %collective-permute-done.1.prev_ref), custom_call_target="tpu_custom_call" | custom-call | tf_op jit(solution)/shard_map/pallas_call | solution.py:244
  61.0 3.0 %collective-permute-start.2 = (bf16[512,128]{1,0:T(8,128)(2,1)S(1)}, bf16[512,128]{1,0:T(8,128)(2,1)S(1)}, u32[]{:S(2)}, u32[]{:S(2)}) collective-permute-start(bf16[512,128]{1,0:T(8,128)(2,1)S(1)} %shard_map.70.win_ref), channel_id=1, source_target_pairs={{0,1},{1,0},{2,3},{3,2},{4,5},{5,4},{6,7},{7,6},{8,9},{9,8},{10,11... | collective-permute-start | bytes 393224 | tf_op jit(solution)/shard_map/ppermute | solution.py:219
  64.0 0.6 shard_map.69.num_ref
  64.6 0.0 all-to-all-done.2.totals_ref
  64.7 0.7 shard_map.68
  65.3 8.3 %all-to-all-start.3 = ((bf16[4,40,128]{2,1,0:T(8,128)(2,1)}), bf16[4,40,128]{2,1,0:T(8,128)(2,1)S(1)}, u32[]{:S(2)}, u32[]{:S(2)}) async-start(bf16[4,40,128]{2,1,0:T(8,128)(2,1)} %shard_map.68), calls=%async_computation.3 | async-start | bytes 81920 | tf_op jit(solution)/shard_map/all_to_all | solution.py:249
  73.6 0.0 collective-permute-done.2.after_ref.win2_ref
  73.6 4.3 %all-to-all-done.3.prefix_ref = bf16[4,40,128]{2,1,0:T(8,128)(2,1)S(1)} async-done(((bf16[4,40,128]{2,1,0:T(8,128)(2,1)}), bf16[4,40,128]{2,1,0:T(8,128)(2,1)S(1)}, u32[]{:S(2)}, u32[]{:S(2)}) %all-to-all-start.3) | async-done | bytes 40992 | tf_op jit(solution)/shard_map/all_to_all | solution.py:249
  78.0 0.6 shard_map.71.lin_ref
  78.6 3.3 %collective-permute-start.3 = (bf16[512,128]{1,0:T(8,128)(2,1)S(1)}, bf16[512,128]{1,0:T(8,128)(2,1)S(1)}, u32[]{:S(2)}, u32[]{:S(2)}) collective-permute-start(bf16[512,128]{1,0:T(8,128)(2,1)S(1)} %shard_map.71.lin_ref), channel_id=1, source_target_pairs={{0,1},{1,0},{2,3},{3,2},{4,5},{5,4},{6,7},{7,6},{8,9},{9,8},{10,11... | collective-permute-start | bytes 393224 | tf_op jit(solution)/shard_map/ppermute | solution.py:219
  81.9 0.0 collective-permute-done.4.w2_ref.w_ref
  81.9 0.0 copy-done.3
  81.9 1.0 shard_map.73.own_ref
  82.9 0.0 collective-permute-done.3.lin_ref
  82.9 0.4 shard_map.74
  83.4 17.3 %all_to_all.27 = bf16[4,512,256]{2,1,0:T(8,128)(2,1)S(1)} all-to-all(bf16[4,512,256]{2,1,0:T(8,128)(2,1)S(1)} %shard_map.74), channel_id=1, replica_groups={{0,2,4,6},{1,3,5,7},{8,10,12,14},{9,11,13,15},{16,18,20,22},{17,19,21,2..., dimensions={0} | all-to-all | bytes 2097152 | tf_op jit(solution)/shard_map/all_to_all | solution.py:254
  100.7 0.9 reduce_sum.12
Async XLA Ops:
  0.0 24.0 %copy-start.1 = (bf16[2048,256]{1,0:T(8,128)(2,1)S(1)}, bf16[2048,256]{1,0:T(8,128)(2,1)}, u32[]{:S(2)}) copy-start(bf16[2048,256]{1,0:T(8,128)(2,1)} %ww_ref.3) | copy-start | bytes 3145732
  0.0 24.0 %copy-start = (bf16[2048,256]{1,0:T(8,128)(2,1)S(1)}, bf16[2048,256]{1,0:T(8,128)(2,1)}, u32[]{:S(2)}) copy-start(bf16[2048,256]{1,0:T(8,128)(2,1)} %wv_ref.3) | copy-start | bytes 3145732
  0.0 24.0 %copy-start.4 = (bf16[2048,32]{0,1:T(8,128)(2,1)S(1)}, bf16[2048,32]{0,1:T(8,128)(2,1)}, u32[]{:S(2)}) copy-start(bf16[2048,32]{0,1:T(8,128)(2,1)} %param.8) | copy-start | bytes 393220
  0.0 1.1 %copy-start.5 = (bf16[512,256]{1,0:T(8,128)(2,1)S(1)}, bf16[512,256]{1,0:T(8,128)(2,1)}, u32[]{:S(2)}) copy-start(bf16[512,256]{1,0:T(8,128)(2,1)} %x_ref.1) | copy-start | bytes 786436
  1.1 22.9 %copy-start.6 = (f32[2048]{0:T(1024)S(1)}, f32[2048]{0:T(1024)}, u32[]{:S(2)}) copy-start(f32[2048]{0:T(1024)} %param.7) | copy-start | bytes 24580
  16.7 9.6 %collective-permute-start = (bf16[4,512,256]{2,1,0:T(8,128)(2,1)S(1)}, bf16[4,512,256]{2,1,0:T(8,128)(2,1)S(1)}, u32[]{:S(2)}, u32[]{:S(2)}) collective-permute-start(bf16[4,512,256]{2,1,0:T(8,128)(2,1)S(1)} %all_to_all.25.x_ref), channel_id=1, source_target_pairs={{0,1},{1,0},{2,3},{3,2},{4,5},{5,4},{6,7},{7,6},{8,9},{9,8},{10,11... | collective-permute-start | bytes 3145736 | tf_op jit(solution)/shard_map/ppermute | solution.py:219
  36.9 27.8 %all-to-all-start.2 = ((bf16[16,40,128]{2,1,0:T(8,128)(2,1)}), bf16[16,40,128]{2,1,0:T(8,128)(2,1)S(1)}, u32[]{:S(2)}, u32[]{:S(2)}) async-start(bf16[16,40,128]{2,1,0:T(8,128)(2,1)} %shard_map.67), calls=%async_computation.2 | async-start | bytes 327680 | tf_op jit(solution)/shard_map/all_to_all | solution.py:238
  51.8 7.9 %collective-permute-start.1 = (bf16[512,256]{1,0:T(8,128)(2,1)}, bf16[512,256]{1,0:T(8,128)(2,1)S(1)}, u32[]{:S(2)}, u32[]{:S(2)}) collective-permute-start(bf16[512,256]{1,0:T(8,128)(2,1)} %get-tuple-element.18), channel_id=1, source_target_pairs={{0,8},{8,16},{16,24},{24,32},{32,40},{40,48},{48,56},{56,64},{64,7... | collective-permute-start | bytes 786440 | tf_op jit(solution)/shard_map/ppermute | solution.py:241
  54.0 1.2 %copy-start.2 = (bf16[256,2048]{1,0:T(8,128)(2,1)S(1)}, bf16[256,2048]{1,0:T(8,128)(2,1)}, u32[]{:S(2)}) copy-start(bf16[256,2048]{1,0:T(8,128)(2,1)} %w_ref.3) | copy-start | bytes 3145732
  55.3 26.6 %copy-start.3 = (bf16[256,2048]{1,0:T(8,128)(2,1)S(1)}, bf16[256,2048]{1,0:T(8,128)(2,1)}, u32[]{:S(2)}) copy-start(bf16[256,2048]{1,0:T(8,128)(2,1)} %w_ref.3) | copy-start | bytes 3145732
  55.3 26.6 %collective-permute-start.4 = (bf16[4,256,256]{2,1,0:T(8,128)(2,1)S(1)}, bf16[4,256,256]{2,1,0:T(8,128)(2,1)S(1)}, u32[]{:S(2)}, u32[]{:S(2)}) collective-permute-start(bf16[4,256,256]{2,1,0:T(8,128)(2,1)S(1)} %shard_map.72), channel_id=1, source_target_pairs={{0,1},{1,0},{2,3},{3,2},{4,5},{5,4},{6,7},{7,6},{8,9},{9,8},{10,11... | collective-permute-start | bytes 1572872 | tf_op jit(solution)/shard_map/ppermute | solution.py:219
  61.0 12.6 %collective-permute-start.2 = (bf16[512,128]{1,0:T(8,128)(2,1)S(1)}, bf16[512,128]{1,0:T(8,128)(2,1)S(1)}, u32[]{:S(2)}, u32[]{:S(2)}) collective-permute-start(bf16[512,128]{1,0:T(8,128)(2,1)S(1)} %shard_map.70.win_ref), channel_id=1, source_target_pairs={{0,1},{1,0},{2,3},{3,2},{4,5},{5,4},{6,7},{7,6},{8,9},{9,8},{10,11... | collective-permute-start | bytes 393224 | tf_op jit(solution)/shard_map/ppermute | solution.py:219
  65.3 12.6 %all-to-all-start.3 = ((bf16[4,40,128]{2,1,0:T(8,128)(2,1)}), bf16[4,40,128]{2,1,0:T(8,128)(2,1)S(1)}, u32[]{:S(2)}, u32[]{:S(2)}) async-start(bf16[4,40,128]{2,1,0:T(8,128)(2,1)} %shard_map.68), calls=%async_computation.3 | async-start | bytes 81920 | tf_op jit(solution)/shard_map/all_to_all | solution.py:249
  78.6 4.4 %collective-permute-start.3 = (bf16[512,128]{1,0:T(8,128)(2,1)S(1)}, bf16[512,128]{1,0:T(8,128)(2,1)S(1)}, u32[]{:S(2)}, u32[]{:S(2)}) collective-permute-start(bf16[512,128]{1,0:T(8,128)(2,1)S(1)} %shard_map.71.lin_ref), channel_id=1, source_target_pairs={{0,1},{1,0},{2,3},{3,2},{4,5},{5,4},{6,7},{7,6},{8,9},{9,8},{10,11... | collective-permute-start | bytes 393224 | tf_op jit(solution)/shard_map/ppermute | solution.py:219
